TPU v7x, 32 devices: a whole 2x2x4 slice. The times are simulated.
32 devices in a mesh: dp: 2 (over core), seq: 4 (over z), expert: 4 (over y, x).
Axes of the slice: x: 2, y: 2, z: 4, core: 2. Of those that a mesh axis runs over, the one named last changes fastest.
Arguments:
- tokens: bfloat16 [8192, 2048], P(('dp', 'seq')), may hold values from -6 to 6
- phi: bfloat16 [2048, 8], P(None, 'expert'), may hold values from -40 to 40
- w_in: bfloat16 [8, 2048, 8192], P('expert', None, ('dp', 'seq')), may hold values from -1 to 1
- w_out: bfloat16 [8, 8192, 2048], P('expert', ('dp', 'seq')), may hold values from -0.25 to 0.25
Outputs:
- mixed: bfloat16 [8192, 2048], P(('dp', 'seq', 'expert'))
All inputs are finite; a program needn't handle non-finite values.
Results may differ from a plain program's by a relative error of at most 0.0068.
Values may be sent and summed in bfloat16 or wider, within the bound.
No kernel may reach another device: no remote copies, remote signals or barrier semaphores. Data moves between devices by JAX's collectives and lax.ppermute only.
A program may use at most 64 MiB of HBM per device.

v0:
```python
import jax
import jax.numpy as jnp
from jax import lax
from jax.sharding import PartitionSpec as P


def on_device(tokens, phi, w_in, w_out):
    logits = lax.dot_general(
        phi, tokens, (((0,), (1,)), ((), ())), preferred_element_type=jnp.float32
    )
    slot_max = lax.pmax(jnp.max(logits, axis=1), "seq")
    spread = jnp.exp(logits - slot_max[:, None])
    numerator = jnp.dot(spread.astype(jnp.bfloat16), tokens, preferred_element_type=jnp.float32)
    denominator = jnp.sum(spread, axis=1)
    numer_seq, denom_seq = lax.psum((numerator, denominator), "seq")
    own_slots = (numer_seq / denom_seq[:, None]).astype(jnp.bfloat16)
    slot_in = lax.all_gather(own_slots[None], "dp", axis=0, tiled=True)
    hidden = jax.nn.gelu(
        jnp.einsum("ced,edf->cef", slot_in, w_in, preferred_element_type=jnp.float32),
        approximate=True,
    ).astype(jnp.bfloat16)
    partial_value = jnp.einsum("cef,efd->ced", hidden, w_out, preferred_element_type=jnp.float32)
    totals = lax.psum(partial_value, ("dp", "seq"))
    summed = lax.dynamic_index_in_dim(totals, lax.axis_index("dp"), 0, keepdims=False)
    slot_out = summed.astype(jnp.bfloat16)
    row_max = lax.pmax(jnp.max(logits, axis=0), "expert")
    combine_weights = jnp.exp(logits - row_max[None, :])
    local_numer = lax.dot_general(
        combine_weights.astype(jnp.bfloat16),
        slot_out,
        (((0,), (0,)), ((), ())),
        preferred_element_type=jnp.float32,
    )
    mixed_numer, mixed_denom = (
        lax.psum_scatter(local_numer, "expert", scatter_dimension=0, tiled=True),
        lax.psum_scatter(
            jnp.sum(combine_weights, axis=0), "expert", scatter_dimension=0, tiled=True
        ),
    )
    return (mixed_numer / mixed_denom[:, None]).astype(jnp.bfloat16)


def solution(mesh):
    placed = (
        P(("dp", "seq"), None),
        P(None, "expert"),
        P("expert", None, ("dp", "seq")),
        P("expert", ("dp", "seq"), None),
    )
    return jax.shard_map(
        on_device,
        mesh=mesh,
        in_specs=placed,
        out_specs=P(("dp", "seq", "expert"), None),
        check_vma=False,
    )
```

profile of v0, /device:TPU:0, one launch (start us, length us, event | category | flops | bytes accessed | tf_op | source)
XLA Modules:
  0.0 187.5 jit_solution(3251949685809820711)
XLA Ops:
  6.5 0.0 copy-start
  6.5 0.0 reduce-scatter.2.cloned.1.call-start
  6.5 0.7 copy-done
  7.2 3.5 %fusion.30 = (f32[1024]{0:T(1024)S(1)}, f32[2]{0:T(128)S(1)}, f32[2,1024]{1,0:T(2,128)S(1)}) fusion(bf16[2048,2]{0,1:T(2,128)(2,1)S(1)} %copy-done, bf16[1024,2048]{1,0:T(8,128)(2,1)} %param.4), kind=kOutput, calls=%fused_computation.35 | convolution fusion | flops 8391678 | bytes 4214792 | tf_op jit(solution)/shard_map/dot_general | solution.py:8
  10.7 11.4 %pmax.14 = f32[1024]{0:T(1024)S(1)} all-reduce(f32[1024]{0:T(1024)S(1)} %get-tuple-element.7), channel_id=1, replica_groups=mesh['dp'=2,'seq'=4,'expert'=4] {'expert'}, use_global_device_ids=true, to_apply=%region_1.0 | all-reduce | flops 1024 | bytes 8192 | tf_op jit(solution)/shard_map/pmax | solution.py:26
  22.1 12.0 %pmax.15 = f32[2]{0:T(128)S(1)} all-reduce(f32[2]{0:T(128)S(1)} %get-tuple-element.8), channel_id=1, replica_groups=mesh['dp'=2,'seq'=4,'expert'=4] {'seq'}, use_global_device_ids=true, to_apply=%region_3.0 | all-reduce | flops 2 | bytes 16 | tf_op jit(solution)/shard_map/pmax | solution.py:11
  34.0 2.9 %fusion.22 = f32[2,2048]{1,0:T(2,128)S(1)} fusion(bf16[1024,2048]{1,0:T(8,128)(2,1)} %param.4, f32[2,1024]{1,0:T(2,128)S(1)} %get-tuple-element.11, f32[2]{0:T(128)S(1)} %pmax.15), kind=kOutput, calls=%fused_computation.29 | convolution fusion | flops 8392704 | bytes 4218888 | tf_op jit(solution)/shard_map/dot_general | solution.py:13
  36.9 0.2 fusion.18
  37.1 15.7 %all-reduce.1 = (f32[2,2048]{1,0:T(2,128)S(1)}, f32[2]{0:T(128)S(1)}) all-reduce(f32[2,2048]{1,0:T(2,128)S(1)} %fusion.22, f32[2]{0:T(128)S(1)} %get-tuple-element.6), channel_id=1, replica_groups=mesh['dp'=2,'seq'=4,'expert'=4] {'seq'}, use_global_device_ids=true, to_apply=%region_4.0 | all-reduce | flops 4098 | bytes 32784 | tf_op jit(solution)/shard_map/psum | solution.py:15
  52.9 0.1 fusion.17
  53.0 1.8 all-gather.1
  54.8 8.0 %convolution_bitcast_fusion = f32[2,2,2048]{2,0,1:T(2,128)S(1)} fusion(bf16[2,1024,2048]{2,1,0:T(8,128)(2,1)} %param.7, bf16[2,2048,1024]{2,1,0:T(8,128)(2,1)} %param.6, bf16[2,2,2048]{2,1,0:T(2,128)(2,1)S(1)} %all-gather.1), kind=kOutput, calls=%fused_computation | convolution fusion | flops 33591296 | bytes 16826368 | tf_op jit(solution)/shard_map/cef,efd->ced/dot_general | solution.py:22
  62.8 27.6 %psum.23 = bf16[2,2,2048]{2,0,1:T(2,128)(2,1)S(1)} all-reduce(f32[2,2,2048]{2,0,1:T(2,128)S(1)} %convolution_bitcast_fusion), channel_id=1, replica_groups=mesh['dp'=2,'seq'=4,'expert'=4] {'dp','seq'}, use_global_device_ids=true, to_apply=%region_7.8 | all-reduce | flops 8192 | bytes 49152 | tf_op jit(solution)/shard_map/psum | solution.py:23
  90.4 0.0 copy-start.1
  90.4 4.5 %fusion.10 = f32[1024,2048]{1,0:T(8,128)} fusion(bf16[1,2,2048]{2,0,1:T(2,128)(2,1)S(1)} %dynamic-slice_convert_fusion, f32[2,1024]{1,0:T(2,128)S(1)} %get-tuple-element.11, f32[1024]{0:T(1024)S(1)} %pmax.14), kind=kOutput, calls=%fused_computation.15 | convolution fusion | flops 8392704 | bytes 8409088 | tf_op jit(solution)/shard_map/dot_general | solution.py:28
  94.9 0.0 reduce-scatter.2.cloned.1.call-update
  95.0 0.0 copy-done.1
  95.0 0.6 dynamic-slice
  96.2 8.2 %all-reduce = f32[1024]{0:T(1024)S(1)} all-reduce(f32[1024]{0:T(1024)S(1)} %get-tuple-element.5), channel_id=4, replica_groups=mesh['dp'=2,'seq'=4,'expert'=4] {'expert'}, use_global_device_ids=true, to_apply=%region_10.11.clone | all-reduce | flops 1024 | bytes 8192
  104.4 0.1 dynamic-slice.1
  104.5 73.4 %reduce-scatter.2.cloned.1.call-done = f32[256,2048]{1,0:T(8,128)} async-done(((f32[1024,2048]{1,0:T(8,128)}), f32[256,2048]{1,0:T(8,128)}) %reduce-scatter.2.cloned.1.call-update) | async-done | bytes 2097168 | tf_op jit(solution)/shard_map/reduce_scatter | solution.py:35
  177.9 2.8 %divide_convert_fusion = bf16[256,2048]{1,0:T(8,128)(2,1)} fusion(f32[256,2048]{1,0:T(8,128)} %reduce-scatter.2.cloned.1.call-done, f32[256]{0:T(256)S(1)} %dynamic-slice.1), kind=kLoop, calls=%fused_computation.1 | loop fusion | flops 1048576 | bytes 3146752 | tf_op jit(solution)/shard_map/convert_element_type | solution.py:40
  (1 shorter events, 0.0 us)
Async XLA Ops:
  6.5 0.7 copy-start
  6.5 171.3 %reduce-scatter.2.cloned.1.call-start = ((), (), s32[]{:S(2)}) async-start(), calls=%async_computation.1 | async-start | bytes 10485760 | tf_op jit(solution)/shard_map/reduce_scatter | solution.py:35
  90.4 4.6 %copy-start.1 = (u32[32]{0:T(128)S(1)}, u32[32]{0:T(128)}, u32[]{:S(2)}) copy-start(u32[32]{0:T(128)} %constant.29) | copy-start | bytes 388
Sparse Core Ops, SparseCore 0:
  95.1 82.7 reduce-scatter.1
where the time goes:
time: 188 us
  blocking collectives  76.6 us (41%)
  waiting for transfers between devices  73.4 us (39%)
  matrix products  18.9 us (10%)
  between operations  14.1 us (8%)
  other arithmetic  3.1 us (2%)
    reduce_scatter x1, waiting for transfers between devices, on_device(): lax.psum_scatter(local_numer, 'expert', scatter_dimension=0, tiled=True)  73.4 us
    psum x1, blocking collectives, on_device(): totals = lax.psum(partial_value, ('dp', 'seq'))  27.6 us
    psum x1, blocking collectives, on_device(): numer_seq, denom_seq = lax.psum((numerator, denominator), 'seq')  15.7 us
    pmax x1, blocking collectives, on_device(): slot_max = lax.pmax(jnp.max(logits, axis=1), 'seq')  12 us
    pmax x1, blocking collectives, on_device(): row_max = lax.pmax(jnp.max(logits, axis=0), 'expert')  11.4 us
    unnamed x1, blocking collectives  8.17 us
    dot_general x1, matrix products, on_device(): jnp.einsum('cef,efd->ced', hidden, w_out, preferred_element_type=jnp.floa...  8.04 us
    dot_general x1, matrix products, on_device(): lax.dot_general(combine_weights.astype(jnp.bfloat16), slot_out, (((0,), (...  4.53 us
  transfers between devices with their start and end apart: 1, of which 1 were waited for; matrix products, arithmetic and copies ran while one was open for 0% of the time, Pallas kernels for 0%

commit v1 on v0

v1 whole, which is shorter than its diff:
```python
import functools

import jax
import jax.numpy as jnp
from jax import lax
from jax.experimental import pallas as pl
from jax.experimental.pallas import tpu as pltpu
from jax.sharding import PartitionSpec as P

F32, BF16 = jnp.float32, jnp.bfloat16
LANES = 128
VMEM = pl.BlockSpec(memory_space=pltpu.VMEM)


def params(mib):
    return pltpu.CompilerParams(vmem_limit_bytes=mib << 20)


def partners(n, step):
    if n & (n - 1):
        return [(i, (i + step) % n) for i in range(n)]
    return [(i, i ^ step) for i in range(n)]


def gathered(x, axis, n):
    return [x] + [lax.ppermute(x, axis, partners(n, step)) for step in range(1, n)]


def slot_sums_kernel(chunks, phi_ref, tokens_ref, packed_ref, logits_ref, held, sems):
    rows, width = tokens_ref.shape[0] // chunks, tokens_ref.shape[1]

    def copy(c):
        part = pl.ds(c * rows, rows)
        return pltpu.make_async_copy(tokens_ref.at[part], held.at[part], sems.at[c])

    for c in range(chunks):
        copy(c).start()
    phi = phi_ref[...].T
    tops, sums, totals = [], [], []
    for c in range(chunks):
        copy(c).wait()
        part = held[pl.ds(c * rows, rows), :]
        logits = lax.dot_general(phi, part, (((1,), (1,)), ((), ())), preferred_element_type=F32)
        logits_ref[:, pl.ds(c * rows, rows)] = logits
        top = jnp.max(logits, axis=1, keepdims=True)
        spread = jnp.exp(logits - top)
        tops.append(top)
        totals.append(jnp.sum(spread, axis=1, keepdims=True))
        sums.append(jnp.dot(spread.astype(BF16), part, preferred_element_type=F32))
    top = functools.reduce(jnp.maximum, tops)
    scales = [jnp.exp(t - top) for t in tops]
    packed_ref[:, :width] = sum(s * v for s, v in zip(scales, sums))
    total = sum(s * v for s, v in zip(scales, totals))
    lane = lax.broadcasted_iota(jnp.int32, (top.shape[0], LANES), 1)
    packed_ref[:, width:] = jnp.where(lane == 0, top, total)


def slot_sums(phi, tokens, chunks=4):
    slots, (count, width) = phi.shape[1], tokens.shape
    return pl.pallas_call(
        functools.partial(slot_sums_kernel, chunks),
        out_shape=(
            jax.ShapeDtypeStruct((slots, width + LANES), F32),
            jax.ShapeDtypeStruct((slots, count), F32),
        ),
        in_specs=[VMEM, pl.BlockSpec(memory_space=pl.ANY)],
        out_specs=(VMEM, VMEM),
        scratch_shapes=[pltpu.VMEM(tokens.shape, BF16), pltpu.SemaphoreType.DMA((chunks,))],
        compiler_params=params(16),
    )(phi, tokens)


def slot_inputs_kernel(*refs):
    *packed, out_ref = refs
    width = out_ref.shape[1]
    tops = [p[:, width : width + 1] for p in packed]
    top = functools.reduce(jnp.maximum, tops)
    scales = [jnp.exp(t - top) for t in tops]
    total = sum(s * p[:, width + 1 : width + 2] for s, p in zip(scales, packed))
    out_ref[...] = sum(s * p[:, :width] for s, p in zip(scales, packed)) / total


def slot_inputs(packed):
    slots, wide = packed[0].shape
    return pl.pallas_call(
        slot_inputs_kernel,
        out_shape=jax.ShapeDtypeStruct((slots, wide - LANES), F32),
        in_specs=[VMEM] * len(packed),
        out_specs=VMEM,
        cost_estimate=pl.CostEstimate(flops=10_000_000_000, bytes_accessed=0, transcendentals=0),
        compiler_params=params(4),
    )(*packed)


def gelu(v):
    return 0.5 * v * (1.0 + jnp.tanh(0.7978845608028654 * (v + 0.044715 * v * v * v)))


def experts_kernel(clips, *refs):
    x_refs, (first_ref, second_ref), out_refs = refs[:clips], refs[clips:-clips], refs[-clips:]
    for e in range(first_ref.shape[0]):
        x = jnp.concatenate([x_ref[e : e + 1, :] for x_ref in x_refs], axis=0).astype(BF16)
        hidden = gelu(jnp.dot(x, first_ref[e], preferred_element_type=F32)).astype(BF16)
        value = jnp.dot(hidden, second_ref[e], preferred_element_type=F32)
        for c in range(clips):
            out_refs[c][e : e + 1, :] = value[c : c + 1, :]


def experts(slot_in, w_in, w_out):
    clips = len(slot_in)
    return pl.pallas_call(
        functools.partial(experts_kernel, clips),
        out_shape=[jax.ShapeDtypeStruct(x.shape, F32) for x in slot_in],
        in_specs=[VMEM] * (clips + 2),
        out_specs=[VMEM] * clips,
        compiler_params=params(4),
    )(*slot_in, w_in, w_out)


def pack_kernel(*refs):
    *values, logits_ref, out_ref = refs
    width = values[0].shape[1]
    out_ref[:, :width] = sum(v[...] for v in values).astype(BF16).astype(F32)
    out_ref[:, width:] = logits_ref[...]


def pack(values, logits):
    slots, width = values[0].shape
    return pl.pallas_call(
        pack_kernel,
        out_shape=jax.ShapeDtypeStruct((slots, width + logits.shape[1]), F32),
        in_specs=[VMEM] * (len(values) + 1),
        out_specs=VMEM,
        compiler_params=params(4),
    )(*values, logits)


def mix_kernel(*refs):
    *slot_out, logits_ref, out_ref = refs
    logits = logits_ref[...]
    weight = jnp.exp(logits - jnp.max(logits, axis=0, keepdims=True))
    weight = (weight / jnp.sum(weight, axis=0, keepdims=True)).astype(BF16)
    width = out_ref.shape[1]
    values = jnp.concatenate([s[:, :width] for s in slot_out], axis=0).astype(BF16)
    out_ref[...] = lax.dot_general(
        weight, values, (((0,), (0,)), ((), ())), preferred_element_type=F32
    ).astype(BF16)


def mix(packed, logits, width):
    return pl.pallas_call(
        mix_kernel,
        out_shape=jax.ShapeDtypeStruct((logits.shape[1], width), BF16),
        in_specs=[VMEM] * (len(packed) + 1),
        out_specs=VMEM,
        compiler_params=params(8),
    )(*packed, logits)


def on_device(sizes, tokens, phi, w_in, w_out):
    cores, seqs, groups = sizes
    count, width = tokens.shape
    packed, logits = slot_sums(phi, tokens)
    own_in = slot_inputs(gathered(packed, "seq", seqs))
    slot_in = gathered(own_in, "dp", cores)
    partial = experts(slot_in, w_in, w_out)
    own = partial[0]
    for step in range(1, cores):
        own = own + lax.ppermute(partial[step], "dp", partners(cores, step))
    mine = pack(gathered(own, "seq", seqs), logits)
    everyone = gathered(mine, "expert", groups)
    rows = count // groups
    all_logits = jnp.concatenate([v[:, width:] for v in everyone], axis=0)
    first = lax.axis_index("expert") * rows
    return mix(everyone, lax.dynamic_slice_in_dim(all_logits, first, rows, axis=1), width)


def solution(mesh):
    sizes = tuple(mesh.shape[axis] for axis in ("dp", "seq", "expert"))
    placed = (
        P(("dp", "seq"), None),
        P(None, "expert"),
        P("expert", None, ("dp", "seq")),
        P("expert", ("dp", "seq"), None),
    )
    return jax.shard_map(
        functools.partial(on_device, sizes),
        mesh=mesh,
        in_specs=placed,
        out_specs=P(("dp", "seq", "expert"), None),
        check_vma=False,
    )
```

time: 188 us -> 37.8 us (0.20)
  blocking collectives: 76.6 us -> 0 us
  waiting for transfers between devices: 73.4 us -> 11.4 us
  matrix products: 18.9 us -> 0 us
  starting transfers between devices: 0.01 us -> 14 us
  between operations: 14.1 us -> 0.11 us
  Pallas kernels: 0 us -> 8.84 us
  other arithmetic: 3.1 us -> 0.09 us
    reduce_scatter x1 -> x0, waiting for transfers between devices: 73.4 us -> none  [on_device(): lax.psum_scatter(local_numer, 'expert', scatter_dimension=0, tiled=True)]
    psum x2 -> x0, blocking collectives: 43.3 us -> none  [the longest x1 27.6 us: on_device(): totals = lax.psum(partial_value, ('dp', 'seq'))]
    pmax x2 -> x0, blocking collectives: 23.3 us -> none  [the longest x1 12 us: on_device(): slot_max = lax.pmax(jnp.max(logits, axis=1), 'seq')]
    dot_general x4 -> x0, matrix products: 18.9 us -> none  [the longest x1 8.04 us: on_device(): jnp.einsum('cef,efd->ced', hidden, w_out, preferred_element_type=jnp.floa...]
    ppermute x0 -> x11, starting transfers between devices: none -> 14 us  [the longest x10 13.8 us: gathered(): lax.ppermute(x, axis, partners(n, step))]
    ppermute x0 -> x11, waiting for transfers between devices: none -> 11.4 us  [the longest x10 10.3 us: gathered(): lax.ppermute(x, axis, partners(n, step))]
    pallas_call x0 -> x5, Pallas kernels: none -> 8.84 us  [the longest x1 4.87 us: slot_sums(): pl.pallas_call(functools.partial(slot_sums_kernel, chunks), out_shape=(ja...]
    unnamed x1 -> x0, blocking collectives: 8.17 us -> none
  transfers between devices with their start and end apart: 1 -> 11, of which waited for: 1 -> 10; matrix products, arithmetic and copies ran while one was open for 0% -> 0% of each run, Pallas kernels for 0% -> 0%
where the time goes in v1:
time: 37.8 us; the launch traced here: 37.6 us
  starting transfers between devices  14 us (37%)
  waiting for transfers between devices  11.4 us (30%)
  Pallas kernels  8.84 us (23%)
  local copies, waits for them, and re-layouts  3.22 us (9%)
    ppermute x10, starting transfers between devices, gathered(): lax.ppermute(x, axis, partners(n, step))  13.8 us
    ppermute x10, waiting for transfers between devices, gathered(): lax.ppermute(x, axis, partners(n, step))  10.3 us
    pallas_call x1, Pallas kernels, slot_sums(): pl.pallas_call(functools.partial(slot_sums_kernel, chunks), out_shape=(ja...  4.87 us
    unnamed x11, local copies, waits for them, and re-layouts  3.22 us
    pallas_call x1, Pallas kernels, experts(): pl.pallas_call(functools.partial(experts_kernel, clips), out_shape=[jax.S...  2.34 us
    pallas_call x1, Pallas kernels, mix(): pl.pallas_call(mix_kernel, out_shape=jax.ShapeDtypeStruct((logits.shape[1...  1.46 us
    ppermute x1, waiting for transfers between devices, on_device(): own = own + lax.ppermute(partial[step], 'dp', partners(cores, step))  1.03 us
  transfers between devices with their start and end apart: 11, of which 10 were waited for; matrix products, arithmetic and copies ran while one was open for 0% of the time, Pallas kernels for 0%

profile of v1, /device:TPU:0, one launch (start us, length us, event | category | flops | bytes accessed | tf_op | source)
XLA Modules:
  0.0 37.6 jit_solution(7771901837762729338)
XLA Ops:
  0.0 1.0 %copy.5.phi_ref = bf16[2048,2]{1,0:T(8,128)(2,1)S(1)} copy(bf16[2048,2]{0,1:T(2,128)(2,1)} %param.5) | data formatting | bytes 16384 | tf_op args[1]
  1.0 0.0 copy-start
  1.0 2.2 %copy-done = bf16[1024,2048]{1,0:T(8,128)(2,1)S(1)} copy-done((bf16[1024,2048]{1,0:T(8,128)(2,1)S(1)}, bf16[1024,2048]{1,0:T(8,128)(2,1)}, u32[]{:S(2)}) %copy-start) | copy-done | bytes 4194328
  3.2 4.9 %shard_map.46 = (f32[2,2176]{1,0:T(2,128)S(1)}, f32[2,1024]{1,0:T(2,128)S(1)}) custom-call(bf16[2048,2]{1,0:T(8,128)(2,1)S(1)} %copy.5.phi_ref, bf16[1024,2048]{1,0:T(8,128)(2,1)S(1)} %copy-done), custom_call_target="tpu_custom_call" | custom-call | tf_op jit(solution)/shard_map/pallas_call | solution.py:60
  8.1 0.0 slice-start
  8.1 0.0 slice-start.2
  8.1 0.0 slice-start.1
  8.1 0.0 slice-start.3
  8.1 5.1 %collective-permute-start.2 = (f32[2,2176]{1,0:T(2,128)S(1)}, f32[2,2176]{1,0:T(2,128)S(1)}, u32[]{:S(2)}, u32[]{:S(2)}) collective-permute-start(f32[2,2176]{1,0:T(2,128)S(1)} %get-tuple-element.9.refs_0_), channel_id=1, source_target_pairs={{0,12},{4,8},{8,4},{12,0},{1,13},{5,9},{9,5},{13,1},{2,14},{6,10},... | collective-permute-start | bytes 52232 | tf_op jit(solution)/shard_map/ppermute | solution.py:26
  13.2 0.0 collective-permute-start.1
  13.2 0.6 %collective-permute-start = (f32[2,2176]{1,0:T(2,128)S(1)}, f32[2,2176]{1,0:T(2,128)S(1)}, u32[]{:S(2)}, u32[]{:S(2)}) collective-permute-start(f32[2,2176]{1,0:T(2,128)S(1)} %get-tuple-element.9.refs_0_), channel_id=1, source_target_pairs={{0,4},{4,0},{8,12},{12,8},{1,5},{5,1},{9,13},{13,9},{2,6},{6,2},{1... | collective-permute-start | bytes 52232 | tf_op jit(solution)/shard_map/ppermute | solution.py:26
  13.9 1.1 %collective-permute-done.2.refs_3_ = f32[2,2176]{1,0:T(2,128)S(1)} collective-permute-done((f32[2,2176]{1,0:T(2,128)S(1)}, f32[2,2176]{1,0:T(2,128)S(1)}, u32[]{:S(2)}, u32[]{:S(2)}) %collective-permute-start.2) | collective-permute-done | bytes 17440 | tf_op jit(solution)/shard_map/ppermute | solution.py:26
  15.0 2.9 %collective-permute-done.1.refs_2_ = f32[2,2176]{1,0:T(2,128)S(1)} collective-permute-done((f32[2,2176]{1,0:T(2,128)S(1)}, f32[2,2176]{1,0:T(2,128)S(1)}, u32[]{:S(2)}, u32[]{:S(2)}) %collective-permute-start.1) | collective-permute-done | bytes 17440 | tf_op jit(solution)/shard_map/ppermute | solution.py:26
  17.9 0.0 collective-permute-done.refs_1_
  17.9 0.1 shard_map.47.refs_0_
  18.0 0.0 collective-permute-start.3
  18.1 1.2 %collective-permute-done.3.refs_1_ = f32[2,2048]{1,0:T(2,128)S(1)} collective-permute-done((f32[2,2048]{1,0:T(2,128)S(1)}, f32[2,2048]{1,0:T(2,128)S(1)}, u32[]{:S(2)}, u32[]{:S(2)}) %collective-permute-start.3) | collective-permute-done | bytes 16416 | tf_op jit(solution)/shard_map/ppermute | solution.py:26
  19.2 0.0 slice-done
  19.2 0.0 slice-done.2
  19.2 0.0 slice-done.1
  19.3 0.0 slice-done.3
  19.3 2.3 %shard_map.48 = (f32[2,2048]{1,0:T(2,128)S(1)}, f32[2,2048]{1,0:T(2,128)S(1)}) custom-call(f32[2,2048]{1,0:T(2,128)S(1)} %shard_map.47.refs_0_, f32[2,2048]{1,0:T(2,128)S(1)} %collective-permute-done.3.refs_1_, bf16[2,2048,1024]{2,1,0:T(8,128)(2,1)S(1)} %bitcast.1, bf16[2,1024,2048]{2,1,0:T(8,128)(2,1)S(1)} %bitcast.3), custom_call_target="tpu_custom_call" | custom-call | tf_op jit(solution)/shard_map/pallas_call | solution.py:111
  21.6 0.2 collective-permute-start.4
  21.8 1.0 %collective-permute-done.4 = f32[2,2048]{1,0:T(2,128)S(1)} collective-permute-done((f32[2,2048]{1,0:T(2,128)S(1)}, f32[2,2048]{1,0:T(2,128)S(1)}, u32[]{:S(2)}, u32[]{:S(2)}) %collective-permute-start.4) | collective-permute-done | bytes 16416 | tf_op jit(solution)/shard_map/ppermute | solution.py:169
  22.8 1.5 %collective-permute-start.7 = (f32[2,2048]{1,0:T(2,128)S(1)}, f32[2,2048]{1,0:T(2,128)S(1)}, u32[]{:S(2)}, u32[]{:S(2)}) collective-permute-start(f32[2,2048]{1,0:T(2,128)S(1)} %add.6.refs_0_), channel_id=1, source_target_pairs={{0,12},{4,8},{8,4},{12,0},{1,13},{5,9},{9,5},{13,1},{2,14},{6,10},... | collective-permute-start | bytes 49160 | tf_op jit(solution)/shard_map/ppermute | solution.py:26
  24.4 0.6 %collective-permute-start.6 = (f32[2,2048]{1,0:T(2,128)S(1)}, f32[2,2048]{1,0:T(2,128)S(1)}, u32[]{:S(2)}, u32[]{:S(2)}) collective-permute-start(f32[2,2048]{1,0:T(2,128)S(1)} %add.6.refs_0_), channel_id=1, source_target_pairs={{0,8},{4,12},{8,0},{12,4},{1,9},{5,13},{9,1},{13,5},{2,10},{6,14},... | collective-permute-start | bytes 49160 | tf_op jit(solution)/shard_map/ppermute | solution.py:26
  25.0 2.3 %collective-permute-start.5 = (f32[2,2048]{1,0:T(2,128)S(1)}, f32[2,2048]{1,0:T(2,128)S(1)}, u32[]{:S(2)}, u32[]{:S(2)}) collective-permute-start(f32[2,2048]{1,0:T(2,128)S(1)} %add.6.refs_0_), channel_id=1, source_target_pairs={{0,4},{4,0},{8,12},{12,8},{1,5},{5,1},{9,13},{13,9},{2,6},{6,2},{1... | collective-permute-start | bytes 49160 | tf_op jit(solution)/shard_map/ppermute | solution.py:26
  27.3 1.3 %collective-permute-done.7.refs_3_ = f32[2,2048]{1,0:T(2,128)S(1)} collective-permute-done((f32[2,2048]{1,0:T(2,128)S(1)}, f32[2,2048]{1,0:T(2,128)S(1)}, u32[]{:S(2)}, u32[]{:S(2)}) %collective-permute-start.7) | collective-permute-done | bytes 16416 | tf_op jit(solution)/shard_map/ppermute | solution.py:26
  28.6 0.4 %collective-permute-done.6.refs_2_ = f32[2,2048]{1,0:T(2,128)S(1)} collective-permute-done((f32[2,2048]{1,0:T(2,128)S(1)}, f32[2,2048]{1,0:T(2,128)S(1)}, u32[]{:S(2)}, u32[]{:S(2)}) %collective-permute-start.6) | collective-permute-done | bytes 16416 | tf_op jit(solution)/shard_map/ppermute | solution.py:26
  29.0 0.2 collective-permute-done.5.refs_1_
  29.2 2.5 %collective-permute-start.10 = (f32[2,3072]{1,0:T(2,128)S(1)}, f32[2,3072]{1,0:T(2,128)S(1)}, u32[]{:S(2)}, u32[]{:S(2)}) collective-permute-start(f32[2,3072]{1,0:T(2,128)S(1)} %shard_map.49.refs_0_), channel_id=1, source_target_pairs={{0,3},{1,2},{2,1},{3,0},{4,7},{5,6},{6,5},{7,4},{8,11},{9,10},{10,... | collective-permute-start | bytes 73736 | tf_op jit(solution)/shard_map/ppermute | solution.py:26
  31.7 0.5 %collective-permute-start.9 = (f32[2,3072]{1,0:T(2,128)S(1)}, f32[2,3072]{1,0:T(2,128)S(1)}, u32[]{:S(2)}, u32[]{:S(2)}) collective-permute-start(f32[2,3072]{1,0:T(2,128)S(1)} %shard_map.49.refs_0_), channel_id=1, source_target_pairs={{0,2},{1,3},{2,0},{3,1},{4,6},{5,7},{6,4},{7,5},{8,10},{9,11},{10,... | collective-permute-start | bytes 73736 | tf_op jit(solution)/shard_map/ppermute | solution.py:26
  32.2 0.5 %collective-permute-start.8 = (f32[2,3072]{1,0:T(2,128)S(1)}, f32[2,3072]{1,0:T(2,128)S(1)}, u32[]{:S(2)}, u32[]{:S(2)}) collective-permute-start(f32[2,3072]{1,0:T(2,128)S(1)} %shard_map.49.refs_0_), channel_id=1, source_target_pairs={{0,1},{1,0},{2,3},{3,2},{4,5},{5,4},{6,7},{7,6},{8,9},{9,8},{10,11... | collective-permute-start | bytes 73736 | tf_op jit(solution)/shard_map/ppermute | solution.py:26
  32.8 1.2 %collective-permute-done.10.refs_3_ = f32[2,3072]{1,0:T(2,128)S(1)} collective-permute-done((f32[2,3072]{1,0:T(2,128)S(1)}, f32[2,3072]{1,0:T(2,128)S(1)}, u32[]{:S(2)}, u32[]{:S(2)}) %collective-permute-start.10) | collective-permute-done | bytes 24608 | tf_op jit(solution)/shard_map/ppermute | solution.py:26
  34.0 1.5 %collective-permute-done.9.refs_2_ = f32[2,3072]{1,0:T(2,128)S(1)} collective-permute-done((f32[2,3072]{1,0:T(2,128)S(1)}, f32[2,3072]{1,0:T(2,128)S(1)}, u32[]{:S(2)}, u32[]{:S(2)}) %collective-permute-start.9) | collective-permute-done | bytes 24608 | tf_op jit(solution)/shard_map/ppermute | solution.py:26
  35.5 0.5 %collective-permute-done.8.refs_1_ = f32[2,3072]{1,0:T(2,128)S(1)} collective-permute-done((f32[2,3072]{1,0:T(2,128)S(1)}, f32[2,3072]{1,0:T(2,128)S(1)}, u32[]{:S(2)}, u32[]{:S(2)}) %collective-permute-start.8) | collective-permute-done | bytes 24608 | tf_op jit(solution)/shard_map/ppermute | solution.py:26
  36.0 0.1 fusion.2.refs_4_
  36.1 1.5 %shard_map.50 = bf16[256,2048]{1,0:T(8,128)(2,1)} custom-call(f32[2,3072]{1,0:T(2,128)S(1)} %shard_map.49.refs_0_, f32[2,3072]{1,0:T(2,128)S(1)} %collective-permute-done.8.refs_1_, f32[2,3072]{1,0:T(2,128)S(1)} %collective-permute-done.9.refs_2_, f32[2,3072]{1,0:T(2,128)S(1)} %collective-permute-done.10.refs_3_, f32[8,256]{1,0:T(8,128)S(1)} %fusion.2.refs_4_), custom_call_target="tpu_custom_call" | custom-call | tf_op jit(solution)/shard_map/pallas_call | solution.py:151
  (8 shorter events, 0.0 us)
Async XLA Ops:
  1.0 2.2 %copy-start = (bf16[1024,2048]{1,0:T(8,128)(2,1)S(1)}, bf16[1024,2048]{1,0:T(8,128)(2,1)}, u32[]{:S(2)}) copy-start(bf16[1024,2048]{1,0:T(8,128)(2,1)} %tokens_ref.1) | copy-start | bytes 12582916
  8.1 11.2 %slice-start = ((s8[8388608]{0:T(1024)(128)(4,1)}), s8[4194304]{0:T(1024)(128)(4,1)S(1)}, s32[]{:S(2)}) async-start(s8[8388608]{0:T(1024)(128)(4,1)} %bitcast), calls=%async_computation | async-start | bytes 8388608
  8.1 11.2 %slice-start.2 = ((s8[8388608]{0:T(1024)(128)(4,1)}), s8[4194304]{0:T(1024)(128)(4,1)S(1)}, s32[]{:S(2)}) async-start(s8[8388608]{0:T(1024)(128)(4,1)} %bitcast.2), calls=%async_computation.2 | async-start | bytes 8388608
  8.1 11.1 %slice-start.1 = ((s8[8388608]{0:T(1024)(128)(4,1)}), s8[4194304]{0:T(1024)(128)(4,1)S(1)}, s32[]{:S(2)}) async-start(s8[8388608]{0:T(1024)(128)(4,1)} %bitcast), calls=%async_computation.1 | async-start | bytes 8388608
  8.1 11.1 %slice-start.3 = ((s8[8388608]{0:T(1024)(128)(4,1)}), s8[4194304]{0:T(1024)(128)(4,1)S(1)}, s32[]{:S(2)}) async-start(s8[8388608]{0:T(1024)(128)(4,1)} %bitcast.2), calls=%async_computation.3 | async-start | bytes 8388608
  8.1 6.8 %collective-permute-start.2 = (f32[2,2176]{1,0:T(2,128)S(1)}, f32[2,2176]{1,0:T(2,128)S(1)}, u32[]{:S(2)}, u32[]{:S(2)}) collective-permute-start(f32[2,2176]{1,0:T(2,128)S(1)} %get-tuple-element.9.refs_0_), channel_id=1, source_target_pairs={{0,12},{4,8},{8,4},{12,0},{1,13},{5,9},{9,5},{13,1},{2,14},{6,10},... | collective-permute-start | bytes 52232 | tf_op jit(solution)/shard_map/ppermute | solution.py:26
  13.2 4.6 %collective-permute-start.1 = (f32[2,2176]{1,0:T(2,128)S(1)}, f32[2,2176]{1,0:T(2,128)S(1)}, u32[]{:S(2)}, u32[]{:S(2)}) collective-permute-start(f32[2,2176]{1,0:T(2,128)S(1)} %get-tuple-element.9.refs_0_), channel_id=1, source_target_pairs={{0,8},{4,12},{8,0},{12,4},{1,9},{5,13},{9,1},{13,5},{2,10},{6,14},... | collective-permute-start | bytes 52232 | tf_op jit(solution)/shard_map/ppermute | solution.py:26
  13.2 4.6 %collective-permute-start = (f32[2,2176]{1,0:T(2,128)S(1)}, f32[2,2176]{1,0:T(2,128)S(1)}, u32[]{:S(2)}, u32[]{:S(2)}) collective-permute-start(f32[2,2176]{1,0:T(2,128)S(1)} %get-tuple-element.9.refs_0_), channel_id=1, source_target_pairs={{0,4},{4,0},{8,12},{12,8},{1,5},{5,1},{9,13},{13,9},{2,6},{6,2},{1... | collective-permute-start | bytes 52232 | tf_op jit(solution)/shard_map/ppermute | solution.py:26
  18.0 1.2 %collective-permute-start.3 = (f32[2,2048]{1,0:T(2,128)S(1)}, f32[2,2048]{1,0:T(2,128)S(1)}, u32[]{:S(2)}, u32[]{:S(2)}) collective-permute-start(f32[2,2048]{1,0:T(2,128)S(1)} %shard_map.47.refs_0_), channel_id=1, source_target_pairs={{0,16},{16,0},{1,17},{17,1},{2,18},{18,2},{3,19},{19,3},{4,20},{20... | collective-permute-start | bytes 49160 | tf_op jit(solution)/shard_map/ppermute | solution.py:26
  21.6 1.2 %collective-permute-start.4 = (f32[2,2048]{1,0:T(2,128)S(1)}, f32[2,2048]{1,0:T(2,128)S(1)}, u32[]{:S(2)}, u32[]{:S(2)}) collective-permute-start(f32[2,2048]{1,0:T(2,128)S(1)} %get-tuple-element.11), channel_id=1, source_target_pairs={{0,16},{16,0},{1,17},{17,1},{2,18},{18,2},{3,19},{19,3},{4,20},{20... | collective-permute-start | bytes 49160 | tf_op jit(solution)/shard_map/ppermute | solution.py:169
  22.8 5.7 %collective-permute-start.7 = (f32[2,2048]{1,0:T(2,128)S(1)}, f32[2,2048]{1,0:T(2,128)S(1)}, u32[]{:S(2)}, u32[]{:S(2)}) collective-permute-start(f32[2,2048]{1,0:T(2,128)S(1)} %add.6.refs_0_), channel_id=1, source_target_pairs={{0,12},{4,8},{8,4},{12,0},{1,13},{5,9},{9,5},{13,1},{2,14},{6,10},... | collective-permute-start | bytes 49160 | tf_op jit(solution)/shard_map/ppermute | solution.py:26
  24.4 4.7 %collective-permute-start.6 = (f32[2,2048]{1,0:T(2,128)S(1)}, f32[2,2048]{1,0:T(2,128)S(1)}, u32[]{:S(2)}, u32[]{:S(2)}) collective-permute-start(f32[2,2048]{1,0:T(2,128)S(1)} %add.6.refs_0_), channel_id=1, source_target_pairs={{0,8},{4,12},{8,0},{12,4},{1,9},{5,13},{9,1},{13,5},{2,10},{6,14},... | collective-permute-start | bytes 49160 | tf_op jit(solution)/shard_map/ppermute | solution.py:26
  25.0 4.2 %collective-permute-start.5 = (f32[2,2048]{1,0:T(2,128)S(1)}, f32[2,2048]{1,0:T(2,128)S(1)}, u32[]{:S(2)}, u32[]{:S(2)}) collective-permute-start(f32[2,2048]{1,0:T(2,128)S(1)} %add.6.refs_0_), channel_id=1, source_target_pairs={{0,4},{4,0},{8,12},{12,8},{1,5},{5,1},{9,13},{13,9},{2,6},{6,2},{1... | collective-permute-start | bytes 49160 | tf_op jit(solution)/shard_map/ppermute | solution.py:26
  29.2 4.8 %collective-permute-start.10 = (f32[2,3072]{1,0:T(2,128)S(1)}, f32[2,3072]{1,0:T(2,128)S(1)}, u32[]{:S(2)}, u32[]{:S(2)}) collective-permute-start(f32[2,3072]{1,0:T(2,128)S(1)} %shard_map.49.refs_0_), channel_id=1, source_target_pairs={{0,3},{1,2},{2,1},{3,0},{4,7},{5,6},{6,5},{7,4},{8,11},{9,10},{10,... | collective-permute-start | bytes 73736 | tf_op jit(solution)/shard_map/ppermute | solution.py:26
  31.7 3.8 %collective-permute-start.9 = (f32[2,3072]{1,0:T(2,128)S(1)}, f32[2,3072]{1,0:T(2,128)S(1)}, u32[]{:S(2)}, u32[]{:S(2)}) collective-permute-start(f32[2,3072]{1,0:T(2,128)S(1)} %shard_map.49.refs_0_), channel_id=1, source_target_pairs={{0,2},{1,3},{2,0},{3,1},{4,6},{5,7},{6,4},{7,5},{8,10},{9,11},{10,... | collective-permute-start | bytes 73736 | tf_op jit(solution)/shard_map/ppermute | solution.py:26
  32.2 3.8 %collective-permute-start.8 = (f32[2,3072]{1,0:T(2,128)S(1)}, f32[2,3072]{1,0:T(2,128)S(1)}, u32[]{:S(2)}, u32[]{:S(2)}) collective-permute-start(f32[2,3072]{1,0:T(2,128)S(1)} %shard_map.49.refs_0_), channel_id=1, source_target_pairs={{0,1},{1,0},{2,3},{3,2},{4,5},{5,4},{6,7},{7,6},{8,9},{9,8},{10,11... | collective-permute-start | bytes 73736 | tf_op jit(solution)/shard_map/ppermute | solution.py:26

commit v2 on v1

--- a/solution.py
+++ b/solution.py
@@ -12,6 +12,10 @@
 VMEM = pl.BlockSpec(memory_space=pltpu.VMEM)
 
 
+def in_hbm(x):
+    return pltpu.with_memory_space_constraint(x, pltpu.HBM)
+
+
 def params(mib):
     return pltpu.CompilerParams(vmem_limit_bytes=mib << 20)
 
@@ -26,48 +30,66 @@
     return [x] + [lax.ppermute(x, axis, partners(n, step)) for step in range(1, n)]
 
 
-def slot_sums_kernel(chunks, phi_ref, tokens_ref, packed_ref, logits_ref, held, sems):
-    rows, width = tokens_ref.shape[0] // chunks, tokens_ref.shape[1]
+def slot_sums_kernel(chunks, phi_hbm, tokens_hbm, packed_ref, logits_ref, phi_ref, held, sems):
+    slots, width = phi_ref.shape
+    rows = tokens_hbm.shape[0] // chunks
 
     def copy(c):
         part = pl.ds(c * rows, rows)
-        return pltpu.make_async_copy(tokens_ref.at[part], held.at[part], sems.at[c])
-
+        return pltpu.make_async_copy(tokens_hbm.at[part], held.at[part], sems.at[c])
+
+    phi_copy = pltpu.make_async_copy(phi_hbm, phi_ref, sems.at[chunks])
+    phi_copy.start()
     for c in range(chunks):
         copy(c).start()
-    phi = phi_ref[...].T
+    phi_copy.wait()
+    spare = jnp.zeros((8 - slots % 8, width), F32)
+    phi = jnp.concatenate([phi_ref[...].astype(F32), spare], axis=0).T.astype(BF16)
     tops, sums, totals = [], [], []
-    for c in range(chunks):
-        copy(c).wait()
-        part = held[pl.ds(c * rows, rows), :]
-        logits = lax.dot_general(phi, part, (((1,), (1,)), ((), ())), preferred_element_type=F32)
-        logits_ref[:, pl.ds(c * rows, rows)] = logits
+
+    def finish(c, by_token):
+        part = pl.ds(c * rows, rows)
+        logits = by_token.T[:slots]
+        logits_ref[:, part] = logits
         top = jnp.max(logits, axis=1, keepdims=True)
         spread = jnp.exp(logits - top)
         tops.append(top)
         totals.append(jnp.sum(spread, axis=1, keepdims=True))
-        sums.append(jnp.dot(spread.astype(BF16), part, preferred_element_type=F32))
+        sums.append(jnp.dot(spread.astype(BF16), held[part, :], preferred_element_type=F32))
+
+    before = None
+    for c in range(chunks):
+        copy(c).wait()
+        now = jnp.dot(held[pl.ds(c * rows, rows), :], phi, preferred_element_type=F32)
+        if c:
+            finish(c - 1, before)
+        before = now
+    finish(chunks - 1, before)
     top = functools.reduce(jnp.maximum, tops)
     scales = [jnp.exp(t - top) for t in tops]
     packed_ref[:, :width] = sum(s * v for s, v in zip(scales, sums))
     total = sum(s * v for s, v in zip(scales, totals))
-    lane = lax.broadcasted_iota(jnp.int32, (top.shape[0], LANES), 1)
+    lane = lax.broadcasted_iota(jnp.int32, (slots, LANES), 1)
     packed_ref[:, width:] = jnp.where(lane == 0, top, total)
 
 
 def slot_sums(phi, tokens, chunks=4):
-    slots, (count, width) = phi.shape[1], tokens.shape
+    (slots, width), count = phi.shape, tokens.shape[0]
     return pl.pallas_call(
         functools.partial(slot_sums_kernel, chunks),
         out_shape=(
             jax.ShapeDtypeStruct((slots, width + LANES), F32),
             jax.ShapeDtypeStruct((slots, count), F32),
         ),
-        in_specs=[VMEM, pl.BlockSpec(memory_space=pl.ANY)],
+        in_specs=[pl.BlockSpec(memory_space=pltpu.HBM)] * 2,
         out_specs=(VMEM, VMEM),
-        scratch_shapes=[pltpu.VMEM(tokens.shape, BF16), pltpu.SemaphoreType.DMA((chunks,))],
+        scratch_shapes=[
+            pltpu.VMEM(phi.shape, BF16),
+            pltpu.VMEM(tokens.shape, BF16),
+            pltpu.SemaphoreType.DMA((chunks + 1,)),
+        ],
         compiler_params=params(16),
-    )(phi, tokens)
+    )(in_hbm(phi), in_hbm(tokens))
 
 
 def slot_inputs_kernel(*refs):
@@ -135,24 +157,36 @@
     )(*values, logits)
 
 
-def mix_kernel(*refs):
-    *slot_out, logits_ref, out_ref = refs
+def mix_kernel(chunks, *refs):
+    *slot_out, logits_ref, out_hbm, rows_ref, sems = refs
     logits = logits_ref[...]
     weight = jnp.exp(logits - jnp.max(logits, axis=0, keepdims=True))
     weight = (weight / jnp.sum(weight, axis=0, keepdims=True)).astype(BF16)
-    width = out_ref.shape[1]
+    rows, width = rows_ref.shape[0] // chunks, rows_ref.shape[1]
     values = jnp.concatenate([s[:, :width] for s in slot_out], axis=0).astype(BF16)
-    out_ref[...] = lax.dot_general(
-        weight, values, (((0,), (0,)), ((), ())), preferred_element_type=F32
-    ).astype(BF16)
-
-
-def mix(packed, logits, width):
-    return pl.pallas_call(
-        mix_kernel,
-        out_shape=jax.ShapeDtypeStruct((logits.shape[1], width), BF16),
+    copies = []
+    for c in range(chunks):
+        part = pl.ds(c * rows, rows)
+        rows_ref[part, :] = lax.dot_general(
+            weight[:, c * rows : (c + 1) * rows],
+            values,
+            (((0,), (0,)), ((), ())),
+            preferred_element_type=F32,
+        ).astype(BF16)
+        copies.append(pltpu.make_async_copy(rows_ref.at[part], out_hbm.at[part], sems.at[c]))
+        copies[-1].start()
+    for copy in copies:
+        copy.wait()
+
+
+def mix(packed, logits, width, chunks=4):
+    shape = (logits.shape[1], width)
+    return pl.pallas_call(
+        functools.partial(mix_kernel, chunks),
+        out_shape=jax.ShapeDtypeStruct(shape, BF16),
         in_specs=[VMEM] * (len(packed) + 1),
-        out_specs=VMEM,
+        out_specs=pl.BlockSpec(memory_space=pl.ANY),
+        scratch_shapes=[pltpu.VMEM(shape, BF16), pltpu.SemaphoreType.DMA((chunks,))],
         compiler_params=params(8),
     )(*packed, logits)
 
@@ -160,7 +194,7 @@
 def on_device(sizes, tokens, phi, w_in, w_out):
     cores, seqs, groups = sizes
     count, width = tokens.shape
-    packed, logits = slot_sums(phi, tokens)
+    packed, logits = slot_sums(phi.T, tokens)
     own_in = slot_inputs(gathered(packed, "seq", seqs))
     slot_in = gathered(own_in, "dp", cores)
     partial = experts(slot_in, w_in, w_out)

time: 37.8 us -> 33.1 us (0.88)
  local copies, waits for them, and re-layouts: 3.22 us -> 0.03 us
  Pallas kernels: 8.84 us -> 7.32 us
    unnamed x11 -> x8, local copies, waits for them, and re-layouts: 3.22 us -> 0.02 us
    pallas_call x1, Pallas kernels: 4.87 us -> 3.52 us  [slot_sums(): pl.pallas_call(functools.partial(slot_sums_kernel, chunks), out_shape=(ja...]
where the time goes in v2:
time: 33.1 us; the launch traced here: 32.9 us
  starting transfers between devices  13.9 us (42%)
  waiting for transfers between devices  11.4 us (34%)
  Pallas kernels  7.32 us (22%)
    ppermute x10, starting transfers between devices, gathered(): lax.ppermute(x, axis, partners(n, step))  13.8 us
    ppermute x10, waiting for transfers between devices, gathered(): lax.ppermute(x, axis, partners(n, step))  10.3 us
    pallas_call x1, Pallas kernels, slot_sums(): pl.pallas_call(functools.partial(slot_sums_kernel, chunks), out_shape=(ja...  3.52 us
    pallas_call x1, Pallas kernels, experts(): pl.pallas_call(functools.partial(experts_kernel, clips), out_shape=[jax.S...  2.34 us
    pallas_call x1, Pallas kernels, mix(): pl.pallas_call(functools.partial(mix_kernel, chunks), out_shape=jax.Shape...  1.28 us
    ppermute x1, waiting for transfers between devices, on_device(): own = own + lax.ppermute(partial[step], 'dp', partners(cores, step))  1.03 us
  transfers between devices with their start and end apart: 11, of which 10 were waited for; matrix products, arithmetic and copies ran while one was open for 0% of the time, Pallas kernels for 0%

profile of v2, /device:TPU:0, one launch (start us, length us, event | category | flops | bytes accessed | tf_op | source)
XLA Modules:
  0.0 32.9 jit_solution(3447425478809855275)
XLA Ops:
  0.0 3.5 %shard_map.46 = (f32[2,2176]{1,0:T(2,128)S(1)}, f32[2,1024]{1,0:T(2,128)S(1)}) custom-call(bf16[2,2048]{1,0:T(2,128)(2,1)} %bitcast.5, bf16[1024,2048]{1,0:T(8,128)(2,1)} %tokens_hbm.1), custom_call_target="tpu_custom_call" | custom-call | tf_op jit(solution)/shard_map/pallas_call | solution.py:78
  3.5 0.0 slice-start
  3.5 0.0 slice-start.2
  3.6 0.0 slice-start.1
  3.6 0.0 slice-start.3
  3.6 5.1 %collective-permute-start.2 = (f32[2,2176]{1,0:T(2,128)S(1)}, f32[2,2176]{1,0:T(2,128)S(1)}, u32[]{:S(2)}, u32[]{:S(2)}) collective-permute-start(f32[2,2176]{1,0:T(2,128)S(1)} %get-tuple-element.9.refs_0_), channel_id=1, source_target_pairs={{0,12},{4,8},{8,4},{12,0},{1,13},{5,9},{9,5},{13,1},{2,14},{6,10},... | collective-permute-start | bytes 52232 | tf_op jit(solution)/shard_map/ppermute | solution.py:30
  8.7 0.0 collective-permute-start.1
  8.7 0.6 %collective-permute-start = (f32[2,2176]{1,0:T(2,128)S(1)}, f32[2,2176]{1,0:T(2,128)S(1)}, u32[]{:S(2)}, u32[]{:S(2)}) collective-permute-start(f32[2,2176]{1,0:T(2,128)S(1)} %get-tuple-element.9.refs_0_), channel_id=1, source_target_pairs={{0,4},{4,0},{8,12},{12,8},{1,5},{5,1},{9,13},{13,9},{2,6},{6,2},{1... | collective-permute-start | bytes 52232 | tf_op jit(solution)/shard_map/ppermute | solution.py:30
  9.3 1.1 %collective-permute-done.2.refs_3_ = f32[2,2176]{1,0:T(2,128)S(1)} collective-permute-done((f32[2,2176]{1,0:T(2,128)S(1)}, f32[2,2176]{1,0:T(2,128)S(1)}, u32[]{:S(2)}, u32[]{:S(2)}) %collective-permute-start.2) | collective-permute-done | bytes 17440 | tf_op jit(solution)/shard_map/ppermute | solution.py:30
  10.4 2.9 %collective-permute-done.1.refs_2_ = f32[2,2176]{1,0:T(2,128)S(1)} collective-permute-done((f32[2,2176]{1,0:T(2,128)S(1)}, f32[2,2176]{1,0:T(2,128)S(1)}, u32[]{:S(2)}, u32[]{:S(2)}) %collective-permute-start.1) | collective-permute-done | bytes 17440 | tf_op jit(solution)/shard_map/ppermute | solution.py:30
  13.3 0.0 collective-permute-done.refs_1_
  13.3 0.1 shard_map.47.refs_0_
  13.5 0.0 collective-permute-start.3
  13.5 1.2 %collective-permute-done.3.refs_1_ = f32[2,2048]{1,0:T(2,128)S(1)} collective-permute-done((f32[2,2048]{1,0:T(2,128)S(1)}, f32[2,2048]{1,0:T(2,128)S(1)}, u32[]{:S(2)}, u32[]{:S(2)}) %collective-permute-start.3) | collective-permute-done | bytes 16416 | tf_op jit(solution)/shard_map/ppermute | solution.py:30
  14.7 0.0 slice-done
  14.7 0.0 slice-done.2
  14.7 0.0 slice-done.1
  14.7 0.0 slice-done.3
  14.7 2.3 %shard_map.48 = (f32[2,2048]{1,0:T(2,128)S(1)}, f32[2,2048]{1,0:T(2,128)S(1)}) custom-call(f32[2,2048]{1,0:T(2,128)S(1)} %shard_map.47.refs_0_, f32[2,2048]{1,0:T(2,128)S(1)} %collective-permute-done.3.refs_1_, bf16[2,2048,1024]{2,1,0:T(8,128)(2,1)S(1)} %bitcast.2, bf16[2,1024,2048]{2,1,0:T(8,128)(2,1)S(1)} %bitcast.4), custom_call_target="tpu_custom_call" | custom-call | tf_op jit(solution)/shard_map/pallas_call | solution.py:133
  17.1 0.2 collective-permute-start.4
  17.2 1.0 %collective-permute-done.4 = f32[2,2048]{1,0:T(2,128)S(1)} collective-permute-done((f32[2,2048]{1,0:T(2,128)S(1)}, f32[2,2048]{1,0:T(2,128)S(1)}, u32[]{:S(2)}, u32[]{:S(2)}) %collective-permute-start.4) | collective-permute-done | bytes 16416 | tf_op jit(solution)/shard_map/ppermute | solution.py:203
  18.3 1.5 %collective-permute-start.7 = (f32[2,2048]{1,0:T(2,128)S(1)}, f32[2,2048]{1,0:T(2,128)S(1)}, u32[]{:S(2)}, u32[]{:S(2)}) collective-permute-start(f32[2,2048]{1,0:T(2,128)S(1)} %add.6.refs_0_), channel_id=1, source_target_pairs={{0,12},{4,8},{8,4},{12,0},{1,13},{5,9},{9,5},{13,1},{2,14},{6,10},... | collective-permute-start | bytes 49160 | tf_op jit(solution)/shard_map/ppermute | solution.py:30
  19.8 0.6 %collective-permute-start.6 = (f32[2,2048]{1,0:T(2,128)S(1)}, f32[2,2048]{1,0:T(2,128)S(1)}, u32[]{:S(2)}, u32[]{:S(2)}) collective-permute-start(f32[2,2048]{1,0:T(2,128)S(1)} %add.6.refs_0_), channel_id=1, source_target_pairs={{0,8},{4,12},{8,0},{12,4},{1,9},{5,13},{9,1},{13,5},{2,10},{6,14},... | collective-permute-start | bytes 49160 | tf_op jit(solution)/shard_map/ppermute | solution.py:30
  20.4 2.3 %collective-permute-start.5 = (f32[2,2048]{1,0:T(2,128)S(1)}, f32[2,2048]{1,0:T(2,128)S(1)}, u32[]{:S(2)}, u32[]{:S(2)}) collective-permute-start(f32[2,2048]{1,0:T(2,128)S(1)} %add.6.refs_0_), channel_id=1, source_target_pairs={{0,4},{4,0},{8,12},{12,8},{1,5},{5,1},{9,13},{13,9},{2,6},{6,2},{1... | collective-permute-start | bytes 49160 | tf_op jit(solution)/shard_map/ppermute | solution.py:30
  22.7 1.3 %collective-permute-done.7.refs_3_ = f32[2,2048]{1,0:T(2,128)S(1)} collective-permute-done((f32[2,2048]{1,0:T(2,128)S(1)}, f32[2,2048]{1,0:T(2,128)S(1)}, u32[]{:S(2)}, u32[]{:S(2)}) %collective-permute-start.7) | collective-permute-done | bytes 16416 | tf_op jit(solution)/shard_map/ppermute | solution.py:30
  24.0 0.4 %collective-permute-done.6.refs_2_ = f32[2,2048]{1,0:T(2,128)S(1)} collective-permute-done((f32[2,2048]{1,0:T(2,128)S(1)}, f32[2,2048]{1,0:T(2,128)S(1)}, u32[]{:S(2)}, u32[]{:S(2)}) %collective-permute-start.6) | collective-permute-done | bytes 16416 | tf_op jit(solution)/shard_map/ppermute | solution.py:30
  24.5 0.2 collective-permute-done.5.refs_1_
  24.6 2.5 %collective-permute-start.10 = (f32[2,3072]{1,0:T(2,128)S(1)}, f32[2,3072]{1,0:T(2,128)S(1)}, u32[]{:S(2)}, u32[]{:S(2)}) collective-permute-start(f32[2,3072]{1,0:T(2,128)S(1)} %shard_map.49.refs_0_), channel_id=1, source_target_pairs={{0,3},{1,2},{2,1},{3,0},{4,7},{5,6},{6,5},{7,4},{8,11},{9,10},{10,... | collective-permute-start | bytes 73736 | tf_op jit(solution)/shard_map/ppermute | solution.py:30
  27.2 0.5 %collective-permute-start.9 = (f32[2,3072]{1,0:T(2,128)S(1)}, f32[2,3072]{1,0:T(2,128)S(1)}, u32[]{:S(2)}, u32[]{:S(2)}) collective-permute-start(f32[2,3072]{1,0:T(2,128)S(1)} %shard_map.49.refs_0_), channel_id=1, source_target_pairs={{0,2},{1,3},{2,0},{3,1},{4,6},{5,7},{6,4},{7,5},{8,10},{9,11},{10,... | collective-permute-start | bytes 73736 | tf_op jit(solution)/shard_map/ppermute | solution.py:30
  27.7 0.5 %collective-permute-start.8 = (f32[2,3072]{1,0:T(2,128)S(1)}, f32[2,3072]{1,0:T(2,128)S(1)}, u32[]{:S(2)}, u32[]{:S(2)}) collective-permute-start(f32[2,3072]{1,0:T(2,128)S(1)} %shard_map.49.refs_0_), channel_id=1, source_target_pairs={{0,1},{1,0},{2,3},{3,2},{4,5},{5,4},{6,7},{7,6},{8,9},{9,8},{10,11... | collective-permute-start | bytes 73736 | tf_op jit(solution)/shard_map/ppermute | solution.py:30
  28.2 1.2 %collective-permute-done.10.refs_3_ = f32[2,3072]{1,0:T(2,128)S(1)} collective-permute-done((f32[2,3072]{1,0:T(2,128)S(1)}, f32[2,3072]{1,0:T(2,128)S(1)}, u32[]{:S(2)}, u32[]{:S(2)}) %collective-permute-start.10) | collective-permute-done | bytes 24608 | tf_op jit(solution)/shard_map/ppermute | solution.py:30
  29.4 1.6 %collective-permute-done.9.refs_2_ = f32[2,3072]{1,0:T(2,128)S(1)} collective-permute-done((f32[2,3072]{1,0:T(2,128)S(1)}, f32[2,3072]{1,0:T(2,128)S(1)}, u32[]{:S(2)}, u32[]{:S(2)}) %collective-permute-start.9) | collective-permute-done | bytes 24608 | tf_op jit(solution)/shard_map/ppermute | solution.py:30
  31.0 0.5 %collective-permute-done.8.refs_1_ = f32[2,3072]{1,0:T(2,128)S(1)} collective-permute-done((f32[2,3072]{1,0:T(2,128)S(1)}, f32[2,3072]{1,0:T(2,128)S(1)}, u32[]{:S(2)}, u32[]{:S(2)}) %collective-permute-start.8) | collective-permute-done | bytes 24608 | tf_op jit(solution)/shard_map/ppermute | solution.py:30
  31.5 0.1 fusion.2.refs_4_
  31.6 1.3 %shard_map.50 = bf16[256,2048]{1,0:T(8,128)(2,1)} custom-call(f32[2,3072]{1,0:T(2,128)S(1)} %shard_map.49.refs_0_, f32[2,3072]{1,0:T(2,128)S(1)} %collective-permute-done.8.refs_1_, f32[2,3072]{1,0:T(2,128)S(1)} %collective-permute-done.9.refs_2_, f32[2,3072]{1,0:T(2,128)S(1)} %collective-permute-done.10.refs_3_, f32[8,256]{1,0:T(8,128)S(1)} %fusion.2.refs_4_), custom_call_target="tpu_custom_call" | custom-call | tf_op jit(solution)/shard_map/pallas_call | solution.py:184
  (8 shorter events, 0.0 us)
Async XLA Ops:
  3.5 11.2 %slice-start = ((s8[8388608]{0:T(1024)(128)(4,1)}), s8[4194304]{0:T(1024)(128)(4,1)S(1)}, s32[]{:S(2)}) async-start(s8[8388608]{0:T(1024)(128)(4,1)} %bitcast.1), calls=%async_computation | async-start | bytes 8388608
  3.5 11.2 %slice-start.2 = ((s8[8388608]{0:T(1024)(128)(4,1)}), s8[4194304]{0:T(1024)(128)(4,1)S(1)}, s32[]{:S(2)}) async-start(s8[8388608]{0:T(1024)(128)(4,1)} %bitcast.3), calls=%async_computation.2 | async-start | bytes 8388608
  3.6 11.1 %slice-start.1 = ((s8[8388608]{0:T(1024)(128)(4,1)}), s8[4194304]{0:T(1024)(128)(4,1)S(1)}, s32[]{:S(2)}) async-start(s8[8388608]{0:T(1024)(128)(4,1)} %bitcast.1), calls=%async_computation.1 | async-start | bytes 8388608
  3.6 11.1 %slice-start.3 = ((s8[8388608]{0:T(1024)(128)(4,1)}), s8[4194304]{0:T(1024)(128)(4,1)S(1)}, s32[]{:S(2)}) async-start(s8[8388608]{0:T(1024)(128)(4,1)} %bitcast.3), calls=%async_computation.3 | async-start | bytes 8388608
  3.6 6.8 %collective-permute-start.2 = (f32[2,2176]{1,0:T(2,128)S(1)}, f32[2,2176]{1,0:T(2,128)S(1)}, u32[]{:S(2)}, u32[]{:S(2)}) collective-permute-start(f32[2,2176]{1,0:T(2,128)S(1)} %get-tuple-element.9.refs_0_), channel_id=1, source_target_pairs={{0,12},{4,8},{8,4},{12,0},{1,13},{5,9},{9,5},{13,1},{2,14},{6,10},... | collective-permute-start | bytes 52232 | tf_op jit(solution)/shard_map/ppermute | solution.py:30
  8.7 4.6 %collective-permute-start.1 = (f32[2,2176]{1,0:T(2,128)S(1)}, f32[2,2176]{1,0:T(2,128)S(1)}, u32[]{:S(2)}, u32[]{:S(2)}) collective-permute-start(f32[2,2176]{1,0:T(2,128)S(1)} %get-tuple-element.9.refs_0_), channel_id=1, source_target_pairs={{0,8},{4,12},{8,0},{12,4},{1,9},{5,13},{9,1},{13,5},{2,10},{6,14},... | collective-permute-start | bytes 52232 | tf_op jit(solution)/shard_map/ppermute | solution.py:30
  8.7 4.6 %collective-permute-start = (f32[2,2176]{1,0:T(2,128)S(1)}, f32[2,2176]{1,0:T(2,128)S(1)}, u32[]{:S(2)}, u32[]{:S(2)}) collective-permute-start(f32[2,2176]{1,0:T(2,128)S(1)} %get-tuple-element.9.refs_0_), channel_id=1, source_target_pairs={{0,4},{4,0},{8,12},{12,8},{1,5},{5,1},{9,13},{13,9},{2,6},{6,2},{1... | collective-permute-start | bytes 52232 | tf_op jit(solution)/shard_map/ppermute | solution.py:30
  13.5 1.2 %collective-permute-start.3 = (f32[2,2048]{1,0:T(2,128)S(1)}, f32[2,2048]{1,0:T(2,128)S(1)}, u32[]{:S(2)}, u32[]{:S(2)}) collective-permute-start(f32[2,2048]{1,0:T(2,128)S(1)} %shard_map.47.refs_0_), channel_id=1, source_target_pairs={{0,16},{16,0},{1,17},{17,1},{2,18},{18,2},{3,19},{19,3},{4,20},{20... | collective-permute-start | bytes 49160 | tf_op jit(solution)/shard_map/ppermute | solution.py:30
  17.1 1.2 %collective-permute-start.4 = (f32[2,2048]{1,0:T(2,128)S(1)}, f32[2,2048]{1,0:T(2,128)S(1)}, u32[]{:S(2)}, u32[]{:S(2)}) collective-permute-start(f32[2,2048]{1,0:T(2,128)S(1)} %get-tuple-element.11), channel_id=1, source_target_pairs={{0,16},{16,0},{1,17},{17,1},{2,18},{18,2},{3,19},{19,3},{4,20},{20... | collective-permute-start | bytes 49160 | tf_op jit(solution)/shard_map/ppermute | solution.py:203
  18.3 5.7 %collective-permute-start.7 = (f32[2,2048]{1,0:T(2,128)S(1)}, f32[2,2048]{1,0:T(2,128)S(1)}, u32[]{:S(2)}, u32[]{:S(2)}) collective-permute-start(f32[2,2048]{1,0:T(2,128)S(1)} %add.6.refs_0_), channel_id=1, source_target_pairs={{0,12},{4,8},{8,4},{12,0},{1,13},{5,9},{9,5},{13,1},{2,14},{6,10},... | collective-permute-start | bytes 49160 | tf_op jit(solution)/shard_map/ppermute | solution.py:30
  19.8 4.7 %collective-permute-start.6 = (f32[2,2048]{1,0:T(2,128)S(1)}, f32[2,2048]{1,0:T(2,128)S(1)}, u32[]{:S(2)}, u32[]{:S(2)}) collective-permute-start(f32[2,2048]{1,0:T(2,128)S(1)} %add.6.refs_0_), channel_id=1, source_target_pairs={{0,8},{4,12},{8,0},{12,4},{1,9},{5,13},{9,1},{13,5},{2,10},{6,14},... | collective-permute-start | bytes 49160 | tf_op jit(solution)/shard_map/ppermute | solution.py:30
  20.4 4.2 %collective-permute-start.5 = (f32[2,2048]{1,0:T(2,128)S(1)}, f32[2,2048]{1,0:T(2,128)S(1)}, u32[]{:S(2)}, u32[]{:S(2)}) collective-permute-start(f32[2,2048]{1,0:T(2,128)S(1)} %add.6.refs_0_), channel_id=1, source_target_pairs={{0,4},{4,0},{8,12},{12,8},{1,5},{5,1},{9,13},{13,9},{2,6},{6,2},{1... | collective-permute-start | bytes 49160 | tf_op jit(solution)/shard_map/ppermute | solution.py:30
  24.6 4.8 %collective-permute-start.10 = (f32[2,3072]{1,0:T(2,128)S(1)}, f32[2,3072]{1,0:T(2,128)S(1)}, u32[]{:S(2)}, u32[]{:S(2)}) collective-permute-start(f32[2,3072]{1,0:T(2,128)S(1)} %shard_map.49.refs_0_), channel_id=1, source_target_pairs={{0,3},{1,2},{2,1},{3,0},{4,7},{5,6},{6,5},{7,4},{8,11},{9,10},{10,... | collective-permute-start | bytes 73736 | tf_op jit(solution)/shard_map/ppermute | solution.py:30
  27.2 3.8 %collective-permute-start.9 = (f32[2,3072]{1,0:T(2,128)S(1)}, f32[2,3072]{1,0:T(2,128)S(1)}, u32[]{:S(2)}, u32[]{:S(2)}) collective-permute-start(f32[2,3072]{1,0:T(2,128)S(1)} %shard_map.49.refs_0_), channel_id=1, source_target_pairs={{0,2},{1,3},{2,0},{3,1},{4,6},{5,7},{6,4},{7,5},{8,10},{9,11},{10,... | collective-permute-start | bytes 73736 | tf_op jit(solution)/shard_map/ppermute | solution.py:30
  27.7 3.8 %collective-permute-start.8 = (f32[2,3072]{1,0:T(2,128)S(1)}, f32[2,3072]{1,0:T(2,128)S(1)}, u32[]{:S(2)}, u32[]{:S(2)}) collective-permute-start(f32[2,3072]{1,0:T(2,128)S(1)} %shard_map.49.refs_0_), channel_id=1, source_target_pairs={{0,1},{1,0},{2,3},{3,2},{4,5},{5,4},{6,7},{7,6},{8,9},{9,8},{10,11... | collective-permute-start | bytes 73736 | tf_op jit(solution)/shard_map/ppermute | solution.py:30

commit v3 on v2

v3 whole, which is shorter than its diff:
```python
import functools

import jax
import jax.numpy as jnp
from jax import lax
from jax.experimental import pallas as pl
from jax.experimental.pallas import tpu as pltpu
from jax.sharding import PartitionSpec as P

F32, BF16 = jnp.float32, jnp.bfloat16
LANES = 128
VMEM = pl.BlockSpec(memory_space=pltpu.VMEM)


def in_hbm(x):
    return pltpu.with_memory_space_constraint(x, pltpu.HBM)


def params(mib):
    return pltpu.CompilerParams(vmem_limit_bytes=mib << 20)


def partners(n, step):
    if n & (n - 1):
        return [(i, (i + step) % n) for i in range(n)]
    return [(i, i ^ step) for i in range(n)]


def middle_first(n):
    return sorted(range(1, n), key=lambda step: (step != n // 2, step))


def exchange(x, sizes, axis, step):
    cores, seqs, groups = sizes
    to = dict(partners(seqs if axis == "seq" else groups, step))
    pairs = []
    for core in range(cores):
        for seq in range(seqs):
            for group in range(groups):
                place = (core * seqs + seq) * groups + group
                target_seq, target_group = (to[seq], group) if axis == "seq" else (seq, to[group])
                pairs.append((place, ((core ^ 1) * seqs + target_seq) * groups + target_group))
    return lax.ppermute(x, ("dp", "seq", "expert"), pairs)


def slot_sums_kernel(chunks, phi_hbm, tokens_hbm, packed_ref, phi_ref, held, sems):
    slots, width = phi_ref.shape
    rows = tokens_hbm.shape[0] // chunks
    wide = width + LANES

    def copy(c):
        part = pl.ds(c * rows, rows)
        return pltpu.make_async_copy(tokens_hbm.at[part], held.at[part], sems.at[c])

    phi_copy = pltpu.make_async_copy(phi_hbm, phi_ref, sems.at[chunks])
    phi_copy.start()
    for c in range(chunks):
        copy(c).start()
    phi_copy.wait()
    spare = jnp.zeros((8 - slots % 8, width), F32)
    phi = jnp.concatenate([phi_ref[...].astype(F32), spare], axis=0).T.astype(BF16)
    tops, sums, totals = [], [], []

    def finish(c, by_token):
        part = pl.ds(c * rows, rows)
        logits = by_token.T[:slots]
        packed_ref[:, pl.ds(wide + c * rows, rows)] = logits
        top = jnp.max(logits, axis=1, keepdims=True)
        spread = jnp.exp(logits - top)
        tops.append(top)
        totals.append(jnp.sum(spread, axis=1, keepdims=True))
        sums.append(jnp.dot(spread.astype(BF16), held[part, :], preferred_element_type=F32))

    before = None
    for c in range(chunks):
        copy(c).wait()
        now = jnp.dot(held[pl.ds(c * rows, rows), :], phi, preferred_element_type=F32)
        if c:
            finish(c - 1, before)
        before = now
    finish(chunks - 1, before)
    top = functools.reduce(jnp.maximum, tops)
    scales = [jnp.exp(t - top) for t in tops]
    packed_ref[:, :width] = sum(s * v for s, v in zip(scales, sums))
    total = sum(s * v for s, v in zip(scales, totals))
    lane = lax.broadcasted_iota(jnp.int32, (slots, LANES), 1)
    packed_ref[:, width:wide] = jnp.where(lane == 0, top, total)


def slot_sums(phi, tokens, chunks=4):
    (slots, width), count = phi.shape, tokens.shape[0]
    return pl.pallas_call(
        functools.partial(slot_sums_kernel, chunks),
        out_shape=jax.ShapeDtypeStruct((slots, width + LANES + count), F32),
        in_specs=[pl.BlockSpec(memory_space=pltpu.HBM)] * 2,
        out_specs=VMEM,
        scratch_shapes=[
            pltpu.VMEM(phi.shape, BF16),
            pltpu.VMEM(tokens.shape, BF16),
            pltpu.SemaphoreType.DMA((chunks + 1,)),
        ],
        compiler_params=params(16),
    )(in_hbm(phi), in_hbm(tokens))


def joined(parts, width):
    tops = [p[:, width : width + 1] for p in parts]
    top = functools.reduce(jnp.maximum, tops)
    scales = [jnp.exp(t - top) for t in tops]
    total = sum(s * p[:, width + 1 : width + 2] for s, p in zip(scales, parts))
    return sum(s * p[:, :width] for s, p in zip(scales, parts)), top, total


def swapped(x):
    half = x.shape[0] // 2
    return jnp.concatenate([x[half:], x[:half]], axis=0)


def join_kernel(own_ref, *refs):
    *received, out_ref = refs
    parts = [swapped(r[...]) for r in received]
    value, _, total = joined([own_ref[...]] + parts, out_ref.shape[1])
    out_ref[...] = value / total


def join(own, received):
    slots, wide = own.shape
    return pl.pallas_call(
        join_kernel,
        out_shape=jax.ShapeDtypeStruct((slots, wide - LANES), F32),
        in_specs=[VMEM] * (len(received) + 1),
        out_specs=VMEM,
        cost_estimate=pl.CostEstimate(flops=10_000_000_000, bytes_accessed=0, transcendentals=0),
        compiler_params=params(4),
    )(own, *received)


def gelu(v):
    return 0.5 * v * (1.0 + jnp.tanh(0.7978845608028654 * (v + 0.044715 * v * v * v)))


def experts_kernel(x_ref, first_ref, second_ref, out_ref):
    slots = first_ref.shape[0]
    for e in range(slots):
        x = jnp.concatenate([x_ref[e : e + 1, :], x_ref[slots + e : slots + e + 1, :]], axis=0)
        hidden = jnp.dot(x.astype(BF16), first_ref[e], preferred_element_type=F32)
        value = jnp.dot(gelu(hidden).astype(BF16), second_ref[e], preferred_element_type=F32)
        out_ref[e : e + 1, :] = value[:1]
        out_ref[slots + e : slots + e + 1, :] = value[1:]


def experts(slot_in, w_in, w_out):
    return pl.pallas_call(
        experts_kernel,
        out_shape=jax.ShapeDtypeStruct(slot_in.shape, F32),
        in_specs=[VMEM] * 3,
        out_specs=VMEM,
        compiler_params=params(4),
    )(slot_in, w_in, w_out)


def pack_kernel(chip_ref, *refs):
    *received, logits_ref, own_ref, other_ref = refs
    slots, width = own_ref.shape[0], chip_ref.shape[1]
    total = chip_ref[...]
    for r in received:
        total += swapped(r[...])
    total = total.astype(BF16).astype(F32)
    for out_ref, part in ((own_ref, slice(0, slots)), (other_ref, slice(slots, 2 * slots))):
        out_ref[:, :width] = total[part]
        out_ref[:, width:] = logits_ref[part, :]


def pack(chip, received, logits):
    slots, width = chip.shape
    shape = jax.ShapeDtypeStruct((slots // 2, width + logits.shape[1]), F32)
    return pl.pallas_call(
        pack_kernel,
        out_shape=(shape, shape),
        in_specs=[VMEM] * (len(received) + 2),
        out_specs=(VMEM, VMEM),
        compiler_params=params(4),
    )(chip, *received, logits)


def mix_kernel(chunks, *refs):
    *packed, out_hbm, rows_ref, sems = refs
    (count, width), group = rows_ref.shape, lax.axis_index("expert")
    rows = count // chunks
    values = jnp.concatenate([p[:, :width] for p in packed], axis=0).astype(BF16)
    everything = jnp.concatenate([p[:, width:] for p in packed], axis=0)
    logits = everything[:, :count]
    for g in range(1, len(packed)):
        logits = jnp.where(group == g, everything[:, g * count : (g + 1) * count], logits)
    weight = jnp.exp(logits - jnp.max(logits, axis=0, keepdims=True))
    weight = (weight / jnp.sum(weight, axis=0, keepdims=True)).astype(BF16)
    copies = []
    for c in range(chunks):
        part = pl.ds(c * rows, rows)
        rows_ref[part, :] = lax.dot_general(
            weight[:, c * rows : (c + 1) * rows],
            values,
            (((0,), (0,)), ((), ())),
            preferred_element_type=F32,
        ).astype(BF16)
        copies.append(pltpu.make_async_copy(rows_ref.at[part], out_hbm.at[part], sems.at[c]))
        copies[-1].start()
    for copy in copies:
        copy.wait()


def mix(packed, width, chunks=4):
    shape = ((packed[0].shape[1] - width) // len(packed), width)
    return pl.pallas_call(
        functools.partial(mix_kernel, chunks),
        out_shape=jax.ShapeDtypeStruct(shape, BF16),
        in_specs=[VMEM] * len(packed),
        out_specs=pl.BlockSpec(memory_space=pl.ANY),
        scratch_shapes=[pltpu.VMEM(shape, BF16), pltpu.SemaphoreType.DMA((chunks,))],
        compiler_params=params(8),
    )(*packed)


def on_device(sizes, tokens, phi, w_in, w_out):
    cores, seqs, groups = sizes
    width = tokens.shape[1]
    swap = partners(cores, 1)
    packed = slot_sums(phi.T, tokens)
    both = jnp.concatenate([packed, lax.ppermute(packed, "dp", swap)], axis=0)
    both, logits = both[:, : width + LANES], both[:, width + LANES :]
    slot_in = join(both, [exchange(both, sizes, "seq", step) for step in range(1, seqs)])
    partial = experts(slot_in, w_in, w_out)
    chip = partial + swapped(lax.ppermute(partial, "dp", swap))
    sums = [exchange(chip, sizes, "seq", step) for step in middle_first(seqs)]
    own, other = pack(chip, sums, logits)
    everyone = [own] + [exchange(other, sizes, "expert", step) for step in range(1, groups)]
    return mix(everyone, width)


def solution(mesh):
    sizes = tuple(mesh.shape[axis] for axis in ("dp", "seq", "expert"))
    placed = (
        P(("dp", "seq"), None),
        P(None, "expert"),
        P("expert", None, ("dp", "seq")),
        P("expert", ("dp", "seq"), None),
    )
    return jax.shard_map(
        functools.partial(on_device, sizes),
        mesh=mesh,
        in_specs=placed,
        out_specs=P(("dp", "seq", "expert"), None),
        check_vma=False,
    )
```

time: 33.1 us -> 32 us (0.967)
  waiting for transfers between devices: 11.4 us -> 10.8 us
  starting transfers between devices: 13.9 us -> 13.4 us
    ppermute x11, waiting for transfers between devices: 11.4 us -> 10.8 us  [the longest x9 9.06 us: exchange(): return lax.ppermute(x, ('dp', 'seq', 'expert'), pairs)]
    ppermute x11, starting transfers between devices: 13.9 us -> 13.4 us  [the longest x9 12.5 us: exchange(): return lax.ppermute(x, ('dp', 'seq', 'expert'), pairs)]
where the time goes in v3:
time: 32 us; the launch traced here: 31.7 us
  starting transfers between devices  13.4 us (42%)
  waiting for transfers between devices  10.8 us (34%)
  Pallas kernels  7.36 us (23%)
    ppermute x9, starting transfers between devices, exchange(): return lax.ppermute(x, ('dp', 'seq', 'expert'), pairs)  12.5 us
    ppermute x9, waiting for transfers between devices, exchange(): return lax.ppermute(x, ('dp', 'seq', 'expert'), pairs)  9.06 us
    pallas_call x1, Pallas kernels, slot_sums(): pl.pallas_call(functools.partial(slot_sums_kernel, chunks), out_shape=jax...  3.52 us
    pallas_call x1, Pallas kernels, experts(): pl.pallas_call(experts_kernel, out_shape=jax.ShapeDtypeStruct(slot_in.sha...  2.34 us
    pallas_call x1, Pallas kernels, mix(): pl.pallas_call(functools.partial(mix_kernel, chunks), out_shape=jax.Shape...  1.28 us
    ppermute x1, waiting for transfers between devices, on_device(): chip = partial + swapped(lax.ppermute(partial, 'dp', swap))  0.86 us
    ppermute x1, waiting for transfers between devices, on_device(): both = jnp.concatenate([packed, lax.ppermute(packed, 'dp', swap)], axis=0)  0.85 us
  transfers between devices with their start and end apart: 11, of which 10 were waited for; matrix products, arithmetic and copies ran while one was open for 0% of the time, Pallas kernels for 0%

profile of v3, /device:TPU:0, one launch (start us, length us, event | category | flops | bytes accessed | tf_op | source)
XLA Modules:
  0.0 31.7 jit_solution(4579117780290809768)
XLA Ops:
  0.0 3.5 %shard_map.46 = f32[2,3200]{1,0:T(2,128)S(1)} custom-call(bf16[2,2048]{1,0:T(2,128)(2,1)} %bitcast.5, bf16[1024,2048]{1,0:T(8,128)(2,1)} %tokens_hbm.1), custom_call_target="tpu_custom_call" | custom-call | tf_op jit(solution)/shard_map/pallas_call | solution.py:92
  3.5 0.5 %collective-permute-start = (f32[2,3200]{1,0:T(2,128)S(1)}, f32[2,3200]{1,0:T(2,128)S(1)}, u32[]{:S(2)}, u32[]{:S(2)}) collective-permute-start(f32[2,3200]{1,0:T(2,128)S(1)} %shard_map.46), channel_id=1, source_target_pairs={{0,16},{16,0},{1,17},{17,1},{2,18},{18,2},{3,19},{19,3},{4,20},{20... | collective-permute-start | bytes 76808 | tf_op jit(solution)/shard_map/ppermute | solution.py:229
  4.0 0.9 %collective-permute-done = f32[2,3200]{1,0:T(2,128)S(1)} collective-permute-done((f32[2,3200]{1,0:T(2,128)S(1)}, f32[2,3200]{1,0:T(2,128)S(1)}, u32[]{:S(2)}, u32[]{:S(2)}) %collective-permute-start) | collective-permute-done | bytes 25632 | tf_op jit(solution)/shard_map/ppermute | solution.py:229
  4.9 0.0 slice-start
  4.9 0.0 slice-start.2
  4.9 0.0 slice-start.1
  4.9 0.0 slice-start.3
  5.0 4.8 %collective-permute-start.3 = (f32[4,2176]{1,0:T(4,128)S(1)}, f32[4,2176]{1,0:T(4,128)S(1)}, u32[]{:S(2)}, u32[]{:S(2)}) collective-permute-start(f32[4,2176]{1,0:T(4,128)S(1)} %fusion.own_ref), channel_id=1, source_target_pairs={{0,28},{1,29},{2,30},{3,31},{4,24},{5,25},{6,26},{7,27},{8,20},{9,... | collective-permute-start | bytes 104456 | tf_op jit(solution)/shard_map/ppermute | solution.py:43
  9.7 0.0 collective-permute-start.2
  9.7 0.6 %collective-permute-start.1 = (f32[4,2176]{1,0:T(4,128)S(1)}, f32[4,2176]{1,0:T(4,128)S(1)}, u32[]{:S(2)}, u32[]{:S(2)}) collective-permute-start(f32[4,2176]{1,0:T(4,128)S(1)} %fusion.own_ref), channel_id=1, source_target_pairs={{0,20},{1,21},{2,22},{3,23},{4,16},{5,17},{6,18},{7,19},{8,28},{9,... | collective-permute-start | bytes 104456 | tf_op jit(solution)/shard_map/ppermute | solution.py:43
  10.3 1.2 %collective-permute-done.3.refs_2_ = f32[4,2176]{1,0:T(4,128)S(1)} collective-permute-done((f32[4,2176]{1,0:T(4,128)S(1)}, f32[4,2176]{1,0:T(4,128)S(1)}, u32[]{:S(2)}, u32[]{:S(2)}) %collective-permute-start.3) | collective-permute-done | bytes 34848 | tf_op jit(solution)/shard_map/ppermute | solution.py:43
  11.6 2.4 %collective-permute-done.2.refs_1_ = f32[4,2176]{1,0:T(4,128)S(1)} collective-permute-done((f32[4,2176]{1,0:T(4,128)S(1)}, f32[4,2176]{1,0:T(4,128)S(1)}, u32[]{:S(2)}, u32[]{:S(2)}) %collective-permute-start.2) | collective-permute-done | bytes 34848 | tf_op jit(solution)/shard_map/ppermute | solution.py:43
  14.0 0.0 collective-permute-done.1.refs_0_
  14.0 0.2 shard_map.47.x_ref
  14.2 0.0 slice-done
  14.2 0.0 slice-done.2
  14.2 0.0 slice-done.1
  14.2 0.0 slice-done.3
  14.2 2.3 %shard_map.48 = f32[4,2048]{1,0:T(4,128)S(1)} custom-call(f32[4,2048]{1,0:T(4,128)S(1)} %shard_map.47.x_ref, bf16[2,2048,1024]{2,1,0:T(8,128)(2,1)S(1)} %bitcast.2, bf16[2,1024,2048]{2,1,0:T(8,128)(2,1)S(1)} %bitcast.4), custom_call_target="tpu_custom_call" | custom-call | tf_op jit(solution)/shard_map/pallas_call | solution.py:153
  16.6 0.4 %collective-permute-start.4 = (f32[4,2048]{1,0:T(4,128)S(1)}, f32[4,2048]{1,0:T(4,128)S(1)}, u32[]{:S(2)}, u32[]{:S(2)}) collective-permute-start(f32[4,2048]{1,0:T(4,128)S(1)} %shard_map.48), channel_id=1, source_target_pairs={{0,16},{16,0},{1,17},{17,1},{2,18},{18,2},{3,19},{19,3},{4,20},{20... | collective-permute-start | bytes 98312 | tf_op jit(solution)/shard_map/ppermute | solution.py:233
  16.9 0.9 %collective-permute-done.4 = f32[4,2048]{1,0:T(4,128)S(1)} collective-permute-done((f32[4,2048]{1,0:T(4,128)S(1)}, f32[4,2048]{1,0:T(4,128)S(1)}, u32[]{:S(2)}, u32[]{:S(2)}) %collective-permute-start.4) | collective-permute-done | bytes 32800 | tf_op jit(solution)/shard_map/ppermute | solution.py:233
  17.8 1.8 %collective-permute-start.7 = (f32[4,2048]{1,0:T(4,128)S(1)}, f32[4,2048]{1,0:T(4,128)S(1)}, u32[]{:S(2)}, u32[]{:S(2)}) collective-permute-start(f32[4,2048]{1,0:T(4,128)S(1)} %maximum_add_fusion.chip_ref), channel_id=1, source_target_pairs={{0,28},{1,29},{2,30},{3,31},{4,24},{5,25},{6,26},{7,27},{8,20},{9,... | collective-permute-start | bytes 98312 | tf_op jit(solution)/shard_map/ppermute | solution.py:43
  19.7 0.5 %collective-permute-start.6 = (f32[4,2048]{1,0:T(4,128)S(1)}, f32[4,2048]{1,0:T(4,128)S(1)}, u32[]{:S(2)}, u32[]{:S(2)}) collective-permute-start(f32[4,2048]{1,0:T(4,128)S(1)} %maximum_add_fusion.chip_ref), channel_id=1, source_target_pairs={{0,20},{1,21},{2,22},{3,23},{4,16},{5,17},{6,18},{7,19},{8,28},{9,... | collective-permute-start | bytes 98312 | tf_op jit(solution)/shard_map/ppermute | solution.py:43
  20.2 1.8 %collective-permute-start.5 = (f32[4,2048]{1,0:T(4,128)S(1)}, f32[4,2048]{1,0:T(4,128)S(1)}, u32[]{:S(2)}, u32[]{:S(2)}) collective-permute-start(f32[4,2048]{1,0:T(4,128)S(1)} %maximum_add_fusion.chip_ref), channel_id=1, source_target_pairs={{0,24},{1,25},{2,26},{3,27},{4,28},{5,29},{6,30},{7,31},{8,16},{9,... | collective-permute-start | bytes 98312 | tf_op jit(solution)/shard_map/ppermute | solution.py:43
  22.0 1.2 %collective-permute-done.7.refs_2_ = f32[4,2048]{1,0:T(4,128)S(1)} collective-permute-done((f32[4,2048]{1,0:T(4,128)S(1)}, f32[4,2048]{1,0:T(4,128)S(1)}, u32[]{:S(2)}, u32[]{:S(2)}) %collective-permute-start.7) | collective-permute-done | bytes 32800 | tf_op jit(solution)/shard_map/ppermute | solution.py:43
  23.1 0.7 %collective-permute-done.6.refs_1_ = f32[4,2048]{1,0:T(4,128)S(1)} collective-permute-done((f32[4,2048]{1,0:T(4,128)S(1)}, f32[4,2048]{1,0:T(4,128)S(1)}, u32[]{:S(2)}, u32[]{:S(2)}) %collective-permute-start.6) | collective-permute-done | bytes 32800 | tf_op jit(solution)/shard_map/ppermute | solution.py:43
  23.9 0.5 %collective-permute-done.5.refs_0_ = f32[4,2048]{1,0:T(4,128)S(1)} collective-permute-done((f32[4,2048]{1,0:T(4,128)S(1)}, f32[4,2048]{1,0:T(4,128)S(1)}, u32[]{:S(2)}, u32[]{:S(2)}) %collective-permute-start.5) | collective-permute-done | bytes 32800 | tf_op jit(solution)/shard_map/ppermute | solution.py:43
  24.5 2.3 %collective-permute-start.10 = (f32[2,3072]{1,0:T(2,128)S(1)}, f32[2,3072]{1,0:T(2,128)S(1)}, u32[]{:S(2)}, u32[]{:S(2)}) collective-permute-start(f32[2,3072]{1,0:T(2,128)S(1)} %get-tuple-element.8), channel_id=1, source_target_pairs={{0,19},{1,18},{2,17},{3,16},{4,23},{5,22},{6,21},{7,20},{8,27},{9,... | collective-permute-start | bytes 73736 | tf_op jit(solution)/shard_map/ppermute | solution.py:43
  26.8 0.4 %collective-permute-start.9 = (f32[2,3072]{1,0:T(2,128)S(1)}, f32[2,3072]{1,0:T(2,128)S(1)}, u32[]{:S(2)}, u32[]{:S(2)}) collective-permute-start(f32[2,3072]{1,0:T(2,128)S(1)} %get-tuple-element.8), channel_id=1, source_target_pairs={{0,18},{1,19},{2,16},{3,17},{4,22},{5,23},{6,20},{7,21},{8,26},{9,... | collective-permute-start | bytes 73736 | tf_op jit(solution)/shard_map/ppermute | solution.py:43
  27.2 0.3 collective-permute-start.8
  27.5 1.2 %collective-permute-done.10.refs_3_ = f32[2,3072]{1,0:T(2,128)S(1)} collective-permute-done((f32[2,3072]{1,0:T(2,128)S(1)}, f32[2,3072]{1,0:T(2,128)S(1)}, u32[]{:S(2)}, u32[]{:S(2)}) %collective-permute-start.10) | collective-permute-done | bytes 24608 | tf_op jit(solution)/shard_map/ppermute | solution.py:43
  28.7 1.3 %collective-permute-done.9.refs_2_ = f32[2,3072]{1,0:T(2,128)S(1)} collective-permute-done((f32[2,3072]{1,0:T(2,128)S(1)}, f32[2,3072]{1,0:T(2,128)S(1)}, u32[]{:S(2)}, u32[]{:S(2)}) %collective-permute-start.9) | collective-permute-done | bytes 24608 | tf_op jit(solution)/shard_map/ppermute | solution.py:43
  30.0 0.4 %collective-permute-done.8.refs_1_ = f32[2,3072]{1,0:T(2,128)S(1)} collective-permute-done((f32[2,3072]{1,0:T(2,128)S(1)}, f32[2,3072]{1,0:T(2,128)S(1)}, u32[]{:S(2)}, u32[]{:S(2)}) %collective-permute-start.8) | collective-permute-done | bytes 24608 | tf_op jit(solution)/shard_map/ppermute | solution.py:43
  30.5 1.3 %shard_map.50 = bf16[256,2048]{1,0:T(8,128)(2,1)} custom-call(f32[2,3072]{1,0:T(2,128)S(1)} %get-tuple-element.7.refs_0_, f32[2,3072]{1,0:T(2,128)S(1)} %collective-permute-done.8.refs_1_, f32[2,3072]{1,0:T(2,128)S(1)} %collective-permute-done.9.refs_2_, f32[2,3072]{1,0:T(2,128)S(1)} %collective-permute-done.10.refs_3_), custom_call_target="tpu_custom_call" | custom-call | tf_op jit(solution)/shard_map/pallas_call | solution.py:214
  (7 shorter events, 0.1 us)
Async XLA Ops:
  3.5 1.4 %collective-permute-start = (f32[2,3200]{1,0:T(2,128)S(1)}, f32[2,3200]{1,0:T(2,128)S(1)}, u32[]{:S(2)}, u32[]{:S(2)}) collective-permute-start(f32[2,3200]{1,0:T(2,128)S(1)} %shard_map.46), channel_id=1, source_target_pairs={{0,16},{16,0},{1,17},{17,1},{2,18},{18,2},{3,19},{19,3},{4,20},{20... | collective-permute-start | bytes 76808 | tf_op jit(solution)/shard_map/ppermute | solution.py:229
  4.9 9.3 %slice-start = ((s8[8388608]{0:T(1024)(128)(4,1)}), s8[4194304]{0:T(1024)(128)(4,1)S(1)}, s32[]{:S(2)}) async-start(s8[8388608]{0:T(1024)(128)(4,1)} %bitcast.1), calls=%async_computation | async-start | bytes 8388608
  4.9 9.3 %slice-start.2 = ((s8[8388608]{0:T(1024)(128)(4,1)}), s8[4194304]{0:T(1024)(128)(4,1)S(1)}, s32[]{:S(2)}) async-start(s8[8388608]{0:T(1024)(128)(4,1)} %bitcast.3), calls=%async_computation.2 | async-start | bytes 8388608
  4.9 9.3 %slice-start.1 = ((s8[8388608]{0:T(1024)(128)(4,1)}), s8[4194304]{0:T(1024)(128)(4,1)S(1)}, s32[]{:S(2)}) async-start(s8[8388608]{0:T(1024)(128)(4,1)} %bitcast.1), calls=%async_computation.1 | async-start | bytes 8388608
  4.9 9.3 %slice-start.3 = ((s8[8388608]{0:T(1024)(128)(4,1)}), s8[4194304]{0:T(1024)(128)(4,1)S(1)}, s32[]{:S(2)}) async-start(s8[8388608]{0:T(1024)(128)(4,1)} %bitcast.3), calls=%async_computation.3 | async-start | bytes 8388608
  5.0 6.6 %collective-permute-start.3 = (f32[4,2176]{1,0:T(4,128)S(1)}, f32[4,2176]{1,0:T(4,128)S(1)}, u32[]{:S(2)}, u32[]{:S(2)}) collective-permute-start(f32[4,2176]{1,0:T(4,128)S(1)} %fusion.own_ref), channel_id=1, source_target_pairs={{0,28},{1,29},{2,30},{3,31},{4,24},{5,25},{6,26},{7,27},{8,20},{9,... | collective-permute-start | bytes 104456 | tf_op jit(solution)/shard_map/ppermute | solution.py:43
  9.7 4.3 %collective-permute-start.2 = (f32[4,2176]{1,0:T(4,128)S(1)}, f32[4,2176]{1,0:T(4,128)S(1)}, u32[]{:S(2)}, u32[]{:S(2)}) collective-permute-start(f32[4,2176]{1,0:T(4,128)S(1)} %fusion.own_ref), channel_id=1, source_target_pairs={{0,24},{1,25},{2,26},{3,27},{4,28},{5,29},{6,30},{7,31},{8,16},{9,... | collective-permute-start | bytes 104456 | tf_op jit(solution)/shard_map/ppermute | solution.py:43
  9.7 4.3 %collective-permute-start.1 = (f32[4,2176]{1,0:T(4,128)S(1)}, f32[4,2176]{1,0:T(4,128)S(1)}, u32[]{:S(2)}, u32[]{:S(2)}) collective-permute-start(f32[4,2176]{1,0:T(4,128)S(1)} %fusion.own_ref), channel_id=1, source_target_pairs={{0,20},{1,21},{2,22},{3,23},{4,16},{5,17},{6,18},{7,19},{8,28},{9,... | collective-permute-start | bytes 104456 | tf_op jit(solution)/shard_map/ppermute | solution.py:43
  16.6 1.2 %collective-permute-start.4 = (f32[4,2048]{1,0:T(4,128)S(1)}, f32[4,2048]{1,0:T(4,128)S(1)}, u32[]{:S(2)}, u32[]{:S(2)}) collective-permute-start(f32[4,2048]{1,0:T(4,128)S(1)} %shard_map.48), channel_id=1, source_target_pairs={{0,16},{16,0},{1,17},{17,1},{2,18},{18,2},{3,19},{19,3},{4,20},{20... | collective-permute-start | bytes 98312 | tf_op jit(solution)/shard_map/ppermute | solution.py:233
  17.8 5.3 %collective-permute-start.7 = (f32[4,2048]{1,0:T(4,128)S(1)}, f32[4,2048]{1,0:T(4,128)S(1)}, u32[]{:S(2)}, u32[]{:S(2)}) collective-permute-start(f32[4,2048]{1,0:T(4,128)S(1)} %maximum_add_fusion.chip_ref), channel_id=1, source_target_pairs={{0,28},{1,29},{2,30},{3,31},{4,24},{5,25},{6,26},{7,27},{8,20},{9,... | collective-permute-start | bytes 98312 | tf_op jit(solution)/shard_map/ppermute | solution.py:43
  19.7 4.2 %collective-permute-start.6 = (f32[4,2048]{1,0:T(4,128)S(1)}, f32[4,2048]{1,0:T(4,128)S(1)}, u32[]{:S(2)}, u32[]{:S(2)}) collective-permute-start(f32[4,2048]{1,0:T(4,128)S(1)} %maximum_add_fusion.chip_ref), channel_id=1, source_target_pairs={{0,20},{1,21},{2,22},{3,23},{4,16},{5,17},{6,18},{7,19},{8,28},{9,... | collective-permute-start | bytes 98312 | tf_op jit(solution)/shard_map/ppermute | solution.py:43
  20.2 4.2 %collective-permute-start.5 = (f32[4,2048]{1,0:T(4,128)S(1)}, f32[4,2048]{1,0:T(4,128)S(1)}, u32[]{:S(2)}, u32[]{:S(2)}) collective-permute-start(f32[4,2048]{1,0:T(4,128)S(1)} %maximum_add_fusion.chip_ref), channel_id=1, source_target_pairs={{0,24},{1,25},{2,26},{3,27},{4,28},{5,29},{6,30},{7,31},{8,16},{9,... | collective-permute-start | bytes 98312 | tf_op jit(solution)/shard_map/ppermute | solution.py:43
  24.5 4.2 %collective-permute-start.10 = (f32[2,3072]{1,0:T(2,128)S(1)}, f32[2,3072]{1,0:T(2,128)S(1)}, u32[]{:S(2)}, u32[]{:S(2)}) collective-permute-start(f32[2,3072]{1,0:T(2,128)S(1)} %get-tuple-element.8), channel_id=1, source_target_pairs={{0,19},{1,18},{2,17},{3,16},{4,23},{5,22},{6,21},{7,20},{8,27},{9,... | collective-permute-start | bytes 73736 | tf_op jit(solution)/shard_map/ppermute | solution.py:43
  26.8 3.3 %collective-permute-start.9 = (f32[2,3072]{1,0:T(2,128)S(1)}, f32[2,3072]{1,0:T(2,128)S(1)}, u32[]{:S(2)}, u32[]{:S(2)}) collective-permute-start(f32[2,3072]{1,0:T(2,128)S(1)} %get-tuple-element.8), channel_id=1, source_target_pairs={{0,18},{1,19},{2,16},{3,17},{4,22},{5,23},{6,20},{7,21},{8,26},{9,... | collective-permute-start | bytes 73736 | tf_op jit(solution)/shard_map/ppermute | solution.py:43
  27.2 3.3 %collective-permute-start.8 = (f32[2,3072]{1,0:T(2,128)S(1)}, f32[2,3072]{1,0:T(2,128)S(1)}, u32[]{:S(2)}, u32[]{:S(2)}) collective-permute-start(f32[2,3072]{1,0:T(2,128)S(1)} %get-tuple-element.8), channel_id=1, source_target_pairs={{0,17},{1,16},{2,19},{3,18},{4,21},{5,20},{6,23},{7,22},{8,25},{9,... | collective-permute-start | bytes 73736 | tf_op jit(solution)/shard_map/ppermute | solution.py:43

commit v4 on v3

--- a/solution.py
+++ b/solution.py
@@ -41,6 +41,28 @@
                 target_seq, target_group = (to[seq], group) if axis == "seq" else (seq, to[group])
                 pairs.append((place, ((core ^ 1) * seqs + target_seq) * groups + target_group))
     return lax.ppermute(x, ("dp", "seq", "expert"), pairs)
+
+
+def scalars(top, total):
+    lane = lax.broadcasted_iota(jnp.int32, (top.shape[0], LANES), 1)
+    lanes = jnp.zeros(lane.shape, F32)
+    for at, rest in ((0, top), (3, total)):
+        for i in range(3):
+            piece = rest.astype(BF16).astype(F32)
+            lanes = jnp.where(lane == at + i, piece, lanes)
+            rest = rest - piece
+    return lanes
+
+
+def joined(parts, width):
+    def scalar(part, at):
+        return sum(part[:, width + at + i : width + at + i + 1] for i in range(3))
+
+    tops = [scalar(p, 0) for p in parts]
+    top = functools.reduce(jnp.maximum, tops)
+    scales = [jnp.exp(t - top) for t in tops]
+    total = sum(s * scalar(p, 3) for s, p in zip(scales, parts))
+    return sum(s * p[:, :width] for s, p in zip(scales, parts)) / total
 
 
 def slot_sums_kernel(chunks, phi_hbm, tokens_hbm, packed_ref, phi_ref, held, sems):
@@ -83,8 +105,7 @@
     scales = [jnp.exp(t - top) for t in tops]
     packed_ref[:, :width] = sum(s * v for s, v in zip(scales, sums))
     total = sum(s * v for s, v in zip(scales, totals))
-    lane = lax.broadcasted_iota(jnp.int32, (slots, LANES), 1)
-    packed_ref[:, width:wide] = jnp.where(lane == 0, top, total)
+    packed_ref[:, width:wide] = scalars(top, total)
 
 
 def slot_sums(phi, tokens, chunks=4):
@@ -103,60 +124,60 @@
     )(in_hbm(phi), in_hbm(tokens))
 
 
-def joined(parts, width):
-    tops = [p[:, width : width + 1] for p in parts]
-    top = functools.reduce(jnp.maximum, tops)
-    scales = [jnp.exp(t - top) for t in tops]
-    total = sum(s * p[:, width + 1 : width + 2] for s, p in zip(scales, parts))
-    return sum(s * p[:, :width] for s, p in zip(scales, parts)), top, total
-
-
 def swapped(x):
     half = x.shape[0] // 2
     return jnp.concatenate([x[half:], x[:half]], axis=0)
 
 
-def join_kernel(own_ref, *refs):
-    *received, out_ref = refs
-    parts = [swapped(r[...]) for r in received]
-    value, _, total = joined([own_ref[...]] + parts, out_ref.shape[1])
-    out_ref[...] = value / total
-
-
-def join(own, received):
-    slots, wide = own.shape
-    return pl.pallas_call(
-        join_kernel,
-        out_shape=jax.ShapeDtypeStruct((slots, wide - LANES), F32),
-        in_specs=[VMEM] * (len(received) + 1),
-        out_specs=VMEM,
+def pair_kernel(own_ref, other_ref, sent_ref, both_ref, logits_ref):
+    slots, wide = own_ref.shape[0], both_ref.shape[1]
+    for i, ref in enumerate((own_ref, other_ref)):
+        part = slice(i * slots, (i + 1) * slots)
+        both_ref[part, :] = ref[:, :wide]
+        logits_ref[part, :] = ref[:, wide:]
+    sent_ref[...] = both_ref[...].astype(BF16)
+
+
+def pair(own, other, wide):
+    slots = 2 * own.shape[0]
+    return pl.pallas_call(
+        pair_kernel,
+        out_shape=(
+            jax.ShapeDtypeStruct((slots, wide), BF16),
+            jax.ShapeDtypeStruct((slots, wide), F32),
+            jax.ShapeDtypeStruct((slots, own.shape[1] - wide), F32),
+        ),
+        in_specs=[VMEM] * 2,
+        out_specs=(VMEM,) * 3,
         cost_estimate=pl.CostEstimate(flops=10_000_000_000, bytes_accessed=0, transcendentals=0),
         compiler_params=params(4),
-    )(own, *received)
+    )(own, other)
 
 
 def gelu(v):
     return 0.5 * v * (1.0 + jnp.tanh(0.7978845608028654 * (v + 0.044715 * v * v * v)))
 
 
-def experts_kernel(x_ref, first_ref, second_ref, out_ref):
-    slots = first_ref.shape[0]
+def experts_kernel(both_ref, *refs):
+    *received, first_ref, second_ref, out_ref = refs
+    slots, width = first_ref.shape[:2]
+    slot_in = joined([both_ref[...]] + [swapped(r[...].astype(F32)) for r in received], width)
     for e in range(slots):
-        x = jnp.concatenate([x_ref[e : e + 1, :], x_ref[slots + e : slots + e + 1, :]], axis=0)
+        x = jnp.concatenate([slot_in[e : e + 1], slot_in[slots + e : slots + e + 1]], axis=0)
         hidden = jnp.dot(x.astype(BF16), first_ref[e], preferred_element_type=F32)
         value = jnp.dot(gelu(hidden).astype(BF16), second_ref[e], preferred_element_type=F32)
         out_ref[e : e + 1, :] = value[:1]
         out_ref[slots + e : slots + e + 1, :] = value[1:]
 
 
-def experts(slot_in, w_in, w_out):
+def experts(both, received, w_in, w_out):
     return pl.pallas_call(
         experts_kernel,
-        out_shape=jax.ShapeDtypeStruct(slot_in.shape, F32),
-        in_specs=[VMEM] * 3,
+        out_shape=jax.ShapeDtypeStruct((both.shape[0], w_in.shape[1]), F32),
+        in_specs=[VMEM] * (len(received) + 3),
         out_specs=VMEM,
         compiler_params=params(4),
-    )(slot_in, w_in, w_out)
+    )(both, *received, w_in, w_out)
 
 
 def pack_kernel(chip_ref, *refs):
@@ -164,7 +185,7 @@
     slots, width = own_ref.shape[0], chip_ref.shape[1]
     total = chip_ref[...]
     for r in received:
-        total += swapped(r[...])
+        total += swapped(r[...].astype(F32))
     total = total.astype(BF16).astype(F32)
     for out_ref, part in ((own_ref, slice(0, slots)), (other_ref, slice(slots, 2 * slots))):
         out_ref[:, :width] = total[part]
@@ -226,12 +247,12 @@
     width = tokens.shape[1]
     swap = partners(cores, 1)
     packed = slot_sums(phi.T, tokens)
-    both = jnp.concatenate([packed, lax.ppermute(packed, "dp", swap)], axis=0)
-    both, logits = both[:, : width + LANES], both[:, width + LANES :]
-    slot_in = join(both, [exchange(both, sizes, "seq", step) for step in range(1, seqs)])
-    partial = experts(slot_in, w_in, w_out)
+    sent, both, logits = pair(packed, lax.ppermute(packed, "dp", swap), width + LANES)
+    received = [exchange(sent, sizes, "seq", step) for step in middle_first(seqs)]
+    partial = experts(both, received, w_in, w_out)
     chip = partial + swapped(lax.ppermute(partial, "dp", swap))
-    sums = [exchange(chip, sizes, "seq", step) for step in middle_first(seqs)]
+    sent = chip.astype(BF16)
+    sums = [exchange(sent, sizes, "seq", step) for step in middle_first(seqs)]
     own, other = pack(chip, sums, logits)
     everyone = [own] + [exchange(other, sizes, "expert", step) for step in range(1, groups)]
     return mix(everyone, width)

time: 32 us -> 31.3 us (0.978)
  waiting for transfers between devices: 10.8 us -> 9.78 us
    ppermute x9, waiting for transfers between devices: 9.06 us -> 8.07 us  [exchange(): return lax.ppermute(x, ('dp', 'seq', 'expert'), pairs)]
where the time goes in v4:
time: 31.3 us; the launch traced here: 31.1 us
  starting transfers between devices  13.6 us (43%)
  waiting for transfers between devices  9.78 us (31%)
  Pallas kernels  7.59 us (24%)
    ppermute x9, starting transfers between devices, exchange(): return lax.ppermute(x, ('dp', 'seq', 'expert'), pairs)  12.7 us
    ppermute x9, waiting for transfers between devices, exchange(): return lax.ppermute(x, ('dp', 'seq', 'expert'), pairs)  8.07 us
    pallas_call x1, Pallas kernels, slot_sums(): pl.pallas_call(functools.partial(slot_sums_kernel, chunks), out_shape=jax...  3.67 us
    pallas_call x1, Pallas kernels, experts(): pl.pallas_call(experts_kernel, out_shape=jax.ShapeDtypeStruct((both.shape...  2.56 us
    pallas_call x1, Pallas kernels, mix(): pl.pallas_call(functools.partial(mix_kernel, chunks), out_shape=jax.Shape...  1.29 us
    ppermute x1, waiting for transfers between devices, on_device(): chip = partial + swapped(lax.ppermute(partial, 'dp', swap))  0.86 us
    ppermute x1, waiting for transfers between devices, on_device(): lax.ppermute(packed, 'dp', swap)  0.85 us
  transfers between devices with their start and end apart: 11, of which 10 were waited for; matrix products, arithmetic and copies ran while one was open for 0% of the time, Pallas kernels for 0%

profile of v4, /device:TPU:0, one launch (start us, length us, event | category | flops | bytes accessed | tf_op | source)
XLA Modules:
  0.0 31.1 jit_solution(14097053113880644140)
XLA Ops:
  0.0 0.0 slice-start
  0.0 0.0 slice-start.2
  0.0 3.7 %shard_map.46.own_ref = f32[2,3200]{1,0:T(2,128)S(1)} custom-call(bf16[2,2048]{1,0:T(2,128)(2,1)} %bitcast.5, bf16[1024,2048]{1,0:T(8,128)(2,1)} %tokens_hbm.1), custom_call_target="tpu_custom_call" | custom-call | tf_op jit(solution)/shard_map/pallas_call | solution.py:113
  3.7 0.0 slice-start.1
  3.7 0.0 slice-start.3
  3.7 0.5 %collective-permute-start = (f32[2,3200]{1,0:T(2,128)S(1)}, f32[2,3200]{1,0:T(2,128)S(1)}, u32[]{:S(2)}, u32[]{:S(2)}) collective-permute-start(f32[2,3200]{1,0:T(2,128)S(1)} %shard_map.46.own_ref), channel_id=1, source_target_pairs={{0,16},{16,0},{1,17},{17,1},{2,18},{18,2},{3,19},{19,3},{4,20},{20... | collective-permute-start | bytes 76808 | tf_op jit(solution)/shard_map/ppermute | solution.py:250
  4.2 0.9 %collective-permute-done.other_ref = f32[2,3200]{1,0:T(2,128)S(1)} collective-permute-done((f32[2,3200]{1,0:T(2,128)S(1)}, f32[2,3200]{1,0:T(2,128)S(1)}, u32[]{:S(2)}, u32[]{:S(2)}) %collective-permute-start) | collective-permute-done | bytes 25632 | tf_op jit(solution)/shard_map/ppermute | solution.py:250
  5.1 4.8 %collective-permute-start.3 = (bf16[4,2176]{1,0:T(4,128)(2,1)S(1)}, bf16[4,2176]{1,0:T(4,128)(2,1)S(1)}, u32[]{:S(2)}, u32[]{:S(2)}) collective-permute-start(bf16[4,2176]{1,0:T(4,128)(2,1)S(1)} %get-tuple-element.11), channel_id=1, source_target_pairs={{0,28},{1,29},{2,30},{3,31},{4,24},{5,25},{6,26},{7,27},{8,20},{9,... | collective-permute-start | bytes 52232 | tf_op jit(solution)/shard_map/ppermute | solution.py:43
  9.9 0.0 collective-permute-start.2
  9.9 0.6 %collective-permute-start.1 = (bf16[4,2176]{1,0:T(4,128)(2,1)S(1)}, bf16[4,2176]{1,0:T(4,128)(2,1)S(1)}, u32[]{:S(2)}, u32[]{:S(2)}) collective-permute-start(bf16[4,2176]{1,0:T(4,128)(2,1)S(1)} %get-tuple-element.11), channel_id=1, source_target_pairs={{0,24},{1,25},{2,26},{3,27},{4,28},{5,29},{6,30},{7,31},{8,16},{9,... | collective-permute-start | bytes 52232 | tf_op jit(solution)/shard_map/ppermute | solution.py:43
  10.5 0.9 %collective-permute-done.3.refs_2_ = bf16[4,2176]{1,0:T(4,128)(2,1)S(1)} collective-permute-done((bf16[4,2176]{1,0:T(4,128)(2,1)S(1)}, bf16[4,2176]{1,0:T(4,128)(2,1)S(1)}, u32[]{:S(2)}, u32[]{:S(2)}) %collective-permute-start.3) | collective-permute-done | bytes 17440 | tf_op jit(solution)/shard_map/ppermute | solution.py:43
  11.3 1.7 %collective-permute-done.2.refs_1_ = bf16[4,2176]{1,0:T(4,128)(2,1)S(1)} collective-permute-done((bf16[4,2176]{1,0:T(4,128)(2,1)S(1)}, bf16[4,2176]{1,0:T(4,128)(2,1)S(1)}, u32[]{:S(2)}, u32[]{:S(2)}) %collective-permute-start.2) | collective-permute-done | bytes 17440 | tf_op jit(solution)/shard_map/ppermute | solution.py:43
  13.1 0.9 %collective-permute-done.1.refs_0_ = bf16[4,2176]{1,0:T(4,128)(2,1)S(1)} collective-permute-done((bf16[4,2176]{1,0:T(4,128)(2,1)S(1)}, bf16[4,2176]{1,0:T(4,128)(2,1)S(1)}, u32[]{:S(2)}, u32[]{:S(2)}) %collective-permute-start.1) | collective-permute-done | bytes 17440 | tf_op jit(solution)/shard_map/ppermute | solution.py:43
  14.0 0.0 slice-done
  14.0 0.0 slice-done.2
  14.0 0.0 slice-done.1
  14.0 0.0 slice-done.3
  14.0 2.6 %shard_map.48 = f32[4,2048]{1,0:T(4,128)S(1)} custom-call(f32[4,2176]{1,0:T(4,128)S(1)} %get-tuple-element.10.both_ref, bf16[4,2176]{1,0:T(4,128)(2,1)S(1)} %collective-permute-done.1.refs_0_, bf16[4,2176]{1,0:T(4,128)(2,1)S(1)} %collective-permute-done.2.refs_1_, bf16[4,2176]{1,0:T(4,128)(2,1)S(1)} %collective-permute-done.3.refs_2_, ...), custom_call_target="tpu_custom_call" | custom-call | tf_op jit(solution)/shard_map/pallas_call | solution.py:174
  16.6 0.4 %collective-permute-start.4 = (f32[4,2048]{1,0:T(4,128)S(1)}, f32[4,2048]{1,0:T(4,128)S(1)}, u32[]{:S(2)}, u32[]{:S(2)}) collective-permute-start(f32[4,2048]{1,0:T(4,128)S(1)} %shard_map.48), channel_id=1, source_target_pairs={{0,16},{16,0},{1,17},{17,1},{2,18},{18,2},{3,19},{19,3},{4,20},{20... | collective-permute-start | bytes 98312 | tf_op jit(solution)/shard_map/ppermute | solution.py:253
  16.9 0.9 %collective-permute-done.4 = f32[4,2048]{1,0:T(4,128)S(1)} collective-permute-done((f32[4,2048]{1,0:T(4,128)S(1)}, f32[4,2048]{1,0:T(4,128)S(1)}, u32[]{:S(2)}, u32[]{:S(2)}) %collective-permute-start.4) | collective-permute-done | bytes 32800 | tf_op jit(solution)/shard_map/ppermute | solution.py:253
  17.8 1.7 %collective-permute-start.7 = (bf16[4,2048]{1,0:T(4,128)(2,1)S(1)}, bf16[4,2048]{1,0:T(4,128)(2,1)S(1)}, u32[]{:S(2)}, u32[]{:S(2)}) collective-permute-start(bf16[4,2048]{1,0:T(4,128)(2,1)S(1)} %get-tuple-element.15), channel_id=1, source_target_pairs={{0,28},{1,29},{2,30},{3,31},{4,24},{5,25},{6,26},{7,27},{8,20},{9,... | collective-permute-start | bytes 49160 | tf_op jit(solution)/shard_map/ppermute | solution.py:43
  19.5 0.2 collective-permute-start.6
  19.7 2.2 %collective-permute-start.5 = (bf16[4,2048]{1,0:T(4,128)(2,1)S(1)}, bf16[4,2048]{1,0:T(4,128)(2,1)S(1)}, u32[]{:S(2)}, u32[]{:S(2)}) collective-permute-start(bf16[4,2048]{1,0:T(4,128)(2,1)S(1)} %get-tuple-element.15), channel_id=1, source_target_pairs={{0,24},{1,25},{2,26},{3,27},{4,28},{5,29},{6,30},{7,31},{8,16},{9,... | collective-permute-start | bytes 49160 | tf_op jit(solution)/shard_map/ppermute | solution.py:43
  22.0 1.0 %collective-permute-done.7.refs_2_ = bf16[4,2048]{1,0:T(4,128)(2,1)S(1)} collective-permute-done((bf16[4,2048]{1,0:T(4,128)(2,1)S(1)}, bf16[4,2048]{1,0:T(4,128)(2,1)S(1)}, u32[]{:S(2)}, u32[]{:S(2)}) %collective-permute-start.7) | collective-permute-done | bytes 16416 | tf_op jit(solution)/shard_map/ppermute | solution.py:43
  23.0 0.0 collective-permute-done.6.refs_1_
  23.0 0.8 %collective-permute-done.5.refs_0_ = bf16[4,2048]{1,0:T(4,128)(2,1)S(1)} collective-permute-done((bf16[4,2048]{1,0:T(4,128)(2,1)S(1)}, bf16[4,2048]{1,0:T(4,128)(2,1)S(1)}, u32[]{:S(2)}, u32[]{:S(2)}) %collective-permute-start.5) | collective-permute-done | bytes 16416 | tf_op jit(solution)/shard_map/ppermute | solution.py:43
  23.8 2.5 %collective-permute-start.10 = (f32[2,3072]{1,0:T(2,128)S(1)}, f32[2,3072]{1,0:T(2,128)S(1)}, u32[]{:S(2)}, u32[]{:S(2)}) collective-permute-start(f32[2,3072]{1,0:T(2,128)S(1)} %get-tuple-element.14), channel_id=1, source_target_pairs={{0,19},{1,18},{2,17},{3,16},{4,23},{5,22},{6,21},{7,20},{8,27},{9,... | collective-permute-start | bytes 73736 | tf_op jit(solution)/shard_map/ppermute | solution.py:43
  26.3 0.3 collective-permute-start.9
  26.6 0.5 %collective-permute-start.8 = (f32[2,3072]{1,0:T(2,128)S(1)}, f32[2,3072]{1,0:T(2,128)S(1)}, u32[]{:S(2)}, u32[]{:S(2)}) collective-permute-start(f32[2,3072]{1,0:T(2,128)S(1)} %get-tuple-element.14), channel_id=1, source_target_pairs={{0,17},{1,16},{2,19},{3,18},{4,21},{5,20},{6,23},{7,22},{8,25},{9,... | collective-permute-start | bytes 73736 | tf_op jit(solution)/shard_map/ppermute | solution.py:43
  27.1 1.0 %collective-permute-done.10.refs_3_ = f32[2,3072]{1,0:T(2,128)S(1)} collective-permute-done((f32[2,3072]{1,0:T(2,128)S(1)}, f32[2,3072]{1,0:T(2,128)S(1)}, u32[]{:S(2)}, u32[]{:S(2)}) %collective-permute-start.10) | collective-permute-done | bytes 24608 | tf_op jit(solution)/shard_map/ppermute | solution.py:43
  28.0 1.5 %collective-permute-done.9.refs_2_ = f32[2,3072]{1,0:T(2,128)S(1)} collective-permute-done((f32[2,3072]{1,0:T(2,128)S(1)}, f32[2,3072]{1,0:T(2,128)S(1)}, u32[]{:S(2)}, u32[]{:S(2)}) %collective-permute-start.9) | collective-permute-done | bytes 24608 | tf_op jit(solution)/shard_map/ppermute | solution.py:43
  29.5 0.3 collective-permute-done.8.refs_1_
  29.8 1.3 %shard_map.50 = bf16[256,2048]{1,0:T(8,128)(2,1)} custom-call(f32[2,3072]{1,0:T(2,128)S(1)} %get-tuple-element.13.refs_0_, f32[2,3072]{1,0:T(2,128)S(1)} %collective-permute-done.8.refs_1_, f32[2,3072]{1,0:T(2,128)S(1)} %collective-permute-done.9.refs_2_, f32[2,3072]{1,0:T(2,128)S(1)} %collective-permute-done.10.refs_3_), custom_call_target="tpu_custom_call" | custom-call | tf_op jit(solution)/shard_map/pallas_call | solution.py:235
  (6 shorter events, 0.1 us)
Async XLA Ops:
  0.0 14.0 %slice-start = ((s8[8388608]{0:T(1024)(128)(4,1)}), s8[4194304]{0:T(1024)(128)(4,1)S(1)}, s32[]{:S(2)}) async-start(s8[8388608]{0:T(1024)(128)(4,1)} %bitcast.1), calls=%async_computation | async-start | bytes 8388608
  0.0 14.0 %slice-start.2 = ((s8[8388608]{0:T(1024)(128)(4,1)}), s8[4194304]{0:T(1024)(128)(4,1)S(1)}, s32[]{:S(2)}) async-start(s8[8388608]{0:T(1024)(128)(4,1)} %bitcast.3), calls=%async_computation.2 | async-start | bytes 8388608
  3.7 10.3 %slice-start.1 = ((s8[8388608]{0:T(1024)(128)(4,1)}), s8[4194304]{0:T(1024)(128)(4,1)S(1)}, s32[]{:S(2)}) async-start(s8[8388608]{0:T(1024)(128)(4,1)} %bitcast.1), calls=%async_computation.1 | async-start | bytes 8388608
  3.7 10.3 %slice-start.3 = ((s8[8388608]{0:T(1024)(128)(4,1)}), s8[4194304]{0:T(1024)(128)(4,1)S(1)}, s32[]{:S(2)}) async-start(s8[8388608]{0:T(1024)(128)(4,1)} %bitcast.3), calls=%async_computation.3 | async-start | bytes 8388608
  3.7 1.4 %collective-permute-start = (f32[2,3200]{1,0:T(2,128)S(1)}, f32[2,3200]{1,0:T(2,128)S(1)}, u32[]{:S(2)}, u32[]{:S(2)}) collective-permute-start(f32[2,3200]{1,0:T(2,128)S(1)} %shard_map.46.own_ref), channel_id=1, source_target_pairs={{0,16},{16,0},{1,17},{17,1},{2,18},{18,2},{3,19},{19,3},{4,20},{20... | collective-permute-start | bytes 76808 | tf_op jit(solution)/shard_map/ppermute | solution.py:250
  5.1 6.2 %collective-permute-start.3 = (bf16[4,2176]{1,0:T(4,128)(2,1)S(1)}, bf16[4,2176]{1,0:T(4,128)(2,1)S(1)}, u32[]{:S(2)}, u32[]{:S(2)}) collective-permute-start(bf16[4,2176]{1,0:T(4,128)(2,1)S(1)} %get-tuple-element.11), channel_id=1, source_target_pairs={{0,28},{1,29},{2,30},{3,31},{4,24},{5,25},{6,26},{7,27},{8,20},{9,... | collective-permute-start | bytes 52232 | tf_op jit(solution)/shard_map/ppermute | solution.py:43
  9.9 3.2 %collective-permute-start.2 = (bf16[4,2176]{1,0:T(4,128)(2,1)S(1)}, bf16[4,2176]{1,0:T(4,128)(2,1)S(1)}, u32[]{:S(2)}, u32[]{:S(2)}) collective-permute-start(bf16[4,2176]{1,0:T(4,128)(2,1)S(1)} %get-tuple-element.11), channel_id=1, source_target_pairs={{0,20},{1,21},{2,22},{3,23},{4,16},{5,17},{6,18},{7,19},{8,28},{9,... | collective-permute-start | bytes 52232 | tf_op jit(solution)/shard_map/ppermute | solution.py:43
  9.9 4.1 %collective-permute-start.1 = (bf16[4,2176]{1,0:T(4,128)(2,1)S(1)}, bf16[4,2176]{1,0:T(4,128)(2,1)S(1)}, u32[]{:S(2)}, u32[]{:S(2)}) collective-permute-start(bf16[4,2176]{1,0:T(4,128)(2,1)S(1)} %get-tuple-element.11), channel_id=1, source_target_pairs={{0,24},{1,25},{2,26},{3,27},{4,28},{5,29},{6,30},{7,31},{8,16},{9,... | collective-permute-start | bytes 52232 | tf_op jit(solution)/shard_map/ppermute | solution.py:43
  16.6 1.2 %collective-permute-start.4 = (f32[4,2048]{1,0:T(4,128)S(1)}, f32[4,2048]{1,0:T(4,128)S(1)}, u32[]{:S(2)}, u32[]{:S(2)}) collective-permute-start(f32[4,2048]{1,0:T(4,128)S(1)} %shard_map.48), channel_id=1, source_target_pairs={{0,16},{16,0},{1,17},{17,1},{2,18},{18,2},{3,19},{19,3},{4,20},{20... | collective-permute-start | bytes 98312 | tf_op jit(solution)/shard_map/ppermute | solution.py:253
  17.8 5.1 %collective-permute-start.7 = (bf16[4,2048]{1,0:T(4,128)(2,1)S(1)}, bf16[4,2048]{1,0:T(4,128)(2,1)S(1)}, u32[]{:S(2)}, u32[]{:S(2)}) collective-permute-start(bf16[4,2048]{1,0:T(4,128)(2,1)S(1)} %get-tuple-element.15), channel_id=1, source_target_pairs={{0,28},{1,29},{2,30},{3,31},{4,24},{5,25},{6,26},{7,27},{8,20},{9,... | collective-permute-start | bytes 49160 | tf_op jit(solution)/shard_map/ppermute | solution.py:43
  19.5 3.4 %collective-permute-start.6 = (bf16[4,2048]{1,0:T(4,128)(2,1)S(1)}, bf16[4,2048]{1,0:T(4,128)(2,1)S(1)}, u32[]{:S(2)}, u32[]{:S(2)}) collective-permute-start(bf16[4,2048]{1,0:T(4,128)(2,1)S(1)} %get-tuple-element.15), channel_id=1, source_target_pairs={{0,20},{1,21},{2,22},{3,23},{4,16},{5,17},{6,18},{7,19},{8,28},{9,... | collective-permute-start | bytes 49160 | tf_op jit(solution)/shard_map/ppermute | solution.py:43
  19.7 4.1 %collective-permute-start.5 = (bf16[4,2048]{1,0:T(4,128)(2,1)S(1)}, bf16[4,2048]{1,0:T(4,128)(2,1)S(1)}, u32[]{:S(2)}, u32[]{:S(2)}) collective-permute-start(bf16[4,2048]{1,0:T(4,128)(2,1)S(1)} %get-tuple-element.15), channel_id=1, source_target_pairs={{0,24},{1,25},{2,26},{3,27},{4,28},{5,29},{6,30},{7,31},{8,16},{9,... | collective-permute-start | bytes 49160 | tf_op jit(solution)/shard_map/ppermute | solution.py:43
  23.8 4.2 %collective-permute-start.10 = (f32[2,3072]{1,0:T(2,128)S(1)}, f32[2,3072]{1,0:T(2,128)S(1)}, u32[]{:S(2)}, u32[]{:S(2)}) collective-permute-start(f32[2,3072]{1,0:T(2,128)S(1)} %get-tuple-element.14), channel_id=1, source_target_pairs={{0,19},{1,18},{2,17},{3,16},{4,23},{5,22},{6,21},{7,20},{8,27},{9,... | collective-permute-start | bytes 73736 | tf_op jit(solution)/shard_map/ppermute | solution.py:43
  26.3 3.3 %collective-permute-start.9 = (f32[2,3072]{1,0:T(2,128)S(1)}, f32[2,3072]{1,0:T(2,128)S(1)}, u32[]{:S(2)}, u32[]{:S(2)}) collective-permute-start(f32[2,3072]{1,0:T(2,128)S(1)} %get-tuple-element.14), channel_id=1, source_target_pairs={{0,18},{1,19},{2,16},{3,17},{4,22},{5,23},{6,20},{7,21},{8,26},{9,... | collective-permute-start | bytes 73736 | tf_op jit(solution)/shard_map/ppermute | solution.py:43
  26.6 3.3 %collective-permute-start.8 = (f32[2,3072]{1,0:T(2,128)S(1)}, f32[2,3072]{1,0:T(2,128)S(1)}, u32[]{:S(2)}, u32[]{:S(2)}) collective-permute-start(f32[2,3072]{1,0:T(2,128)S(1)} %get-tuple-element.14), channel_id=1, source_target_pairs={{0,17},{1,16},{2,19},{3,18},{4,21},{5,20},{6,23},{7,22},{8,25},{9,... | collective-permute-start | bytes 73736 | tf_op jit(solution)/shard_map/ppermute | solution.py:43

commit v5 on v4

--- a/solution.py
+++ b/solution.py
@@ -26,13 +26,21 @@
     return [(i, i ^ step) for i in range(n)]
 
 
-def middle_first(n):
-    return sorted(range(1, n), key=lambda step: (step != n // 2, step))
-
-
-def exchange(x, sizes, axis, step):
+def around(ring, step):
+    n = len(ring)
+    return [(ring[i], ring[(i + step) % n]) for i in range(n)]
+
+
+def halves_first(n):
+    if n % 2 or n < 4:
+        return list(range(n))
+    inner = halves_first(n // 2)
+    return [2 * i for i in inner] + [2 * i + 1 for i in inner]
+
+
+def exchange(x, sizes, axis, moves):
     cores, seqs, groups = sizes
-    to = dict(partners(seqs if axis == "seq" else groups, step))
+    to = dict(moves)
     pairs = []
     for core in range(cores):
         for seq in range(seqs):
@@ -91,7 +99,7 @@
         spread = jnp.exp(logits - top)
         tops.append(top)
         totals.append(jnp.sum(spread, axis=1, keepdims=True))
-        sums.append(jnp.dot(spread.astype(BF16), held[part, :], preferred_element_type=F32))
+        sums.append(finely(spread, held[part, :]))
 
     before = None
     for c in range(chunks):
@@ -154,6 +162,13 @@
     )(own, other)
 
 
+def finely(x, y):
+    high = x.astype(BF16)
+    low = (x - high.astype(F32)).astype(BF16)
+    both = jnp.dot(jnp.concatenate([high, low], axis=0), y, preferred_element_type=F32)
+    return both[: x.shape[0]] + both[x.shape[0] :]
+
+
 def gelu(v):
     return 0.5 * v * (1.0 + jnp.tanh(0.7978845608028654 * (v + 0.044715 * v * v * v)))
 
@@ -164,8 +179,7 @@
     slot_in = joined([both_ref[...]] + [swapped(r[...].astype(F32)) for r in received], width)
     for e in range(slots):
         x = jnp.concatenate([slot_in[e : e + 1], slot_in[slots + e : slots + e + 1]], axis=0)
-        hidden = jnp.dot(x.astype(BF16), first_ref[e], preferred_element_type=F32)
-        value = jnp.dot(gelu(hidden).astype(BF16), second_ref[e], preferred_element_type=F32)
+        value = finely(gelu(finely(x, first_ref[e])), second_ref[e])
         out_ref[e : e + 1, :] = value[:1]
         out_ref[slots + e : slots + e + 1, :] = value[1:]
 
@@ -248,13 +262,18 @@
     swap = partners(cores, 1)
     packed = slot_sums(phi.T, tokens)
     sent, both, logits = pair(packed, lax.ppermute(packed, "dp", swap), width + LANES)
-    received = [exchange(sent, sizes, "seq", step) for step in middle_first(seqs)]
+    received = [
+        exchange(sent, sizes, "seq", around(halves_first(seqs), step)) for step in [*range(2, seqs), 1]
+    ]
     partial = experts(both, received, w_in, w_out)
     chip = partial + swapped(lax.ppermute(partial, "dp", swap))
     sent = chip.astype(BF16)
-    sums = [exchange(sent, sizes, "seq", step) for step in middle_first(seqs)]
+    sums = [
+        exchange(sent, sizes, "seq", around(range(seqs), step)) for step in range(seqs - 1, 0, -1)
+    ]
     own, other = pack(chip, sums, logits)
-    everyone = [own] + [exchange(other, sizes, "expert", step) for step in range(1, groups)]
+    order = sorted(range(1, groups), key=lambda step: (step != groups // 2, step))
+    everyone = [own] + [exchange(other, sizes, "expert", partners(groups, step)) for step in order]
     return mix(everyone, width)
 
 

time: 31.3 us -> 30.8 us (0.984)
  waiting for transfers between devices: 9.78 us -> 9.41 us
    ppermute x9, waiting for transfers between devices: 8.07 us -> 7.69 us  [exchange(): return lax.ppermute(x, ('dp', 'seq', 'expert'), pairs)]
  transfers between devices with their start and end apart: 11 -> 11, of which waited for: 10 -> 11; matrix products, arithmetic and copies ran while one was open for 0% -> 0% of each run, Pallas kernels for 0% -> 0%
where the time goes in v5:
time: 30.8 us; the launch traced here: 30.7 us
  starting transfers between devices  13.5 us (44%)
  waiting for transfers between devices  9.41 us (31%)
  Pallas kernels  7.63 us (25%)
    ppermute x9, starting transfers between devices, exchange(): return lax.ppermute(x, ('dp', 'seq', 'expert'), pairs)  12.6 us
    ppermute x9, waiting for transfers between devices, exchange(): return lax.ppermute(x, ('dp', 'seq', 'expert'), pairs)  7.69 us
    pallas_call x1, Pallas kernels, slot_sums(): pl.pallas_call(functools.partial(slot_sums_kernel, chunks), out_shape=jax...  3.69 us
    pallas_call x1, Pallas kernels, experts(): pl.pallas_call(experts_kernel, out_shape=jax.ShapeDtypeStruct((both.shape...  2.58 us
    pallas_call x1, Pallas kernels, mix(): pl.pallas_call(functools.partial(mix_kernel, chunks), out_shape=jax.Shape...  1.29 us
    ppermute x1, waiting for transfers between devices, on_device(): chip = partial + swapped(lax.ppermute(partial, 'dp', swap))  0.86 us
    ppermute x1, waiting for transfers between devices, on_device(): lax.ppermute(packed, 'dp', swap)  0.85 us
  transfers between devices with their start and end apart: 11, of which 11 were waited for; matrix products, arithmetic and copies ran while one was open for 0% of the time, Pallas kernels for 0%

profile of v5, /device:TPU:0, one launch (start us, length us, event | category | flops | bytes accessed | tf_op | source)
XLA Modules:
  0.0 30.7 jit_solution(5849835050253229835)
XLA Ops:
  0.0 0.0 slice-start
  0.0 0.0 slice-start.2
  0.0 3.7 %shard_map.46.own_ref = f32[2,3200]{1,0:T(2,128)S(1)} custom-call(bf16[2,2048]{1,0:T(2,128)(2,1)} %bitcast.5, bf16[1024,2048]{1,0:T(8,128)(2,1)} %tokens_hbm.1), custom_call_target="tpu_custom_call" | custom-call | tf_op jit(solution)/shard_map/pallas_call | solution.py:121
  3.7 0.0 slice-start.1
  3.7 0.0 slice-start.3
  3.7 0.5 %collective-permute-start = (f32[2,3200]{1,0:T(2,128)S(1)}, f32[2,3200]{1,0:T(2,128)S(1)}, u32[]{:S(2)}, u32[]{:S(2)}) collective-permute-start(f32[2,3200]{1,0:T(2,128)S(1)} %shard_map.46.own_ref), channel_id=1, source_target_pairs={{0,16},{16,0},{1,17},{17,1},{2,18},{18,2},{3,19},{19,3},{4,20},{20... | collective-permute-start | bytes 76808 | tf_op jit(solution)/shard_map/ppermute | solution.py:264
  4.2 0.9 %collective-permute-done.other_ref = f32[2,3200]{1,0:T(2,128)S(1)} collective-permute-done((f32[2,3200]{1,0:T(2,128)S(1)}, f32[2,3200]{1,0:T(2,128)S(1)}, u32[]{:S(2)}, u32[]{:S(2)}) %collective-permute-start) | collective-permute-done | bytes 25632 | tf_op jit(solution)/shard_map/ppermute | solution.py:264
  5.1 3.8 %collective-permute-start.3 = (bf16[4,2176]{1,0:T(4,128)(2,1)S(1)}, bf16[4,2176]{1,0:T(4,128)(2,1)S(1)}, u32[]{:S(2)}, u32[]{:S(2)}) collective-permute-start(bf16[4,2176]{1,0:T(4,128)(2,1)S(1)} %get-tuple-element.11), channel_id=1, source_target_pairs={{0,24},{1,25},{2,26},{3,27},{4,28},{5,29},{6,30},{7,31},{8,20},{9,... | collective-permute-start | bytes 52232 | tf_op jit(solution)/shard_map/ppermute | solution.py:51
  8.9 1.1 %collective-permute-start.2 = (bf16[4,2176]{1,0:T(4,128)(2,1)S(1)}, bf16[4,2176]{1,0:T(4,128)(2,1)S(1)}, u32[]{:S(2)}, u32[]{:S(2)}) collective-permute-start(bf16[4,2176]{1,0:T(4,128)(2,1)S(1)} %get-tuple-element.11), channel_id=1, source_target_pairs={{0,28},{1,29},{2,30},{3,31},{4,24},{5,25},{6,26},{7,27},{8,16},{9,... | collective-permute-start | bytes 52232 | tf_op jit(solution)/shard_map/ppermute | solution.py:51
  10.0 0.5 %collective-permute-start.1 = (bf16[4,2176]{1,0:T(4,128)(2,1)S(1)}, bf16[4,2176]{1,0:T(4,128)(2,1)S(1)}, u32[]{:S(2)}, u32[]{:S(2)}) collective-permute-start(bf16[4,2176]{1,0:T(4,128)(2,1)S(1)} %get-tuple-element.11), channel_id=1, source_target_pairs={{0,20},{1,21},{2,22},{3,23},{4,16},{5,17},{6,18},{7,19},{8,28},{9,... | collective-permute-start | bytes 52232 | tf_op jit(solution)/shard_map/ppermute | solution.py:51
  10.4 0.9 %collective-permute-done.3.refs_2_ = bf16[4,2176]{1,0:T(4,128)(2,1)S(1)} collective-permute-done((bf16[4,2176]{1,0:T(4,128)(2,1)S(1)}, bf16[4,2176]{1,0:T(4,128)(2,1)S(1)}, u32[]{:S(2)}, u32[]{:S(2)}) %collective-permute-start.3) | collective-permute-done | bytes 17440 | tf_op jit(solution)/shard_map/ppermute | solution.py:51
  11.3 1.6 %collective-permute-done.2.refs_1_ = bf16[4,2176]{1,0:T(4,128)(2,1)S(1)} collective-permute-done((bf16[4,2176]{1,0:T(4,128)(2,1)S(1)}, bf16[4,2176]{1,0:T(4,128)(2,1)S(1)}, u32[]{:S(2)}, u32[]{:S(2)}) %collective-permute-start.2) | collective-permute-done | bytes 17440 | tf_op jit(solution)/shard_map/ppermute | solution.py:51
  12.9 0.2 collective-permute-done.1.refs_0_
  13.1 0.0 slice-done
  13.1 0.0 slice-done.2
  13.1 0.0 slice-done.1
  13.1 0.0 slice-done.3
  13.2 2.6 %shard_map.48 = f32[4,2048]{1,0:T(4,128)S(1)} custom-call(f32[4,2176]{1,0:T(4,128)S(1)} %get-tuple-element.10.both_ref, bf16[4,2176]{1,0:T(4,128)(2,1)S(1)} %collective-permute-done.1.refs_0_, bf16[4,2176]{1,0:T(4,128)(2,1)S(1)} %collective-permute-done.2.refs_1_, bf16[4,2176]{1,0:T(4,128)(2,1)S(1)} %collective-permute-done.3.refs_2_, ...), custom_call_target="tpu_custom_call" | custom-call | tf_op jit(solution)/shard_map/pallas_call | solution.py:188
  15.7 0.4 %collective-permute-start.4 = (f32[4,2048]{1,0:T(4,128)S(1)}, f32[4,2048]{1,0:T(4,128)S(1)}, u32[]{:S(2)}, u32[]{:S(2)}) collective-permute-start(f32[4,2048]{1,0:T(4,128)S(1)} %shard_map.48), channel_id=1, source_target_pairs={{0,16},{16,0},{1,17},{17,1},{2,18},{18,2},{3,19},{19,3},{4,20},{20... | collective-permute-start | bytes 98312 | tf_op jit(solution)/shard_map/ppermute | solution.py:269
  16.1 0.9 %collective-permute-done.4 = f32[4,2048]{1,0:T(4,128)S(1)} collective-permute-done((f32[4,2048]{1,0:T(4,128)S(1)}, f32[4,2048]{1,0:T(4,128)S(1)}, u32[]{:S(2)}, u32[]{:S(2)}) %collective-permute-start.4) | collective-permute-done | bytes 32800 | tf_op jit(solution)/shard_map/ppermute | solution.py:269
  17.0 1.5 %collective-permute-start.7 = (bf16[4,2048]{1,0:T(4,128)(2,1)S(1)}, bf16[4,2048]{1,0:T(4,128)(2,1)S(1)}, u32[]{:S(2)}, u32[]{:S(2)}) collective-permute-start(bf16[4,2048]{1,0:T(4,128)(2,1)S(1)} %get-tuple-element.15), channel_id=1, source_target_pairs={{0,20},{1,21},{2,22},{3,23},{4,24},{5,25},{6,26},{7,27},{8,28},{9,... | collective-permute-start | bytes 49160 | tf_op jit(solution)/shard_map/ppermute | solution.py:51
  18.5 1.7 %collective-permute-start.6 = (bf16[4,2048]{1,0:T(4,128)(2,1)S(1)}, bf16[4,2048]{1,0:T(4,128)(2,1)S(1)}, u32[]{:S(2)}, u32[]{:S(2)}) collective-permute-start(bf16[4,2048]{1,0:T(4,128)(2,1)S(1)} %get-tuple-element.15), channel_id=1, source_target_pairs={{0,24},{1,25},{2,26},{3,27},{4,28},{5,29},{6,30},{7,31},{8,16},{9,... | collective-permute-start | bytes 49160 | tf_op jit(solution)/shard_map/ppermute | solution.py:51
  20.2 1.2 %collective-permute-start.5 = (bf16[4,2048]{1,0:T(4,128)(2,1)S(1)}, bf16[4,2048]{1,0:T(4,128)(2,1)S(1)}, u32[]{:S(2)}, u32[]{:S(2)}) collective-permute-start(bf16[4,2048]{1,0:T(4,128)(2,1)S(1)} %get-tuple-element.15), channel_id=1, source_target_pairs={{0,28},{1,29},{2,30},{3,31},{4,16},{5,17},{6,18},{7,19},{8,20},{9,... | collective-permute-start | bytes 49160 | tf_op jit(solution)/shard_map/ppermute | solution.py:51
  21.3 0.7 %collective-permute-done.7.refs_2_ = bf16[4,2048]{1,0:T(4,128)(2,1)S(1)} collective-permute-done((bf16[4,2048]{1,0:T(4,128)(2,1)S(1)}, bf16[4,2048]{1,0:T(4,128)(2,1)S(1)}, u32[]{:S(2)}, u32[]{:S(2)}) %collective-permute-start.7) | collective-permute-done | bytes 16416 | tf_op jit(solution)/shard_map/ppermute | solution.py:51
  22.0 0.9 %collective-permute-done.6.refs_1_ = bf16[4,2048]{1,0:T(4,128)(2,1)S(1)} collective-permute-done((bf16[4,2048]{1,0:T(4,128)(2,1)S(1)}, bf16[4,2048]{1,0:T(4,128)(2,1)S(1)}, u32[]{:S(2)}, u32[]{:S(2)}) %collective-permute-start.6) | collective-permute-done | bytes 16416 | tf_op jit(solution)/shard_map/ppermute | solution.py:51
  23.0 0.4 %collective-permute-done.5.refs_0_ = bf16[4,2048]{1,0:T(4,128)(2,1)S(1)} collective-permute-done((bf16[4,2048]{1,0:T(4,128)(2,1)S(1)}, bf16[4,2048]{1,0:T(4,128)(2,1)S(1)}, u32[]{:S(2)}, u32[]{:S(2)}) %collective-permute-start.5) | collective-permute-done | bytes 16416 | tf_op jit(solution)/shard_map/ppermute | solution.py:51
  23.4 2.3 %collective-permute-start.10 = (f32[2,3072]{1,0:T(2,128)S(1)}, f32[2,3072]{1,0:T(2,128)S(1)}, u32[]{:S(2)}, u32[]{:S(2)}) collective-permute-start(f32[2,3072]{1,0:T(2,128)S(1)} %get-tuple-element.14), channel_id=1, source_target_pairs={{0,19},{1,18},{2,17},{3,16},{4,23},{5,22},{6,21},{7,20},{8,27},{9,... | collective-permute-start | bytes 73736 | tf_op jit(solution)/shard_map/ppermute | solution.py:51
  25.7 0.5 %collective-permute-start.9 = (f32[2,3072]{1,0:T(2,128)S(1)}, f32[2,3072]{1,0:T(2,128)S(1)}, u32[]{:S(2)}, u32[]{:S(2)}) collective-permute-start(f32[2,3072]{1,0:T(2,128)S(1)} %get-tuple-element.14), channel_id=1, source_target_pairs={{0,17},{1,16},{2,19},{3,18},{4,21},{5,20},{6,23},{7,22},{8,25},{9,... | collective-permute-start | bytes 73736 | tf_op jit(solution)/shard_map/ppermute | solution.py:51
  26.1 0.3 collective-permute-start.8
  26.4 1.2 %collective-permute-done.10.refs_3_ = f32[2,3072]{1,0:T(2,128)S(1)} collective-permute-done((f32[2,3072]{1,0:T(2,128)S(1)}, f32[2,3072]{1,0:T(2,128)S(1)}, u32[]{:S(2)}, u32[]{:S(2)}) %collective-permute-start.10) | collective-permute-done | bytes 24608 | tf_op jit(solution)/shard_map/ppermute | solution.py:51
  27.6 1.3 %collective-permute-done.9.refs_2_ = f32[2,3072]{1,0:T(2,128)S(1)} collective-permute-done((f32[2,3072]{1,0:T(2,128)S(1)}, f32[2,3072]{1,0:T(2,128)S(1)}, u32[]{:S(2)}, u32[]{:S(2)}) %collective-permute-start.9) | collective-permute-done | bytes 24608 | tf_op jit(solution)/shard_map/ppermute | solution.py:51
  28.9 0.5 %collective-permute-done.8.refs_1_ = f32[2,3072]{1,0:T(2,128)S(1)} collective-permute-done((f32[2,3072]{1,0:T(2,128)S(1)}, f32[2,3072]{1,0:T(2,128)S(1)}, u32[]{:S(2)}, u32[]{:S(2)}) %collective-permute-start.8) | collective-permute-done | bytes 24608 | tf_op jit(solution)/shard_map/ppermute | solution.py:51
  29.4 1.3 %shard_map.50 = bf16[256,2048]{1,0:T(8,128)(2,1)} custom-call(f32[2,3072]{1,0:T(2,128)S(1)} %get-tuple-element.13.refs_0_, f32[2,3072]{1,0:T(2,128)S(1)} %collective-permute-done.8.refs_1_, f32[2,3072]{1,0:T(2,128)S(1)} %collective-permute-done.9.refs_2_, f32[2,3072]{1,0:T(2,128)S(1)} %collective-permute-done.10.refs_3_), custom_call_target="tpu_custom_call" | custom-call | tf_op jit(solution)/shard_map/pallas_call | solution.py:249
  (6 shorter events, 0.1 us)
Async XLA Ops:
  0.0 13.1 %slice-start = ((s8[8388608]{0:T(1024)(128)(4,1)}), s8[4194304]{0:T(1024)(128)(4,1)S(1)}, s32[]{:S(2)}) async-start(s8[8388608]{0:T(1024)(128)(4,1)} %bitcast.1), calls=%async_computation | async-start | bytes 8388608
  0.0 13.1 %slice-start.2 = ((s8[8388608]{0:T(1024)(128)(4,1)}), s8[4194304]{0:T(1024)(128)(4,1)S(1)}, s32[]{:S(2)}) async-start(s8[8388608]{0:T(1024)(128)(4,1)} %bitcast.3), calls=%async_computation.2 | async-start | bytes 8388608
  3.7 9.4 %slice-start.1 = ((s8[8388608]{0:T(1024)(128)(4,1)}), s8[4194304]{0:T(1024)(128)(4,1)S(1)}, s32[]{:S(2)}) async-start(s8[8388608]{0:T(1024)(128)(4,1)} %bitcast.1), calls=%async_computation.1 | async-start | bytes 8388608
  3.7 9.4 %slice-start.3 = ((s8[8388608]{0:T(1024)(128)(4,1)}), s8[4194304]{0:T(1024)(128)(4,1)S(1)}, s32[]{:S(2)}) async-start(s8[8388608]{0:T(1024)(128)(4,1)} %bitcast.3), calls=%async_computation.3 | async-start | bytes 8388608
  3.7 1.4 %collective-permute-start = (f32[2,3200]{1,0:T(2,128)S(1)}, f32[2,3200]{1,0:T(2,128)S(1)}, u32[]{:S(2)}, u32[]{:S(2)}) collective-permute-start(f32[2,3200]{1,0:T(2,128)S(1)} %shard_map.46.own_ref), channel_id=1, source_target_pairs={{0,16},{16,0},{1,17},{17,1},{2,18},{18,2},{3,19},{19,3},{4,20},{20... | collective-permute-start | bytes 76808 | tf_op jit(solution)/shard_map/ppermute | solution.py:264
  5.1 6.2 %collective-permute-start.3 = (bf16[4,2176]{1,0:T(4,128)(2,1)S(1)}, bf16[4,2176]{1,0:T(4,128)(2,1)S(1)}, u32[]{:S(2)}, u32[]{:S(2)}) collective-permute-start(bf16[4,2176]{1,0:T(4,128)(2,1)S(1)} %get-tuple-element.11), channel_id=1, source_target_pairs={{0,24},{1,25},{2,26},{3,27},{4,28},{5,29},{6,30},{7,31},{8,20},{9,... | collective-permute-start | bytes 52232 | tf_op jit(solution)/shard_map/ppermute | solution.py:51
  8.9 4.1 %collective-permute-start.2 = (bf16[4,2176]{1,0:T(4,128)(2,1)S(1)}, bf16[4,2176]{1,0:T(4,128)(2,1)S(1)}, u32[]{:S(2)}, u32[]{:S(2)}) collective-permute-start(bf16[4,2176]{1,0:T(4,128)(2,1)S(1)} %get-tuple-element.11), channel_id=1, source_target_pairs={{0,28},{1,29},{2,30},{3,31},{4,24},{5,25},{6,26},{7,27},{8,16},{9,... | collective-permute-start | bytes 52232 | tf_op jit(solution)/shard_map/ppermute | solution.py:51
  10.0 3.2 %collective-permute-start.1 = (bf16[4,2176]{1,0:T(4,128)(2,1)S(1)}, bf16[4,2176]{1,0:T(4,128)(2,1)S(1)}, u32[]{:S(2)}, u32[]{:S(2)}) collective-permute-start(bf16[4,2176]{1,0:T(4,128)(2,1)S(1)} %get-tuple-element.11), channel_id=1, source_target_pairs={{0,20},{1,21},{2,22},{3,23},{4,16},{5,17},{6,18},{7,19},{8,28},{9,... | collective-permute-start | bytes 52232 | tf_op jit(solution)/shard_map/ppermute | solution.py:51
  15.7 1.2 %collective-permute-start.4 = (f32[4,2048]{1,0:T(4,128)S(1)}, f32[4,2048]{1,0:T(4,128)S(1)}, u32[]{:S(2)}, u32[]{:S(2)}) collective-permute-start(f32[4,2048]{1,0:T(4,128)S(1)} %shard_map.48), channel_id=1, source_target_pairs={{0,16},{16,0},{1,17},{17,1},{2,18},{18,2},{3,19},{19,3},{4,20},{20... | collective-permute-start | bytes 98312 | tf_op jit(solution)/shard_map/ppermute | solution.py:269
  17.0 5.0 %collective-permute-start.7 = (bf16[4,2048]{1,0:T(4,128)(2,1)S(1)}, bf16[4,2048]{1,0:T(4,128)(2,1)S(1)}, u32[]{:S(2)}, u32[]{:S(2)}) collective-permute-start(bf16[4,2048]{1,0:T(4,128)(2,1)S(1)} %get-tuple-element.15), channel_id=1, source_target_pairs={{0,20},{1,21},{2,22},{3,23},{4,24},{5,25},{6,26},{7,27},{8,28},{9,... | collective-permute-start | bytes 49160 | tf_op jit(solution)/shard_map/ppermute | solution.py:51
  18.5 4.5 %collective-permute-start.6 = (bf16[4,2048]{1,0:T(4,128)(2,1)S(1)}, bf16[4,2048]{1,0:T(4,128)(2,1)S(1)}, u32[]{:S(2)}, u32[]{:S(2)}) collective-permute-start(bf16[4,2048]{1,0:T(4,128)(2,1)S(1)} %get-tuple-element.15), channel_id=1, source_target_pairs={{0,24},{1,25},{2,26},{3,27},{4,28},{5,29},{6,30},{7,31},{8,16},{9,... | collective-permute-start | bytes 49160 | tf_op jit(solution)/shard_map/ppermute | solution.py:51
  20.2 3.2 %collective-permute-start.5 = (bf16[4,2048]{1,0:T(4,128)(2,1)S(1)}, bf16[4,2048]{1,0:T(4,128)(2,1)S(1)}, u32[]{:S(2)}, u32[]{:S(2)}) collective-permute-start(bf16[4,2048]{1,0:T(4,128)(2,1)S(1)} %get-tuple-element.15), channel_id=1, source_target_pairs={{0,28},{1,29},{2,30},{3,31},{4,16},{5,17},{6,18},{7,19},{8,20},{9,... | collective-permute-start | bytes 49160 | tf_op jit(solution)/shard_map/ppermute | solution.py:51
  23.4 4.2 %collective-permute-start.10 = (f32[2,3072]{1,0:T(2,128)S(1)}, f32[2,3072]{1,0:T(2,128)S(1)}, u32[]{:S(2)}, u32[]{:S(2)}) collective-permute-start(f32[2,3072]{1,0:T(2,128)S(1)} %get-tuple-element.14), channel_id=1, source_target_pairs={{0,19},{1,18},{2,17},{3,16},{4,23},{5,22},{6,21},{7,20},{8,27},{9,... | collective-permute-start | bytes 73736 | tf_op jit(solution)/shard_map/ppermute | solution.py:51
  25.7 3.3 %collective-permute-start.9 = (f32[2,3072]{1,0:T(2,128)S(1)}, f32[2,3072]{1,0:T(2,128)S(1)}, u32[]{:S(2)}, u32[]{:S(2)}) collective-permute-start(f32[2,3072]{1,0:T(2,128)S(1)} %get-tuple-element.14), channel_id=1, source_target_pairs={{0,17},{1,16},{2,19},{3,18},{4,21},{5,20},{6,23},{7,22},{8,25},{9,... | collective-permute-start | bytes 73736 | tf_op jit(solution)/shard_map/ppermute | solution.py:51
  26.1 3.3 %collective-permute-start.8 = (f32[2,3072]{1,0:T(2,128)S(1)}, f32[2,3072]{1,0:T(2,128)S(1)}, u32[]{:S(2)}, u32[]{:S(2)}) collective-permute-start(f32[2,3072]{1,0:T(2,128)S(1)} %get-tuple-element.14), channel_id=1, source_target_pairs={{0,18},{1,19},{2,16},{3,17},{4,22},{5,23},{6,20},{7,21},{8,26},{9,... | collective-permute-start | bytes 73736 | tf_op jit(solution)/shard_map/ppermute | solution.py:51

commit v6 on v5

--- a/solution.py
+++ b/solution.py
@@ -87,8 +87,10 @@
     for c in range(chunks):
         copy(c).start()
     phi_copy.wait()
-    spare = jnp.zeros((8 - slots % 8, width), F32)
-    phi = jnp.concatenate([phi_ref[...].astype(F32), spare], axis=0).T.astype(BF16)
+    spare = 8 - slots % 8
+    by_slot = phi_ref[...].astype(F32)
+    phi = jnp.concatenate([by_slot, jnp.zeros((spare, width), F32)], axis=0).T.astype(BF16)
+    direct = rows // 4
     tops, sums, totals = [], [], []
 
     def finish(c, by_token):
@@ -104,7 +106,11 @@
     before = None
     for c in range(chunks):
         copy(c).wait()
-        now = jnp.dot(held[pl.ds(c * rows, rows), :], phi, preferred_element_type=F32)
+        main = jnp.dot(held[pl.ds(c * rows, rows - direct), :], phi, preferred_element_type=F32)
+        rest = held[pl.ds((c + 1) * rows - direct, direct), :].astype(F32)
+        columns = [jnp.sum(rest * by_slot[s : s + 1], axis=1, keepdims=True) for s in range(slots)]
+        columns.append(jnp.zeros((direct, spare), F32))
+        now = jnp.concatenate([main, jnp.concatenate(columns, axis=1)], axis=0)
         if c:
             finish(c - 1, before)
         before = now
@@ -177,9 +183,13 @@
     *received, first_ref, second_ref, out_ref = refs
     slots, width = first_ref.shape[:2]
     slot_in = joined([both_ref[...]] + [swapped(r[...].astype(F32)) for r in received], width)
+    xs = [
+        jnp.concatenate([slot_in[e : e + 1], slot_in[slots + e : slots + e + 1]], axis=0)
+        for e in range(slots)
+    ]
+    hidden = [gelu(finely(x, first_ref[e])) for e, x in enumerate(xs)]
     for e in range(slots):
-        x = jnp.concatenate([slot_in[e : e + 1], slot_in[slots + e : slots + e + 1]], axis=0)
-        value = finely(gelu(finely(x, first_ref[e])), second_ref[e])
+        value = finely(hidden[e], second_ref[e])
         out_ref[e : e + 1, :] = value[:1]
         out_ref[slots + e : slots + e + 1, :] = value[1:]
 

time: 30.8 us -> 30.6 us (level)
  no operation moved by 1% of the time
where the time goes in v6:
time: 30.6 us; the launch traced here: 30.5 us
  starting transfers between devices  13.5 us (44%)
  waiting for transfers between devices  9.4 us (31%)
  Pallas kernels  7.42 us (24%)
    ppermute x9, starting transfers between devices, exchange(): return lax.ppermute(x, ('dp', 'seq', 'expert'), pairs)  12.7 us
    ppermute x9, waiting for transfers between devices, exchange(): return lax.ppermute(x, ('dp', 'seq', 'expert'), pairs)  7.69 us
    pallas_call x1, Pallas kernels, slot_sums(): pl.pallas_call(functools.partial(slot_sums_kernel, chunks), out_shape=jax...  3.55 us
    pallas_call x1, Pallas kernels, experts(): pl.pallas_call(experts_kernel, out_shape=jax.ShapeDtypeStruct((both.shape...  2.51 us
    pallas_call x1, Pallas kernels, mix(): pl.pallas_call(functools.partial(mix_kernel, chunks), out_shape=jax.Shape...  1.28 us
    ppermute x1, waiting for transfers between devices, on_device(): chip = partial + swapped(lax.ppermute(partial, 'dp', swap))  0.86 us
    ppermute x1, waiting for transfers between devices, on_device(): lax.ppermute(packed, 'dp', swap)  0.85 us
  transfers between devices with their start and end apart: 11, of which 11 were waited for; matrix products, arithmetic and copies ran while one was open for 0% of the time, Pallas kernels for 0%

profile of v6, /device:TPU:0, one launch (start us, length us, event | category | flops | bytes accessed | tf_op | source)
XLA Modules:
  0.0 30.5 jit_solution(8208694642911210586)
XLA Ops:
  0.0 0.0 slice-start
  0.0 0.0 slice-start.2
  0.0 3.6 %shard_map.46.own_ref = f32[2,3200]{1,0:T(2,128)S(1)} custom-call(bf16[2,2048]{1,0:T(2,128)(2,1)} %bitcast.5, bf16[1024,2048]{1,0:T(8,128)(2,1)} %tokens_hbm.1), custom_call_target="tpu_custom_call" | custom-call | tf_op jit(solution)/shard_map/pallas_call | solution.py:127
  3.6 0.0 slice-start.1
  3.6 0.0 slice-start.3
  3.6 0.5 %collective-permute-start = (f32[2,3200]{1,0:T(2,128)S(1)}, f32[2,3200]{1,0:T(2,128)S(1)}, u32[]{:S(2)}, u32[]{:S(2)}) collective-permute-start(f32[2,3200]{1,0:T(2,128)S(1)} %shard_map.46.own_ref), channel_id=1, source_target_pairs={{0,16},{16,0},{1,17},{17,1},{2,18},{18,2},{3,19},{19,3},{4,20},{20... | collective-permute-start | bytes 76808 | tf_op jit(solution)/shard_map/ppermute | solution.py:274
  4.1 0.9 %collective-permute-done.other_ref = f32[2,3200]{1,0:T(2,128)S(1)} collective-permute-done((f32[2,3200]{1,0:T(2,128)S(1)}, f32[2,3200]{1,0:T(2,128)S(1)}, u32[]{:S(2)}, u32[]{:S(2)}) %collective-permute-start) | collective-permute-done | bytes 25632 | tf_op jit(solution)/shard_map/ppermute | solution.py:274
  5.0 3.8 %collective-permute-start.3 = (bf16[4,2176]{1,0:T(4,128)(2,1)S(1)}, bf16[4,2176]{1,0:T(4,128)(2,1)S(1)}, u32[]{:S(2)}, u32[]{:S(2)}) collective-permute-start(bf16[4,2176]{1,0:T(4,128)(2,1)S(1)} %get-tuple-element.11), channel_id=1, source_target_pairs={{0,24},{1,25},{2,26},{3,27},{4,28},{5,29},{6,30},{7,31},{8,20},{9,... | collective-permute-start | bytes 52232 | tf_op jit(solution)/shard_map/ppermute | solution.py:51
  8.8 1.1 %collective-permute-start.2 = (bf16[4,2176]{1,0:T(4,128)(2,1)S(1)}, bf16[4,2176]{1,0:T(4,128)(2,1)S(1)}, u32[]{:S(2)}, u32[]{:S(2)}) collective-permute-start(bf16[4,2176]{1,0:T(4,128)(2,1)S(1)} %get-tuple-element.11), channel_id=1, source_target_pairs={{0,28},{1,29},{2,30},{3,31},{4,24},{5,25},{6,26},{7,27},{8,16},{9,... | collective-permute-start | bytes 52232 | tf_op jit(solution)/shard_map/ppermute | solution.py:51
  9.8 0.5 %collective-permute-start.1 = (bf16[4,2176]{1,0:T(4,128)(2,1)S(1)}, bf16[4,2176]{1,0:T(4,128)(2,1)S(1)}, u32[]{:S(2)}, u32[]{:S(2)}) collective-permute-start(bf16[4,2176]{1,0:T(4,128)(2,1)S(1)} %get-tuple-element.11), channel_id=1, source_target_pairs={{0,20},{1,21},{2,22},{3,23},{4,16},{5,17},{6,18},{7,19},{8,28},{9,... | collective-permute-start | bytes 52232 | tf_op jit(solution)/shard_map/ppermute | solution.py:51
  10.3 0.9 %collective-permute-done.3.refs_2_ = bf16[4,2176]{1,0:T(4,128)(2,1)S(1)} collective-permute-done((bf16[4,2176]{1,0:T(4,128)(2,1)S(1)}, bf16[4,2176]{1,0:T(4,128)(2,1)S(1)}, u32[]{:S(2)}, u32[]{:S(2)}) %collective-permute-start.3) | collective-permute-done | bytes 17440 | tf_op jit(solution)/shard_map/ppermute | solution.py:51
  11.2 1.6 %collective-permute-done.2.refs_1_ = bf16[4,2176]{1,0:T(4,128)(2,1)S(1)} collective-permute-done((bf16[4,2176]{1,0:T(4,128)(2,1)S(1)}, bf16[4,2176]{1,0:T(4,128)(2,1)S(1)}, u32[]{:S(2)}, u32[]{:S(2)}) %collective-permute-start.2) | collective-permute-done | bytes 17440 | tf_op jit(solution)/shard_map/ppermute | solution.py:51
  12.8 0.2 collective-permute-done.1.refs_0_
  13.0 0.0 slice-done
  13.0 0.0 slice-done.2
  13.0 0.0 slice-done.1
  13.0 0.0 slice-done.3
  13.1 2.5 %shard_map.48 = f32[4,2048]{1,0:T(4,128)S(1)} custom-call(f32[4,2176]{1,0:T(4,128)S(1)} %get-tuple-element.10.both_ref, bf16[4,2176]{1,0:T(4,128)(2,1)S(1)} %collective-permute-done.1.refs_0_, bf16[4,2176]{1,0:T(4,128)(2,1)S(1)} %collective-permute-done.2.refs_1_, bf16[4,2176]{1,0:T(4,128)(2,1)S(1)} %collective-permute-done.3.refs_2_, ...), custom_call_target="tpu_custom_call" | custom-call | tf_op jit(solution)/shard_map/pallas_call | solution.py:198
  15.6 0.4 %collective-permute-start.4 = (f32[4,2048]{1,0:T(4,128)S(1)}, f32[4,2048]{1,0:T(4,128)S(1)}, u32[]{:S(2)}, u32[]{:S(2)}) collective-permute-start(f32[4,2048]{1,0:T(4,128)S(1)} %shard_map.48), channel_id=1, source_target_pairs={{0,16},{16,0},{1,17},{17,1},{2,18},{18,2},{3,19},{19,3},{4,20},{20... | collective-permute-start | bytes 98312 | tf_op jit(solution)/shard_map/ppermute | solution.py:279
  15.9 0.9 %collective-permute-done.4 = f32[4,2048]{1,0:T(4,128)S(1)} collective-permute-done((f32[4,2048]{1,0:T(4,128)S(1)}, f32[4,2048]{1,0:T(4,128)S(1)}, u32[]{:S(2)}, u32[]{:S(2)}) %collective-permute-start.4) | collective-permute-done | bytes 32800 | tf_op jit(solution)/shard_map/ppermute | solution.py:279
  16.8 1.5 %collective-permute-start.7 = (bf16[4,2048]{1,0:T(4,128)(2,1)S(1)}, bf16[4,2048]{1,0:T(4,128)(2,1)S(1)}, u32[]{:S(2)}, u32[]{:S(2)}) collective-permute-start(bf16[4,2048]{1,0:T(4,128)(2,1)S(1)} %get-tuple-element.15), channel_id=1, source_target_pairs={{0,20},{1,21},{2,22},{3,23},{4,24},{5,25},{6,26},{7,27},{8,28},{9,... | collective-permute-start | bytes 49160 | tf_op jit(solution)/shard_map/ppermute | solution.py:51
  18.3 1.7 %collective-permute-start.6 = (bf16[4,2048]{1,0:T(4,128)(2,1)S(1)}, bf16[4,2048]{1,0:T(4,128)(2,1)S(1)}, u32[]{:S(2)}, u32[]{:S(2)}) collective-permute-start(bf16[4,2048]{1,0:T(4,128)(2,1)S(1)} %get-tuple-element.15), channel_id=1, source_target_pairs={{0,24},{1,25},{2,26},{3,27},{4,28},{5,29},{6,30},{7,31},{8,16},{9,... | collective-permute-start | bytes 49160 | tf_op jit(solution)/shard_map/ppermute | solution.py:51
  20.0 1.2 %collective-permute-start.5 = (bf16[4,2048]{1,0:T(4,128)(2,1)S(1)}, bf16[4,2048]{1,0:T(4,128)(2,1)S(1)}, u32[]{:S(2)}, u32[]{:S(2)}) collective-permute-start(bf16[4,2048]{1,0:T(4,128)(2,1)S(1)} %get-tuple-element.15), channel_id=1, source_target_pairs={{0,28},{1,29},{2,30},{3,31},{4,16},{5,17},{6,18},{7,19},{8,20},{9,... | collective-permute-start | bytes 49160 | tf_op jit(solution)/shard_map/ppermute | solution.py:51
  21.1 0.7 %collective-permute-done.7.refs_2_ = bf16[4,2048]{1,0:T(4,128)(2,1)S(1)} collective-permute-done((bf16[4,2048]{1,0:T(4,128)(2,1)S(1)}, bf16[4,2048]{1,0:T(4,128)(2,1)S(1)}, u32[]{:S(2)}, u32[]{:S(2)}) %collective-permute-start.7) | collective-permute-done | bytes 16416 | tf_op jit(solution)/shard_map/ppermute | solution.py:51
  21.8 0.9 %collective-permute-done.6.refs_1_ = bf16[4,2048]{1,0:T(4,128)(2,1)S(1)} collective-permute-done((bf16[4,2048]{1,0:T(4,128)(2,1)S(1)}, bf16[4,2048]{1,0:T(4,128)(2,1)S(1)}, u32[]{:S(2)}, u32[]{:S(2)}) %collective-permute-start.6) | collective-permute-done | bytes 16416 | tf_op jit(solution)/shard_map/ppermute | solution.py:51
  22.8 0.4 %collective-permute-done.5.refs_0_ = bf16[4,2048]{1,0:T(4,128)(2,1)S(1)} collective-permute-done((bf16[4,2048]{1,0:T(4,128)(2,1)S(1)}, bf16[4,2048]{1,0:T(4,128)(2,1)S(1)}, u32[]{:S(2)}, u32[]{:S(2)}) %collective-permute-start.5) | collective-permute-done | bytes 16416 | tf_op jit(solution)/shard_map/ppermute | solution.py:51
  23.2 2.3 %collective-permute-start.10 = (f32[2,3072]{1,0:T(2,128)S(1)}, f32[2,3072]{1,0:T(2,128)S(1)}, u32[]{:S(2)}, u32[]{:S(2)}) collective-permute-start(f32[2,3072]{1,0:T(2,128)S(1)} %get-tuple-element.14), channel_id=1, source_target_pairs={{0,19},{1,18},{2,17},{3,16},{4,23},{5,22},{6,21},{7,20},{8,27},{9,... | collective-permute-start | bytes 73736 | tf_op jit(solution)/shard_map/ppermute | solution.py:51
  25.5 0.5 %collective-permute-start.9 = (f32[2,3072]{1,0:T(2,128)S(1)}, f32[2,3072]{1,0:T(2,128)S(1)}, u32[]{:S(2)}, u32[]{:S(2)}) collective-permute-start(f32[2,3072]{1,0:T(2,128)S(1)} %get-tuple-element.14), channel_id=1, source_target_pairs={{0,17},{1,16},{2,19},{3,18},{4,21},{5,20},{6,23},{7,22},{8,25},{9,... | collective-permute-start | bytes 73736 | tf_op jit(solution)/shard_map/ppermute | solution.py:51
  25.9 0.3 collective-permute-start.8
  26.2 1.2 %collective-permute-done.10.refs_3_ = f32[2,3072]{1,0:T(2,128)S(1)} collective-permute-done((f32[2,3072]{1,0:T(2,128)S(1)}, f32[2,3072]{1,0:T(2,128)S(1)}, u32[]{:S(2)}, u32[]{:S(2)}) %collective-permute-start.10) | collective-permute-done | bytes 24608 | tf_op jit(solution)/shard_map/ppermute | solution.py:51
  27.4 1.3 %collective-permute-done.9.refs_2_ = f32[2,3072]{1,0:T(2,128)S(1)} collective-permute-done((f32[2,3072]{1,0:T(2,128)S(1)}, f32[2,3072]{1,0:T(2,128)S(1)}, u32[]{:S(2)}, u32[]{:S(2)}) %collective-permute-start.9) | collective-permute-done | bytes 24608 | tf_op jit(solution)/shard_map/ppermute | solution.py:51
  28.7 0.5 %collective-permute-done.8.refs_1_ = f32[2,3072]{1,0:T(2,128)S(1)} collective-permute-done((f32[2,3072]{1,0:T(2,128)S(1)}, f32[2,3072]{1,0:T(2,128)S(1)}, u32[]{:S(2)}, u32[]{:S(2)}) %collective-permute-start.8) | collective-permute-done | bytes 24608 | tf_op jit(solution)/shard_map/ppermute | solution.py:51
  29.2 1.3 %shard_map.50 = bf16[256,2048]{1,0:T(8,128)(2,1)} custom-call(f32[2,3072]{1,0:T(2,128)S(1)} %get-tuple-element.13.refs_0_, f32[2,3072]{1,0:T(2,128)S(1)} %collective-permute-done.8.refs_1_, f32[2,3072]{1,0:T(2,128)S(1)} %collective-permute-done.9.refs_2_, f32[2,3072]{1,0:T(2,128)S(1)} %collective-permute-done.10.refs_3_), custom_call_target="tpu_custom_call" | custom-call | tf_op jit(solution)/shard_map/pallas_call | solution.py:259
  (6 shorter events, 0.1 us)
Async XLA Ops:
  0.0 13.0 %slice-start = ((s8[8388608]{0:T(1024)(128)(4,1)}), s8[4194304]{0:T(1024)(128)(4,1)S(1)}, s32[]{:S(2)}) async-start(s8[8388608]{0:T(1024)(128)(4,1)} %bitcast.1), calls=%async_computation | async-start | bytes 8388608
  0.0 13.0 %slice-start.2 = ((s8[8388608]{0:T(1024)(128)(4,1)}), s8[4194304]{0:T(1024)(128)(4,1)S(1)}, s32[]{:S(2)}) async-start(s8[8388608]{0:T(1024)(128)(4,1)} %bitcast.3), calls=%async_computation.2 | async-start | bytes 8388608
  3.6 9.5 %slice-start.1 = ((s8[8388608]{0:T(1024)(128)(4,1)}), s8[4194304]{0:T(1024)(128)(4,1)S(1)}, s32[]{:S(2)}) async-start(s8[8388608]{0:T(1024)(128)(4,1)} %bitcast.1), calls=%async_computation.1 | async-start | bytes 8388608
  3.6 9.4 %slice-start.3 = ((s8[8388608]{0:T(1024)(128)(4,1)}), s8[4194304]{0:T(1024)(128)(4,1)S(1)}, s32[]{:S(2)}) async-start(s8[8388608]{0:T(1024)(128)(4,1)} %bitcast.3), calls=%async_computation.3 | async-start | bytes 8388608
  3.6 1.4 %collective-permute-start = (f32[2,3200]{1,0:T(2,128)S(1)}, f32[2,3200]{1,0:T(2,128)S(1)}, u32[]{:S(2)}, u32[]{:S(2)}) collective-permute-start(f32[2,3200]{1,0:T(2,128)S(1)} %shard_map.46.own_ref), channel_id=1, source_target_pairs={{0,16},{16,0},{1,17},{17,1},{2,18},{18,2},{3,19},{19,3},{4,20},{20... | collective-permute-start | bytes 76808 | tf_op jit(solution)/shard_map/ppermute | solution.py:274
  5.0 6.2 %collective-permute-start.3 = (bf16[4,2176]{1,0:T(4,128)(2,1)S(1)}, bf16[4,2176]{1,0:T(4,128)(2,1)S(1)}, u32[]{:S(2)}, u32[]{:S(2)}) collective-permute-start(bf16[4,2176]{1,0:T(4,128)(2,1)S(1)} %get-tuple-element.11), channel_id=1, source_target_pairs={{0,24},{1,25},{2,26},{3,27},{4,28},{5,29},{6,30},{7,31},{8,20},{9,... | collective-permute-start | bytes 52232 | tf_op jit(solution)/shard_map/ppermute | solution.py:51
  8.8 4.1 %collective-permute-start.2 = (bf16[4,2176]{1,0:T(4,128)(2,1)S(1)}, bf16[4,2176]{1,0:T(4,128)(2,1)S(1)}, u32[]{:S(2)}, u32[]{:S(2)}) collective-permute-start(bf16[4,2176]{1,0:T(4,128)(2,1)S(1)} %get-tuple-element.11), channel_id=1, source_target_pairs={{0,28},{1,29},{2,30},{3,31},{4,24},{5,25},{6,26},{7,27},{8,16},{9,... | collective-permute-start | bytes 52232 | tf_op jit(solution)/shard_map/ppermute | solution.py:51
  9.8 3.2 %collective-permute-start.1 = (bf16[4,2176]{1,0:T(4,128)(2,1)S(1)}, bf16[4,2176]{1,0:T(4,128)(2,1)S(1)}, u32[]{:S(2)}, u32[]{:S(2)}) collective-permute-start(bf16[4,2176]{1,0:T(4,128)(2,1)S(1)} %get-tuple-element.11), channel_id=1, source_target_pairs={{0,20},{1,21},{2,22},{3,23},{4,16},{5,17},{6,18},{7,19},{8,28},{9,... | collective-permute-start | bytes 52232 | tf_op jit(solution)/shard_map/ppermute | solution.py:51
  15.6 1.2 %collective-permute-start.4 = (f32[4,2048]{1,0:T(4,128)S(1)}, f32[4,2048]{1,0:T(4,128)S(1)}, u32[]{:S(2)}, u32[]{:S(2)}) collective-permute-start(f32[4,2048]{1,0:T(4,128)S(1)} %shard_map.48), channel_id=1, source_target_pairs={{0,16},{16,0},{1,17},{17,1},{2,18},{18,2},{3,19},{19,3},{4,20},{20... | collective-permute-start | bytes 98312 | tf_op jit(solution)/shard_map/ppermute | solution.py:279
  16.8 5.0 %collective-permute-start.7 = (bf16[4,2048]{1,0:T(4,128)(2,1)S(1)}, bf16[4,2048]{1,0:T(4,128)(2,1)S(1)}, u32[]{:S(2)}, u32[]{:S(2)}) collective-permute-start(bf16[4,2048]{1,0:T(4,128)(2,1)S(1)} %get-tuple-element.15), channel_id=1, source_target_pairs={{0,20},{1,21},{2,22},{3,23},{4,24},{5,25},{6,26},{7,27},{8,28},{9,... | collective-permute-start | bytes 49160 | tf_op jit(solution)/shard_map/ppermute | solution.py:51
  18.3 4.5 %collective-permute-start.6 = (bf16[4,2048]{1,0:T(4,128)(2,1)S(1)}, bf16[4,2048]{1,0:T(4,128)(2,1)S(1)}, u32[]{:S(2)}, u32[]{:S(2)}) collective-permute-start(bf16[4,2048]{1,0:T(4,128)(2,1)S(1)} %get-tuple-element.15), channel_id=1, source_target_pairs={{0,24},{1,25},{2,26},{3,27},{4,28},{5,29},{6,30},{7,31},{8,16},{9,... | collective-permute-start | bytes 49160 | tf_op jit(solution)/shard_map/ppermute | solution.py:51
  20.0 3.2 %collective-permute-start.5 = (bf16[4,2048]{1,0:T(4,128)(2,1)S(1)}, bf16[4,2048]{1,0:T(4,128)(2,1)S(1)}, u32[]{:S(2)}, u32[]{:S(2)}) collective-permute-start(bf16[4,2048]{1,0:T(4,128)(2,1)S(1)} %get-tuple-element.15), channel_id=1, source_target_pairs={{0,28},{1,29},{2,30},{3,31},{4,16},{5,17},{6,18},{7,19},{8,20},{9,... | collective-permute-start | bytes 49160 | tf_op jit(solution)/shard_map/ppermute | solution.py:51
  23.2 4.2 %collective-permute-start.10 = (f32[2,3072]{1,0:T(2,128)S(1)}, f32[2,3072]{1,0:T(2,128)S(1)}, u32[]{:S(2)}, u32[]{:S(2)}) collective-permute-start(f32[2,3072]{1,0:T(2,128)S(1)} %get-tuple-element.14), channel_id=1, source_target_pairs={{0,19},{1,18},{2,17},{3,16},{4,23},{5,22},{6,21},{7,20},{8,27},{9,... | collective-permute-start | bytes 73736 | tf_op jit(solution)/shard_map/ppermute | solution.py:51
  25.5 3.3 %collective-permute-start.9 = (f32[2,3072]{1,0:T(2,128)S(1)}, f32[2,3072]{1,0:T(2,128)S(1)}, u32[]{:S(2)}, u32[]{:S(2)}) collective-permute-start(f32[2,3072]{1,0:T(2,128)S(1)} %get-tuple-element.14), channel_id=1, source_target_pairs={{0,17},{1,16},{2,19},{3,18},{4,21},{5,20},{6,23},{7,22},{8,25},{9,... | collective-permute-start | bytes 73736 | tf_op jit(solution)/shard_map/ppermute | solution.py:51
  25.9 3.3 %collective-permute-start.8 = (f32[2,3072]{1,0:T(2,128)S(1)}, f32[2,3072]{1,0:T(2,128)S(1)}, u32[]{:S(2)}, u32[]{:S(2)}) collective-permute-start(f32[2,3072]{1,0:T(2,128)S(1)} %get-tuple-element.14), channel_id=1, source_target_pairs={{0,18},{1,19},{2,16},{3,17},{4,22},{5,23},{6,20},{7,21},{8,26},{9,... | collective-permute-start | bytes 73736 | tf_op jit(solution)/shard_map/ppermute | solution.py:51

commit v7 on v6

--- a/solution.py
+++ b/solution.py
@@ -51,14 +51,19 @@
     return lax.ppermute(x, ("dp", "seq", "expert"), pairs)
 
 
+def pieces(x):
+    found = []
+    for _ in range(3):
+        found.append(x.astype(BF16).astype(F32))
+        x = x - found[-1]
+    return found
+
+
 def scalars(top, total):
     lane = lax.broadcasted_iota(jnp.int32, (top.shape[0], LANES), 1)
     lanes = jnp.zeros(lane.shape, F32)
-    for at, rest in ((0, top), (3, total)):
-        for i in range(3):
-            piece = rest.astype(BF16).astype(F32)
-            lanes = jnp.where(lane == at + i, piece, lanes)
-            rest = rest - piece
+    for i, piece in enumerate(pieces(top) + pieces(total)):
+        lanes = jnp.where(lane == i, piece, lanes)
     return lanes
 
 
@@ -204,39 +209,53 @@
     )(both, *received, w_in, w_out)
 
 
-def pack_kernel(chip_ref, *refs):
-    *received, logits_ref, own_ref, other_ref = refs
+def pack_kernel(places, chip_ref, *refs):
+    received, (logits_ref, own_ref, *out_refs) = refs[: -len(places) - 2], refs[-len(places) - 2 :]
     slots, width = own_ref.shape[0], chip_ref.shape[1]
+    rows, group = own_ref.shape[1] - width, lax.axis_index("expert")
     total = chip_ref[...]
     for r in received:
         total += swapped(r[...].astype(F32))
-    total = total.astype(BF16).astype(F32)
-    for out_ref, part in ((own_ref, slice(0, slots)), (other_ref, slice(slots, 2 * slots))):
-        out_ref[:, :width] = total[part]
-        out_ref[:, width:] = logits_ref[part, :]
-
-
-def pack(chip, received, logits):
-    slots, width = chip.shape
-    shape = jax.ShapeDtypeStruct((slots // 2, width + logits.shape[1]), F32)
-    return pl.pallas_call(
-        pack_kernel,
-        out_shape=(shape, shape),
+
+    def chosen(part, to):
+        logits = logits_ref[part, to[0] * rows : (to[0] + 1) * rows]
+        for g in range(1, len(to)):
+            here = logits_ref[part, to[g] * rows : (to[g] + 1) * rows]
+            logits = jnp.where(group == g, here, logits)
+        return logits
+
+    own, other = slice(0, slots), slice(slots, 2 * slots)
+    own_ref[:, :width] = total[own]
+    own_ref[:, width:] = chosen(own, range(len(places) + 1))
+    for out_ref, pairs in zip(out_refs, places):
+        logits = pieces(chosen(other, dict(pairs)))
+        out_ref[...] = jnp.concatenate([total[other]] + logits, axis=1).astype(BF16)
+
+
+def pack(chip, received, logits, places):
+    slots, width = chip.shape[0] // 2, chip.shape[1]
+    rows = logits.shape[1] // (len(places) + 1)
+    sent = jax.ShapeDtypeStruct((slots, width + 3 * rows), BF16)
+    return pl.pallas_call(
+        functools.partial(pack_kernel, places),
+        out_shape=[jax.ShapeDtypeStruct((slots, width + rows), F32)] + [sent] * len(places),
         in_specs=[VMEM] * (len(received) + 2),
-        out_specs=(VMEM, VMEM),
+        out_specs=[VMEM] * (len(places) + 1),
         compiler_params=params(4),
     )(chip, *received, logits)
 
 
-def mix_kernel(chunks, *refs):
-    *packed, out_hbm, rows_ref, sems = refs
-    (count, width), group = rows_ref.shape, lax.axis_index("expert")
+def mix_kernel(chunks, own_ref, *refs):
+    *received, out_hbm, rows_ref, sems = refs
+    count, width = rows_ref.shape
     rows = count // chunks
-    values = jnp.concatenate([p[:, :width] for p in packed], axis=0).astype(BF16)
-    everything = jnp.concatenate([p[:, width:] for p in packed], axis=0)
-    logits = everything[:, :count]
-    for g in range(1, len(packed)):
-        logits = jnp.where(group == g, everything[:, g * count : (g + 1) * count], logits)
+    values, logits = [own_ref[:, :width]], [own_ref[:, width:]]
+    for r in received:
+        part = r[...].astype(F32)
+        values.append(part[:, :width])
+        logits.append(sum(part[:, width + i * count : width + (i + 1) * count] for i in range(3)))
+    values = jnp.concatenate(values, axis=0).astype(BF16)
+    logits = jnp.concatenate(logits, axis=0)
     weight = jnp.exp(logits - jnp.max(logits, axis=0, keepdims=True))
     weight = (weight / jnp.sum(weight, axis=0, keepdims=True)).astype(BF16)
     copies = []
@@ -254,16 +273,16 @@
         copy.wait()
 
 
-def mix(packed, width, chunks=4):
-    shape = ((packed[0].shape[1] - width) // len(packed), width)
+def mix(own, received, width, chunks=4):
+    shape = (own.shape[1] - width, width)
     return pl.pallas_call(
         functools.partial(mix_kernel, chunks),
         out_shape=jax.ShapeDtypeStruct(shape, BF16),
-        in_specs=[VMEM] * len(packed),
+        in_specs=[VMEM] * (len(received) + 1),
         out_specs=pl.BlockSpec(memory_space=pl.ANY),
         scratch_shapes=[pltpu.VMEM(shape, BF16), pltpu.SemaphoreType.DMA((chunks,))],
         compiler_params=params(8),
-    )(*packed)
+    )(own, *received)
 
 
 def on_device(sizes, tokens, phi, w_in, w_out):
@@ -281,10 +300,11 @@
     sums = [
         exchange(sent, sizes, "seq", around(range(seqs), step)) for step in range(seqs - 1, 0, -1)
     ]
-    own, other = pack(chip, sums, logits)
-    order = sorted(range(1, groups), key=lambda step: (step != groups // 2, step))
-    everyone = [own] + [exchange(other, sizes, "expert", partners(groups, step)) for step in order]
-    return mix(everyone, width)
+    order = [groups - 1, *range(1, groups - 1)]
+    places = [partners(groups, step) for step in order]
+    own, *others = pack(chip, sums, logits, places)
+    everyone = [exchange(x, sizes, "expert", moves) for x, moves in zip(others, places)]
+    return mix(own, everyone, width)
 
 
 def solution(mesh):

time: 30.6 us -> 30.5 us (level)
  no operation moved by 1% of the time
where the time goes in v7:
time: 30.5 us; the launch traced here: 30.4 us
  starting transfers between devices  13.5 us (44%)
  waiting for transfers between devices  9.26 us (30%)
  Pallas kernels  7.43 us (24%)
    ppermute x9, starting transfers between devices, exchange(): return lax.ppermute(x, ('dp', 'seq', 'expert'), pairs)  12.7 us
    ppermute x9, waiting for transfers between devices, exchange(): return lax.ppermute(x, ('dp', 'seq', 'expert'), pairs)  7.55 us
    pallas_call x1, Pallas kernels, slot_sums(): pl.pallas_call(functools.partial(slot_sums_kernel, chunks), out_shape=jax...  3.55 us
    pallas_call x1, Pallas kernels, experts(): pl.pallas_call(experts_kernel, out_shape=jax.ShapeDtypeStruct((both.shape...  2.51 us
    pallas_call x1, Pallas kernels, mix(): pl.pallas_call(functools.partial(mix_kernel, chunks), out_shape=jax.Shape...  1.29 us
    ppermute x1, waiting for transfers between devices, on_device(): chip = partial + swapped(lax.ppermute(partial, 'dp', swap))  0.86 us
    ppermute x1, waiting for transfers between devices, on_device(): lax.ppermute(packed, 'dp', swap)  0.85 us
  transfers between devices with their start and end apart: 11, of which 11 were waited for; matrix products, arithmetic and copies ran while one was open for 0% of the time, Pallas kernels for 0%

profile of v7, /device:TPU:0, one launch (start us, length us, event | category | flops | bytes accessed | tf_op | source)
XLA Modules:
  0.0 30.4 jit_solution(6362928508344321429)
XLA Ops:
  0.0 0.0 slice-start
  0.0 0.0 slice-start.2
  0.0 3.6 %shard_map.46.own_ref = f32[2,3200]{1,0:T(2,128)S(1)} custom-call(bf16[2,2048]{1,0:T(2,128)(2,1)} %bitcast.5, bf16[1024,2048]{1,0:T(8,128)(2,1)} %tokens_hbm.1), custom_call_target="tpu_custom_call" | custom-call | tf_op jit(solution)/shard_map/pallas_call | solution.py:132
  3.6 0.0 slice-start.1
  3.6 0.0 slice-start.3
  3.6 0.5 %collective-permute-start = (f32[2,3200]{1,0:T(2,128)S(1)}, f32[2,3200]{1,0:T(2,128)S(1)}, u32[]{:S(2)}, u32[]{:S(2)}) collective-permute-start(f32[2,3200]{1,0:T(2,128)S(1)} %shard_map.46.own_ref), channel_id=1, source_target_pairs={{0,16},{16,0},{1,17},{17,1},{2,18},{18,2},{3,19},{19,3},{4,20},{20... | collective-permute-start | bytes 76808 | tf_op jit(solution)/shard_map/ppermute | solution.py:293
  4.1 0.9 %collective-permute-done.other_ref = f32[2,3200]{1,0:T(2,128)S(1)} collective-permute-done((f32[2,3200]{1,0:T(2,128)S(1)}, f32[2,3200]{1,0:T(2,128)S(1)}, u32[]{:S(2)}, u32[]{:S(2)}) %collective-permute-start) | collective-permute-done | bytes 25632 | tf_op jit(solution)/shard_map/ppermute | solution.py:293
  5.0 3.8 %collective-permute-start.3 = (bf16[4,2176]{1,0:T(4,128)(2,1)S(1)}, bf16[4,2176]{1,0:T(4,128)(2,1)S(1)}, u32[]{:S(2)}, u32[]{:S(2)}) collective-permute-start(bf16[4,2176]{1,0:T(4,128)(2,1)S(1)} %get-tuple-element.13), channel_id=1, source_target_pairs={{0,24},{1,25},{2,26},{3,27},{4,28},{5,29},{6,30},{7,31},{8,20},{9,... | collective-permute-start | bytes 52232 | tf_op jit(solution)/shard_map/ppermute | solution.py:51
  8.8 1.1 %collective-permute-start.2 = (bf16[4,2176]{1,0:T(4,128)(2,1)S(1)}, bf16[4,2176]{1,0:T(4,128)(2,1)S(1)}, u32[]{:S(2)}, u32[]{:S(2)}) collective-permute-start(bf16[4,2176]{1,0:T(4,128)(2,1)S(1)} %get-tuple-element.13), channel_id=1, source_target_pairs={{0,28},{1,29},{2,30},{3,31},{4,24},{5,25},{6,26},{7,27},{8,16},{9,... | collective-permute-start | bytes 52232 | tf_op jit(solution)/shard_map/ppermute | solution.py:51
  9.8 0.5 %collective-permute-start.1 = (bf16[4,2176]{1,0:T(4,128)(2,1)S(1)}, bf16[4,2176]{1,0:T(4,128)(2,1)S(1)}, u32[]{:S(2)}, u32[]{:S(2)}) collective-permute-start(bf16[4,2176]{1,0:T(4,128)(2,1)S(1)} %get-tuple-element.13), channel_id=1, source_target_pairs={{0,20},{1,21},{2,22},{3,23},{4,16},{5,17},{6,18},{7,19},{8,28},{9,... | collective-permute-start | bytes 52232 | tf_op jit(solution)/shard_map/ppermute | solution.py:51
  10.3 0.9 %collective-permute-done.3.refs_2_ = bf16[4,2176]{1,0:T(4,128)(2,1)S(1)} collective-permute-done((bf16[4,2176]{1,0:T(4,128)(2,1)S(1)}, bf16[4,2176]{1,0:T(4,128)(2,1)S(1)}, u32[]{:S(2)}, u32[]{:S(2)}) %collective-permute-start.3) | collective-permute-done | bytes 17440 | tf_op jit(solution)/shard_map/ppermute | solution.py:51
  11.2 1.6 %collective-permute-done.2.refs_1_ = bf16[4,2176]{1,0:T(4,128)(2,1)S(1)} collective-permute-done((bf16[4,2176]{1,0:T(4,128)(2,1)S(1)}, bf16[4,2176]{1,0:T(4,128)(2,1)S(1)}, u32[]{:S(2)}, u32[]{:S(2)}) %collective-permute-start.2) | collective-permute-done | bytes 17440 | tf_op jit(solution)/shard_map/ppermute | solution.py:51
  12.8 0.2 collective-permute-done.1.refs_0_
  13.0 0.0 slice-done
  13.0 0.0 slice-done.2
  13.0 0.0 slice-done.1
  13.0 0.0 slice-done.3
  13.1 2.5 %shard_map.48 = f32[4,2048]{1,0:T(4,128)S(1)} custom-call(f32[4,2176]{1,0:T(4,128)S(1)} %get-tuple-element.12.both_ref, bf16[4,2176]{1,0:T(4,128)(2,1)S(1)} %collective-permute-done.1.refs_0_, bf16[4,2176]{1,0:T(4,128)(2,1)S(1)} %collective-permute-done.2.refs_1_, bf16[4,2176]{1,0:T(4,128)(2,1)S(1)} %collective-permute-done.3.refs_2_, ...), custom_call_target="tpu_custom_call" | custom-call | tf_op jit(solution)/shard_map/pallas_call | solution.py:203
  15.6 0.4 %collective-permute-start.4 = (f32[4,2048]{1,0:T(4,128)S(1)}, f32[4,2048]{1,0:T(4,128)S(1)}, u32[]{:S(2)}, u32[]{:S(2)}) collective-permute-start(f32[4,2048]{1,0:T(4,128)S(1)} %shard_map.48), channel_id=1, source_target_pairs={{0,16},{16,0},{1,17},{17,1},{2,18},{18,2},{3,19},{19,3},{4,20},{20... | collective-permute-start | bytes 98312 | tf_op jit(solution)/shard_map/ppermute | solution.py:298
  15.9 0.9 %collective-permute-done.4 = f32[4,2048]{1,0:T(4,128)S(1)} collective-permute-done((f32[4,2048]{1,0:T(4,128)S(1)}, f32[4,2048]{1,0:T(4,128)S(1)}, u32[]{:S(2)}, u32[]{:S(2)}) %collective-permute-start.4) | collective-permute-done | bytes 32800 | tf_op jit(solution)/shard_map/ppermute | solution.py:298
  16.8 1.5 %collective-permute-start.7 = (bf16[4,2048]{1,0:T(4,128)(2,1)S(1)}, bf16[4,2048]{1,0:T(4,128)(2,1)S(1)}, u32[]{:S(2)}, u32[]{:S(2)}) collective-permute-start(bf16[4,2048]{1,0:T(4,128)(2,1)S(1)} %get-tuple-element.19), channel_id=1, source_target_pairs={{0,20},{1,21},{2,22},{3,23},{4,24},{5,25},{6,26},{7,27},{8,28},{9,... | collective-permute-start | bytes 49160 | tf_op jit(solution)/shard_map/ppermute | solution.py:51
  18.3 1.7 %collective-permute-start.6 = (bf16[4,2048]{1,0:T(4,128)(2,1)S(1)}, bf16[4,2048]{1,0:T(4,128)(2,1)S(1)}, u32[]{:S(2)}, u32[]{:S(2)}) collective-permute-start(bf16[4,2048]{1,0:T(4,128)(2,1)S(1)} %get-tuple-element.19), channel_id=1, source_target_pairs={{0,24},{1,25},{2,26},{3,27},{4,28},{5,29},{6,30},{7,31},{8,16},{9,... | collective-permute-start | bytes 49160 | tf_op jit(solution)/shard_map/ppermute | solution.py:51
  20.0 1.2 %collective-permute-start.5 = (bf16[4,2048]{1,0:T(4,128)(2,1)S(1)}, bf16[4,2048]{1,0:T(4,128)(2,1)S(1)}, u32[]{:S(2)}, u32[]{:S(2)}) collective-permute-start(bf16[4,2048]{1,0:T(4,128)(2,1)S(1)} %get-tuple-element.19), channel_id=1, source_target_pairs={{0,28},{1,29},{2,30},{3,31},{4,16},{5,17},{6,18},{7,19},{8,20},{9,... | collective-permute-start | bytes 49160 | tf_op jit(solution)/shard_map/ppermute | solution.py:51
  21.1 0.7 %collective-permute-done.7.refs_2_ = bf16[4,2048]{1,0:T(4,128)(2,1)S(1)} collective-permute-done((bf16[4,2048]{1,0:T(4,128)(2,1)S(1)}, bf16[4,2048]{1,0:T(4,128)(2,1)S(1)}, u32[]{:S(2)}, u32[]{:S(2)}) %collective-permute-start.7) | collective-permute-done | bytes 16416 | tf_op jit(solution)/shard_map/ppermute | solution.py:51
  21.8 0.9 %collective-permute-done.6.refs_1_ = bf16[4,2048]{1,0:T(4,128)(2,1)S(1)} collective-permute-done((bf16[4,2048]{1,0:T(4,128)(2,1)S(1)}, bf16[4,2048]{1,0:T(4,128)(2,1)S(1)}, u32[]{:S(2)}, u32[]{:S(2)}) %collective-permute-start.6) | collective-permute-done | bytes 16416 | tf_op jit(solution)/shard_map/ppermute | solution.py:51
  22.8 0.4 %collective-permute-done.5.refs_0_ = bf16[4,2048]{1,0:T(4,128)(2,1)S(1)} collective-permute-done((bf16[4,2048]{1,0:T(4,128)(2,1)S(1)}, bf16[4,2048]{1,0:T(4,128)(2,1)S(1)}, u32[]{:S(2)}, u32[]{:S(2)}) %collective-permute-start.5) | collective-permute-done | bytes 16416 | tf_op jit(solution)/shard_map/ppermute | solution.py:51
  23.1 0.1 shard_map.49
  23.2 2.3 %collective-permute-start.8 = (bf16[2,2816]{1,0:T(2,128)(2,1)S(1)}, bf16[2,2816]{1,0:T(2,128)(2,1)S(1)}, u32[]{:S(2)}, u32[]{:S(2)}) collective-permute-start(bf16[2,2816]{1,0:T(2,128)(2,1)S(1)} %get-tuple-element.16), channel_id=1, source_target_pairs={{0,19},{1,18},{2,17},{3,16},{4,23},{5,22},{6,21},{7,20},{8,27},{9,... | collective-permute-start | bytes 33800 | tf_op jit(solution)/shard_map/ppermute | solution.py:51
  25.5 0.5 %collective-permute-start.9 = (bf16[2,2816]{1,0:T(2,128)(2,1)S(1)}, bf16[2,2816]{1,0:T(2,128)(2,1)S(1)}, u32[]{:S(2)}, u32[]{:S(2)}) collective-permute-start(bf16[2,2816]{1,0:T(2,128)(2,1)S(1)} %get-tuple-element.17), channel_id=1, source_target_pairs={{0,17},{1,16},{2,19},{3,18},{4,21},{5,20},{6,23},{7,22},{8,25},{9,... | collective-permute-start | bytes 33800 | tf_op jit(solution)/shard_map/ppermute | solution.py:51
  26.0 0.3 collective-permute-start.10
  26.2 1.0 %collective-permute-done.8.refs_0_ = bf16[2,2816]{1,0:T(2,128)(2,1)S(1)} collective-permute-done((bf16[2,2816]{1,0:T(2,128)(2,1)S(1)}, bf16[2,2816]{1,0:T(2,128)(2,1)S(1)}, u32[]{:S(2)}, u32[]{:S(2)}) %collective-permute-start.8) | collective-permute-done | bytes 11296 | tf_op jit(solution)/shard_map/ppermute | solution.py:51
  27.3 1.3 %collective-permute-done.9.refs_1_ = bf16[2,2816]{1,0:T(2,128)(2,1)S(1)} collective-permute-done((bf16[2,2816]{1,0:T(2,128)(2,1)S(1)}, bf16[2,2816]{1,0:T(2,128)(2,1)S(1)}, u32[]{:S(2)}, u32[]{:S(2)}) %collective-permute-start.9) | collective-permute-done | bytes 11296 | tf_op jit(solution)/shard_map/ppermute | solution.py:51
  28.6 0.5 %collective-permute-done.10.refs_2_ = bf16[2,2816]{1,0:T(2,128)(2,1)S(1)} collective-permute-done((bf16[2,2816]{1,0:T(2,128)(2,1)S(1)}, bf16[2,2816]{1,0:T(2,128)(2,1)S(1)}, u32[]{:S(2)}, u32[]{:S(2)}) %collective-permute-start.10) | collective-permute-done | bytes 11296 | tf_op jit(solution)/shard_map/ppermute | solution.py:51
  29.1 1.3 %shard_map.50 = bf16[256,2048]{1,0:T(8,128)(2,1)} custom-call(f32[2,2304]{1,0:T(2,128)S(1)} %get-tuple-element.15.own_ref, bf16[2,2816]{1,0:T(2,128)(2,1)S(1)} %collective-permute-done.8.refs_0_, bf16[2,2816]{1,0:T(2,128)(2,1)S(1)} %collective-permute-done.9.refs_1_, bf16[2,2816]{1,0:T(2,128)(2,1)S(1)} %collective-permute-done.10.refs_2_), custom_call_target="tpu_custom_call" | custom-call | tf_op jit(solution)/shard_map/pallas_call | solution.py:278
  (5 shorter events, 0.1 us)
Async XLA Ops:
  0.0 13.0 %slice-start = ((s8[8388608]{0:T(1024)(128)(4,1)}), s8[4194304]{0:T(1024)(128)(4,1)S(1)}, s32[]{:S(2)}) async-start(s8[8388608]{0:T(1024)(128)(4,1)} %bitcast.1), calls=%async_computation | async-start | bytes 8388608
  0.0 13.0 %slice-start.2 = ((s8[8388608]{0:T(1024)(128)(4,1)}), s8[4194304]{0:T(1024)(128)(4,1)S(1)}, s32[]{:S(2)}) async-start(s8[8388608]{0:T(1024)(128)(4,1)} %bitcast.3), calls=%async_computation.2 | async-start | bytes 8388608
  3.6 9.5 %slice-start.1 = ((s8[8388608]{0:T(1024)(128)(4,1)}), s8[4194304]{0:T(1024)(128)(4,1)S(1)}, s32[]{:S(2)}) async-start(s8[8388608]{0:T(1024)(128)(4,1)} %bitcast.1), calls=%async_computation.1 | async-start | bytes 8388608
  3.6 9.4 %slice-start.3 = ((s8[8388608]{0:T(1024)(128)(4,1)}), s8[4194304]{0:T(1024)(128)(4,1)S(1)}, s32[]{:S(2)}) async-start(s8[8388608]{0:T(1024)(128)(4,1)} %bitcast.3), calls=%async_computation.3 | async-start | bytes 8388608
  3.6 1.4 %collective-permute-start = (f32[2,3200]{1,0:T(2,128)S(1)}, f32[2,3200]{1,0:T(2,128)S(1)}, u32[]{:S(2)}, u32[]{:S(2)}) collective-permute-start(f32[2,3200]{1,0:T(2,128)S(1)} %shard_map.46.own_ref), channel_id=1, source_target_pairs={{0,16},{16,0},{1,17},{17,1},{2,18},{18,2},{3,19},{19,3},{4,20},{20... | collective-permute-start | bytes 76808 | tf_op jit(solution)/shard_map/ppermute | solution.py:293
  5.0 6.2 %collective-permute-start.3 = (bf16[4,2176]{1,0:T(4,128)(2,1)S(1)}, bf16[4,2176]{1,0:T(4,128)(2,1)S(1)}, u32[]{:S(2)}, u32[]{:S(2)}) collective-permute-start(bf16[4,2176]{1,0:T(4,128)(2,1)S(1)} %get-tuple-element.13), channel_id=1, source_target_pairs={{0,24},{1,25},{2,26},{3,27},{4,28},{5,29},{6,30},{7,31},{8,20},{9,... | collective-permute-start | bytes 52232 | tf_op jit(solution)/shard_map/ppermute | solution.py:51
  8.8 4.1 %collective-permute-start.2 = (bf16[4,2176]{1,0:T(4,128)(2,1)S(1)}, bf16[4,2176]{1,0:T(4,128)(2,1)S(1)}, u32[]{:S(2)}, u32[]{:S(2)}) collective-permute-start(bf16[4,2176]{1,0:T(4,128)(2,1)S(1)} %get-tuple-element.13), channel_id=1, source_target_pairs={{0,28},{1,29},{2,30},{3,31},{4,24},{5,25},{6,26},{7,27},{8,16},{9,... | collective-permute-start | bytes 52232 | tf_op jit(solution)/shard_map/ppermute | solution.py:51
  9.8 3.2 %collective-permute-start.1 = (bf16[4,2176]{1,0:T(4,128)(2,1)S(1)}, bf16[4,2176]{1,0:T(4,128)(2,1)S(1)}, u32[]{:S(2)}, u32[]{:S(2)}) collective-permute-start(bf16[4,2176]{1,0:T(4,128)(2,1)S(1)} %get-tuple-element.13), channel_id=1, source_target_pairs={{0,20},{1,21},{2,22},{3,23},{4,16},{5,17},{6,18},{7,19},{8,28},{9,... | collective-permute-start | bytes 52232 | tf_op jit(solution)/shard_map/ppermute | solution.py:51
  15.6 1.2 %collective-permute-start.4 = (f32[4,2048]{1,0:T(4,128)S(1)}, f32[4,2048]{1,0:T(4,128)S(1)}, u32[]{:S(2)}, u32[]{:S(2)}) collective-permute-start(f32[4,2048]{1,0:T(4,128)S(1)} %shard_map.48), channel_id=1, source_target_pairs={{0,16},{16,0},{1,17},{17,1},{2,18},{18,2},{3,19},{19,3},{4,20},{20... | collective-permute-start | bytes 98312 | tf_op jit(solution)/shard_map/ppermute | solution.py:298
  16.8 5.0 %collective-permute-start.7 = (bf16[4,2048]{1,0:T(4,128)(2,1)S(1)}, bf16[4,2048]{1,0:T(4,128)(2,1)S(1)}, u32[]{:S(2)}, u32[]{:S(2)}) collective-permute-start(bf16[4,2048]{1,0:T(4,128)(2,1)S(1)} %get-tuple-element.19), channel_id=1, source_target_pairs={{0,20},{1,21},{2,22},{3,23},{4,24},{5,25},{6,26},{7,27},{8,28},{9,... | collective-permute-start | bytes 49160 | tf_op jit(solution)/shard_map/ppermute | solution.py:51
  18.3 4.5 %collective-permute-start.6 = (bf16[4,2048]{1,0:T(4,128)(2,1)S(1)}, bf16[4,2048]{1,0:T(4,128)(2,1)S(1)}, u32[]{:S(2)}, u32[]{:S(2)}) collective-permute-start(bf16[4,2048]{1,0:T(4,128)(2,1)S(1)} %get-tuple-element.19), channel_id=1, source_target_pairs={{0,24},{1,25},{2,26},{3,27},{4,28},{5,29},{6,30},{7,31},{8,16},{9,... | collective-permute-start | bytes 49160 | tf_op jit(solution)/shard_map/ppermute | solution.py:51
  20.0 3.2 %collective-permute-start.5 = (bf16[4,2048]{1,0:T(4,128)(2,1)S(1)}, bf16[4,2048]{1,0:T(4,128)(2,1)S(1)}, u32[]{:S(2)}, u32[]{:S(2)}) collective-permute-start(bf16[4,2048]{1,0:T(4,128)(2,1)S(1)} %get-tuple-element.19), channel_id=1, source_target_pairs={{0,28},{1,29},{2,30},{3,31},{4,16},{5,17},{6,18},{7,19},{8,20},{9,... | collective-permute-start | bytes 49160 | tf_op jit(solution)/shard_map/ppermute | solution.py:51
  23.2 4.1 %collective-permute-start.8 = (bf16[2,2816]{1,0:T(2,128)(2,1)S(1)}, bf16[2,2816]{1,0:T(2,128)(2,1)S(1)}, u32[]{:S(2)}, u32[]{:S(2)}) collective-permute-start(bf16[2,2816]{1,0:T(2,128)(2,1)S(1)} %get-tuple-element.16), channel_id=1, source_target_pairs={{0,19},{1,18},{2,17},{3,16},{4,23},{5,22},{6,21},{7,20},{8,27},{9,... | collective-permute-start | bytes 33800 | tf_op jit(solution)/shard_map/ppermute | solution.py:51
  25.5 3.1 %collective-permute-start.9 = (bf16[2,2816]{1,0:T(2,128)(2,1)S(1)}, bf16[2,2816]{1,0:T(2,128)(2,1)S(1)}, u32[]{:S(2)}, u32[]{:S(2)}) collective-permute-start(bf16[2,2816]{1,0:T(2,128)(2,1)S(1)} %get-tuple-element.17), channel_id=1, source_target_pairs={{0,17},{1,16},{2,19},{3,18},{4,21},{5,20},{6,23},{7,22},{8,25},{9,... | collective-permute-start | bytes 33800 | tf_op jit(solution)/shard_map/ppermute | solution.py:51
  26.0 3.1 %collective-permute-start.10 = (bf16[2,2816]{1,0:T(2,128)(2,1)S(1)}, bf16[2,2816]{1,0:T(2,128)(2,1)S(1)}, u32[]{:S(2)}, u32[]{:S(2)}) collective-permute-start(bf16[2,2816]{1,0:T(2,128)(2,1)S(1)} %get-tuple-element.18), channel_id=1, source_target_pairs={{0,18},{1,19},{2,16},{3,17},{4,22},{5,23},{6,20},{7,21},{8,26},{9,... | collective-permute-start | bytes 33800 | tf_op jit(solution)/shard_map/ppermute | solution.py:51

commit v8 on v7

--- a/solution.py
+++ b/solution.py
@@ -75,7 +75,7 @@
     top = functools.reduce(jnp.maximum, tops)
     scales = [jnp.exp(t - top) for t in tops]
     total = sum(s * scalar(p, 3) for s, p in zip(scales, parts))
-    return sum(s * p[:, :width] for s, p in zip(scales, parts)) / total
+    return sum(s / total * p[:, :width] for s, p in zip(scales, parts))
 
 
 def slot_sums_kernel(chunks, phi_hbm, tokens_hbm, packed_ref, phi_ref, held, sems):

time: 30.5 us -> 30.5 us (level)
  no operation moved by 1% of the time
where the time goes in v8:
time: 30.5 us; the launch traced here: 30.4 us
  starting transfers between devices  13.5 us (44%)
  waiting for transfers between devices  9.26 us (30%)
  Pallas kernels  7.44 us (24%)
    ppermute x9, starting transfers between devices, exchange(): return lax.ppermute(x, ('dp', 'seq', 'expert'), pairs)  12.7 us
    ppermute x9, waiting for transfers between devices, exchange(): return lax.ppermute(x, ('dp', 'seq', 'expert'), pairs)  7.55 us
    pallas_call x1, Pallas kernels, slot_sums(): pl.pallas_call(functools.partial(slot_sums_kernel, chunks), out_shape=jax...  3.55 us
    pallas_call x1, Pallas kernels, experts(): pl.pallas_call(experts_kernel, out_shape=jax.ShapeDtypeStruct((both.shape...  2.52 us
    pallas_call x1, Pallas kernels, mix(): pl.pallas_call(functools.partial(mix_kernel, chunks), out_shape=jax.Shape...  1.29 us
    ppermute x1, waiting for transfers between devices, on_device(): chip = partial + swapped(lax.ppermute(partial, 'dp', swap))  0.86 us
    ppermute x1, waiting for transfers between devices, on_device(): lax.ppermute(packed, 'dp', swap)  0.85 us
  transfers between devices with their start and end apart: 11, of which 11 were waited for; matrix products, arithmetic and copies ran while one was open for 0% of the time, Pallas kernels for 0%

profile of v8, /device:TPU:0, one launch (start us, length us, event | category | flops | bytes accessed | tf_op | source)
XLA Modules:
  0.0 30.4 jit_solution(4443096935031741501)
XLA Ops:
  0.0 0.0 slice-start
  0.0 0.0 slice-start.2
  0.0 3.6 %shard_map.46.own_ref = f32[2,3200]{1,0:T(2,128)S(1)} custom-call(bf16[2,2048]{1,0:T(2,128)(2,1)} %bitcast.5, bf16[1024,2048]{1,0:T(8,128)(2,1)} %tokens_hbm.1), custom_call_target="tpu_custom_call" | custom-call | tf_op jit(solution)/shard_map/pallas_call | solution.py:132
  3.6 0.0 slice-start.1
  3.6 0.0 slice-start.3
  3.6 0.5 %collective-permute-start = (f32[2,3200]{1,0:T(2,128)S(1)}, f32[2,3200]{1,0:T(2,128)S(1)}, u32[]{:S(2)}, u32[]{:S(2)}) collective-permute-start(f32[2,3200]{1,0:T(2,128)S(1)} %shard_map.46.own_ref), channel_id=1, source_target_pairs={{0,16},{16,0},{1,17},{17,1},{2,18},{18,2},{3,19},{19,3},{4,20},{20... | collective-permute-start | bytes 76808 | tf_op jit(solution)/shard_map/ppermute | solution.py:293
  4.1 0.9 %collective-permute-done.other_ref = f32[2,3200]{1,0:T(2,128)S(1)} collective-permute-done((f32[2,3200]{1,0:T(2,128)S(1)}, f32[2,3200]{1,0:T(2,128)S(1)}, u32[]{:S(2)}, u32[]{:S(2)}) %collective-permute-start) | collective-permute-done | bytes 25632 | tf_op jit(solution)/shard_map/ppermute | solution.py:293
  5.0 3.8 %collective-permute-start.3 = (bf16[4,2176]{1,0:T(4,128)(2,1)S(1)}, bf16[4,2176]{1,0:T(4,128)(2,1)S(1)}, u32[]{:S(2)}, u32[]{:S(2)}) collective-permute-start(bf16[4,2176]{1,0:T(4,128)(2,1)S(1)} %get-tuple-element.13), channel_id=1, source_target_pairs={{0,24},{1,25},{2,26},{3,27},{4,28},{5,29},{6,30},{7,31},{8,20},{9,... | collective-permute-start | bytes 52232 | tf_op jit(solution)/shard_map/ppermute | solution.py:51
  8.8 1.1 %collective-permute-start.2 = (bf16[4,2176]{1,0:T(4,128)(2,1)S(1)}, bf16[4,2176]{1,0:T(4,128)(2,1)S(1)}, u32[]{:S(2)}, u32[]{:S(2)}) collective-permute-start(bf16[4,2176]{1,0:T(4,128)(2,1)S(1)} %get-tuple-element.13), channel_id=1, source_target_pairs={{0,28},{1,29},{2,30},{3,31},{4,24},{5,25},{6,26},{7,27},{8,16},{9,... | collective-permute-start | bytes 52232 | tf_op jit(solution)/shard_map/ppermute | solution.py:51
  9.8 0.5 %collective-permute-start.1 = (bf16[4,2176]{1,0:T(4,128)(2,1)S(1)}, bf16[4,2176]{1,0:T(4,128)(2,1)S(1)}, u32[]{:S(2)}, u32[]{:S(2)}) collective-permute-start(bf16[4,2176]{1,0:T(4,128)(2,1)S(1)} %get-tuple-element.13), channel_id=1, source_target_pairs={{0,20},{1,21},{2,22},{3,23},{4,16},{5,17},{6,18},{7,19},{8,28},{9,... | collective-permute-start | bytes 52232 | tf_op jit(solution)/shard_map/ppermute | solution.py:51
  10.3 0.9 %collective-permute-done.3.refs_2_ = bf16[4,2176]{1,0:T(4,128)(2,1)S(1)} collective-permute-done((bf16[4,2176]{1,0:T(4,128)(2,1)S(1)}, bf16[4,2176]{1,0:T(4,128)(2,1)S(1)}, u32[]{:S(2)}, u32[]{:S(2)}) %collective-permute-start.3) | collective-permute-done | bytes 17440 | tf_op jit(solution)/shard_map/ppermute | solution.py:51
  11.2 1.6 %collective-permute-done.2.refs_1_ = bf16[4,2176]{1,0:T(4,128)(2,1)S(1)} collective-permute-done((bf16[4,2176]{1,0:T(4,128)(2,1)S(1)}, bf16[4,2176]{1,0:T(4,128)(2,1)S(1)}, u32[]{:S(2)}, u32[]{:S(2)}) %collective-permute-start.2) | collective-permute-done | bytes 17440 | tf_op jit(solution)/shard_map/ppermute | solution.py:51
  12.8 0.2 collective-permute-done.1.refs_0_
  13.0 0.0 slice-done
  13.0 0.0 slice-done.2
  13.0 0.0 slice-done.1
  13.0 0.0 slice-done.3
  13.1 2.5 %shard_map.48 = f32[4,2048]{1,0:T(4,128)S(1)} custom-call(f32[4,2176]{1,0:T(4,128)S(1)} %get-tuple-element.12.both_ref, bf16[4,2176]{1,0:T(4,128)(2,1)S(1)} %collective-permute-done.1.refs_0_, bf16[4,2176]{1,0:T(4,128)(2,1)S(1)} %collective-permute-done.2.refs_1_, bf16[4,2176]{1,0:T(4,128)(2,1)S(1)} %collective-permute-done.3.refs_2_, ...), custom_call_target="tpu_custom_call" | custom-call | tf_op jit(solution)/shard_map/pallas_call | solution.py:203
  15.6 0.4 %collective-permute-start.4 = (f32[4,2048]{1,0:T(4,128)S(1)}, f32[4,2048]{1,0:T(4,128)S(1)}, u32[]{:S(2)}, u32[]{:S(2)}) collective-permute-start(f32[4,2048]{1,0:T(4,128)S(1)} %shard_map.48), channel_id=1, source_target_pairs={{0,16},{16,0},{1,17},{17,1},{2,18},{18,2},{3,19},{19,3},{4,20},{20... | collective-permute-start | bytes 98312 | tf_op jit(solution)/shard_map/ppermute | solution.py:298
  15.9 0.9 %collective-permute-done.4 = f32[4,2048]{1,0:T(4,128)S(1)} collective-permute-done((f32[4,2048]{1,0:T(4,128)S(1)}, f32[4,2048]{1,0:T(4,128)S(1)}, u32[]{:S(2)}, u32[]{:S(2)}) %collective-permute-start.4) | collective-permute-done | bytes 32800 | tf_op jit(solution)/shard_map/ppermute | solution.py:298
  16.8 1.5 %collective-permute-start.7 = (bf16[4,2048]{1,0:T(4,128)(2,1)S(1)}, bf16[4,2048]{1,0:T(4,128)(2,1)S(1)}, u32[]{:S(2)}, u32[]{:S(2)}) collective-permute-start(bf16[4,2048]{1,0:T(4,128)(2,1)S(1)} %get-tuple-element.19), channel_id=1, source_target_pairs={{0,20},{1,21},{2,22},{3,23},{4,24},{5,25},{6,26},{7,27},{8,28},{9,... | collective-permute-start | bytes 49160 | tf_op jit(solution)/shard_map/ppermute | solution.py:51
  18.3 1.7 %collective-permute-start.6 = (bf16[4,2048]{1,0:T(4,128)(2,1)S(1)}, bf16[4,2048]{1,0:T(4,128)(2,1)S(1)}, u32[]{:S(2)}, u32[]{:S(2)}) collective-permute-start(bf16[4,2048]{1,0:T(4,128)(2,1)S(1)} %get-tuple-element.19), channel_id=1, source_target_pairs={{0,24},{1,25},{2,26},{3,27},{4,28},{5,29},{6,30},{7,31},{8,16},{9,... | collective-permute-start | bytes 49160 | tf_op jit(solution)/shard_map/ppermute | solution.py:51
  20.0 1.2 %collective-permute-start.5 = (bf16[4,2048]{1,0:T(4,128)(2,1)S(1)}, bf16[4,2048]{1,0:T(4,128)(2,1)S(1)}, u32[]{:S(2)}, u32[]{:S(2)}) collective-permute-start(bf16[4,2048]{1,0:T(4,128)(2,1)S(1)} %get-tuple-element.19), channel_id=1, source_target_pairs={{0,28},{1,29},{2,30},{3,31},{4,16},{5,17},{6,18},{7,19},{8,20},{9,... | collective-permute-start | bytes 49160 | tf_op jit(solution)/shard_map/ppermute | solution.py:51
  21.2 0.7 %collective-permute-done.7.refs_2_ = bf16[4,2048]{1,0:T(4,128)(2,1)S(1)} collective-permute-done((bf16[4,2048]{1,0:T(4,128)(2,1)S(1)}, bf16[4,2048]{1,0:T(4,128)(2,1)S(1)}, u32[]{:S(2)}, u32[]{:S(2)}) %collective-permute-start.7) | collective-permute-done | bytes 16416 | tf_op jit(solution)/shard_map/ppermute | solution.py:51
  21.8 0.9 %collective-permute-done.6.refs_1_ = bf16[4,2048]{1,0:T(4,128)(2,1)S(1)} collective-permute-done((bf16[4,2048]{1,0:T(4,128)(2,1)S(1)}, bf16[4,2048]{1,0:T(4,128)(2,1)S(1)}, u32[]{:S(2)}, u32[]{:S(2)}) %collective-permute-start.6) | collective-permute-done | bytes 16416 | tf_op jit(solution)/shard_map/ppermute | solution.py:51
  22.8 0.4 %collective-permute-done.5.refs_0_ = bf16[4,2048]{1,0:T(4,128)(2,1)S(1)} collective-permute-done((bf16[4,2048]{1,0:T(4,128)(2,1)S(1)}, bf16[4,2048]{1,0:T(4,128)(2,1)S(1)}, u32[]{:S(2)}, u32[]{:S(2)}) %collective-permute-start.5) | collective-permute-done | bytes 16416 | tf_op jit(solution)/shard_map/ppermute | solution.py:51
  23.1 0.1 shard_map.49
  23.2 2.3 %collective-permute-start.8 = (bf16[2,2816]{1,0:T(2,128)(2,1)S(1)}, bf16[2,2816]{1,0:T(2,128)(2,1)S(1)}, u32[]{:S(2)}, u32[]{:S(2)}) collective-permute-start(bf16[2,2816]{1,0:T(2,128)(2,1)S(1)} %get-tuple-element.16), channel_id=1, source_target_pairs={{0,19},{1,18},{2,17},{3,16},{4,23},{5,22},{6,21},{7,20},{8,27},{9,... | collective-permute-start | bytes 33800 | tf_op jit(solution)/shard_map/ppermute | solution.py:51
  25.5 0.5 %collective-permute-start.9 = (bf16[2,2816]{1,0:T(2,128)(2,1)S(1)}, bf16[2,2816]{1,0:T(2,128)(2,1)S(1)}, u32[]{:S(2)}, u32[]{:S(2)}) collective-permute-start(bf16[2,2816]{1,0:T(2,128)(2,1)S(1)} %get-tuple-element.17), channel_id=1, source_target_pairs={{0,17},{1,16},{2,19},{3,18},{4,21},{5,20},{6,23},{7,22},{8,25},{9,... | collective-permute-start | bytes 33800 | tf_op jit(solution)/shard_map/ppermute | solution.py:51
  26.0 0.3 collective-permute-start.10
  26.2 1.0 %collective-permute-done.8.refs_0_ = bf16[2,2816]{1,0:T(2,128)(2,1)S(1)} collective-permute-done((bf16[2,2816]{1,0:T(2,128)(2,1)S(1)}, bf16[2,2816]{1,0:T(2,128)(2,1)S(1)}, u32[]{:S(2)}, u32[]{:S(2)}) %collective-permute-start.8) | collective-permute-done | bytes 11296 | tf_op jit(solution)/shard_map/ppermute | solution.py:51
  27.3 1.3 %collective-permute-done.9.refs_1_ = bf16[2,2816]{1,0:T(2,128)(2,1)S(1)} collective-permute-done((bf16[2,2816]{1,0:T(2,128)(2,1)S(1)}, bf16[2,2816]{1,0:T(2,128)(2,1)S(1)}, u32[]{:S(2)}, u32[]{:S(2)}) %collective-permute-start.9) | collective-permute-done | bytes 11296 | tf_op jit(solution)/shard_map/ppermute | solution.py:51
  28.6 0.5 %collective-permute-done.10.refs_2_ = bf16[2,2816]{1,0:T(2,128)(2,1)S(1)} collective-permute-done((bf16[2,2816]{1,0:T(2,128)(2,1)S(1)}, bf16[2,2816]{1,0:T(2,128)(2,1)S(1)}, u32[]{:S(2)}, u32[]{:S(2)}) %collective-permute-start.10) | collective-permute-done | bytes 11296 | tf_op jit(solution)/shard_map/ppermute | solution.py:51
  29.1 1.3 %shard_map.50 = bf16[256,2048]{1,0:T(8,128)(2,1)} custom-call(f32[2,2304]{1,0:T(2,128)S(1)} %get-tuple-element.15.own_ref, bf16[2,2816]{1,0:T(2,128)(2,1)S(1)} %collective-permute-done.8.refs_0_, bf16[2,2816]{1,0:T(2,128)(2,1)S(1)} %collective-permute-done.9.refs_1_, bf16[2,2816]{1,0:T(2,128)(2,1)S(1)} %collective-permute-done.10.refs_2_), custom_call_target="tpu_custom_call" | custom-call | tf_op jit(solution)/shard_map/pallas_call | solution.py:278
  (5 shorter events, 0.1 us)
Async XLA Ops:
  0.0 13.0 %slice-start = ((s8[8388608]{0:T(1024)(128)(4,1)}), s8[4194304]{0:T(1024)(128)(4,1)S(1)}, s32[]{:S(2)}) async-start(s8[8388608]{0:T(1024)(128)(4,1)} %bitcast.1), calls=%async_computation | async-start | bytes 8388608
  0.0 13.0 %slice-start.2 = ((s8[8388608]{0:T(1024)(128)(4,1)}), s8[4194304]{0:T(1024)(128)(4,1)S(1)}, s32[]{:S(2)}) async-start(s8[8388608]{0:T(1024)(128)(4,1)} %bitcast.3), calls=%async_computation.2 | async-start | bytes 8388608
  3.6 9.5 %slice-start.1 = ((s8[8388608]{0:T(1024)(128)(4,1)}), s8[4194304]{0:T(1024)(128)(4,1)S(1)}, s32[]{:S(2)}) async-start(s8[8388608]{0:T(1024)(128)(4,1)} %bitcast.1), calls=%async_computation.1 | async-start | bytes 8388608
  3.6 9.4 %slice-start.3 = ((s8[8388608]{0:T(1024)(128)(4,1)}), s8[4194304]{0:T(1024)(128)(4,1)S(1)}, s32[]{:S(2)}) async-start(s8[8388608]{0:T(1024)(128)(4,1)} %bitcast.3), calls=%async_computation.3 | async-start | bytes 8388608
  3.6 1.4 %collective-permute-start = (f32[2,3200]{1,0:T(2,128)S(1)}, f32[2,3200]{1,0:T(2,128)S(1)}, u32[]{:S(2)}, u32[]{:S(2)}) collective-permute-start(f32[2,3200]{1,0:T(2,128)S(1)} %shard_map.46.own_ref), channel_id=1, source_target_pairs={{0,16},{16,0},{1,17},{17,1},{2,18},{18,2},{3,19},{19,3},{4,20},{20... | collective-permute-start | bytes 76808 | tf_op jit(solution)/shard_map/ppermute | solution.py:293
  5.0 6.2 %collective-permute-start.3 = (bf16[4,2176]{1,0:T(4,128)(2,1)S(1)}, bf16[4,2176]{1,0:T(4,128)(2,1)S(1)}, u32[]{:S(2)}, u32[]{:S(2)}) collective-permute-start(bf16[4,2176]{1,0:T(4,128)(2,1)S(1)} %get-tuple-element.13), channel_id=1, source_target_pairs={{0,24},{1,25},{2,26},{3,27},{4,28},{5,29},{6,30},{7,31},{8,20},{9,... | collective-permute-start | bytes 52232 | tf_op jit(solution)/shard_map/ppermute | solution.py:51
  8.8 4.1 %collective-permute-start.2 = (bf16[4,2176]{1,0:T(4,128)(2,1)S(1)}, bf16[4,2176]{1,0:T(4,128)(2,1)S(1)}, u32[]{:S(2)}, u32[]{:S(2)}) collective-permute-start(bf16[4,2176]{1,0:T(4,128)(2,1)S(1)} %get-tuple-element.13), channel_id=1, source_target_pairs={{0,28},{1,29},{2,30},{3,31},{4,24},{5,25},{6,26},{7,27},{8,16},{9,... | collective-permute-start | bytes 52232 | tf_op jit(solution)/shard_map/ppermute | solution.py:51
  9.8 3.2 %collective-permute-start.1 = (bf16[4,2176]{1,0:T(4,128)(2,1)S(1)}, bf16[4,2176]{1,0:T(4,128)(2,1)S(1)}, u32[]{:S(2)}, u32[]{:S(2)}) collective-permute-start(bf16[4,2176]{1,0:T(4,128)(2,1)S(1)} %get-tuple-element.13), channel_id=1, source_target_pairs={{0,20},{1,21},{2,22},{3,23},{4,16},{5,17},{6,18},{7,19},{8,28},{9,... | collective-permute-start | bytes 52232 | tf_op jit(solution)/shard_map/ppermute | solution.py:51
  15.6 1.2 %collective-permute-start.4 = (f32[4,2048]{1,0:T(4,128)S(1)}, f32[4,2048]{1,0:T(4,128)S(1)}, u32[]{:S(2)}, u32[]{:S(2)}) collective-permute-start(f32[4,2048]{1,0:T(4,128)S(1)} %shard_map.48), channel_id=1, source_target_pairs={{0,16},{16,0},{1,17},{17,1},{2,18},{18,2},{3,19},{19,3},{4,20},{20... | collective-permute-start | bytes 98312 | tf_op jit(solution)/shard_map/ppermute | solution.py:298
  16.8 5.0 %collective-permute-start.7 = (bf16[4,2048]{1,0:T(4,128)(2,1)S(1)}, bf16[4,2048]{1,0:T(4,128)(2,1)S(1)}, u32[]{:S(2)}, u32[]{:S(2)}) collective-permute-start(bf16[4,2048]{1,0:T(4,128)(2,1)S(1)} %get-tuple-element.19), channel_id=1, source_target_pairs={{0,20},{1,21},{2,22},{3,23},{4,24},{5,25},{6,26},{7,27},{8,28},{9,... | collective-permute-start | bytes 49160 | tf_op jit(solution)/shard_map/ppermute | solution.py:51
  18.3 4.5 %collective-permute-start.6 = (bf16[4,2048]{1,0:T(4,128)(2,1)S(1)}, bf16[4,2048]{1,0:T(4,128)(2,1)S(1)}, u32[]{:S(2)}, u32[]{:S(2)}) collective-permute-start(bf16[4,2048]{1,0:T(4,128)(2,1)S(1)} %get-tuple-element.19), channel_id=1, source_target_pairs={{0,24},{1,25},{2,26},{3,27},{4,28},{5,29},{6,30},{7,31},{8,16},{9,... | collective-permute-start | bytes 49160 | tf_op jit(solution)/shard_map/ppermute | solution.py:51
  20.0 3.2 %collective-permute-start.5 = (bf16[4,2048]{1,0:T(4,128)(2,1)S(1)}, bf16[4,2048]{1,0:T(4,128)(2,1)S(1)}, u32[]{:S(2)}, u32[]{:S(2)}) collective-permute-start(bf16[4,2048]{1,0:T(4,128)(2,1)S(1)} %get-tuple-element.19), channel_id=1, source_target_pairs={{0,28},{1,29},{2,30},{3,31},{4,16},{5,17},{6,18},{7,19},{8,20},{9,... | collective-permute-start | bytes 49160 | tf_op jit(solution)/shard_map/ppermute | solution.py:51
  23.2 4.1 %collective-permute-start.8 = (bf16[2,2816]{1,0:T(2,128)(2,1)S(1)}, bf16[2,2816]{1,0:T(2,128)(2,1)S(1)}, u32[]{:S(2)}, u32[]{:S(2)}) collective-permute-start(bf16[2,2816]{1,0:T(2,128)(2,1)S(1)} %get-tuple-element.16), channel_id=1, source_target_pairs={{0,19},{1,18},{2,17},{3,16},{4,23},{5,22},{6,21},{7,20},{8,27},{9,... | collective-permute-start | bytes 33800 | tf_op jit(solution)/shard_map/ppermute | solution.py:51
  25.5 3.1 %collective-permute-start.9 = (bf16[2,2816]{1,0:T(2,128)(2,1)S(1)}, bf16[2,2816]{1,0:T(2,128)(2,1)S(1)}, u32[]{:S(2)}, u32[]{:S(2)}) collective-permute-start(bf16[2,2816]{1,0:T(2,128)(2,1)S(1)} %get-tuple-element.17), channel_id=1, source_target_pairs={{0,17},{1,16},{2,19},{3,18},{4,21},{5,20},{6,23},{7,22},{8,25},{9,... | collective-permute-start | bytes 33800 | tf_op jit(solution)/shard_map/ppermute | solution.py:51
  26.0 3.1 %collective-permute-start.10 = (bf16[2,2816]{1,0:T(2,128)(2,1)S(1)}, bf16[2,2816]{1,0:T(2,128)(2,1)S(1)}, u32[]{:S(2)}, u32[]{:S(2)}) collective-permute-start(bf16[2,2816]{1,0:T(2,128)(2,1)S(1)} %get-tuple-element.18), channel_id=1, source_target_pairs={{0,18},{1,19},{2,16},{3,17},{4,22},{5,23},{6,20},{7,21},{8,26},{9,... | collective-permute-start | bytes 33800 | tf_op jit(solution)/shard_map/ppermute | solution.py:51
